TPU v7x, 32 devices: a whole 2x2x4 slice. The times are simulated.
32 devices in a mesh: dp: 16 (over z, y, x), sub: 2 (over core).
Axes of the slice: x: 2, y: 2, z: 4, core: 2. Of those that a mesh axis runs over, the one named last changes fastest.
Arguments:
- images: bfloat16 [256, 49, 2048], P(('dp', 'sub')), may hold values from -20 to 20
- pixel_mask: int32 [256, 49], P(('dp', 'sub')), may hold values from 0 to 1, as said below
- pairing: int32 [256], replicated, may hold values from 0 to 127, as said below
- w_reduce: bfloat16 [2048, 512], replicated, may hold values from -0.125 to 0.125
- w_spatial: bfloat16 [3, 3, 512, 512], replicated, may hold values from -0.09375 to 0.09375
- w_expand: bfloat16 [512, 2048], replicated, may hold values from -0.25 to 0.25
- w_project: bfloat16 [2048, 1024], replicated, may hold values from -0.125 to 0.125
- w_code: bfloat16 [1024, 128], replicated, may hold values from -0.1875 to 0.1875
- norm_reduce: float32 [2, 512], replicated, may hold values from 0.5 to 1.5
- norm_spatial: float32 [2, 512], replicated, may hold values from 0.5 to 1.5
- norm_expand: float32 [2, 2048], replicated, may hold values from 0.5 to 1.5
- norm_project: float32 [2, 1024], replicated, may hold values from 0.5 to 1.5
Outputs:
- loss_value: float32 [], replicated
- grad_images: float32 [256, 49, 2048], P(('dp', 'sub'))
- grad_reduce: float32 [2048, 512], replicated
- grad_spatial: float32 [3, 3, 512, 512], replicated
- grad_expand: float32 [512, 2048], replicated
- grad_project: float32 [2048, 1024], replicated
- grad_code: float32 [1024, 128], replicated
- grad_norm_reduce: float32 [2, 512], replicated
- grad_norm_spatial: float32 [2, 512], replicated
- grad_norm_expand: float32 [2, 2048], replicated
- grad_norm_project: float32 [2, 1024], replicated
Inputs may be any that keep to these rules, and one draw needn't show every extreme that they name: `pixel_mask`: each image's valid pixels form the top-left block of 4 to 7 rows and 4 to 7 columns. `pairing`: every pair is named by exactly two images.
All inputs are finite; a program needn't handle non-finite values.
Results may differ from a plain program's by a relative error of at most 0.012.
Values sent between devices are 32-bit elements; how exact they have to be, the bound alone decides.
A program may use at most 320 MiB of HBM per device.

v0:
```python
import jax
import jax.numpy as jnp
from jax import lax
from jax.sharding import PartitionSpec as P

SIDE = 7


epsilon = 1e-05
whiten_floor = 0.001


def silu_slope(values):
    sigmoid_value = jax.nn.sigmoid(values)
    return sigmoid_value * (1.0 + values * (1.0 - sigmoid_value))


def moments(sum_value, sum_square, total_count):
    centre = sum_value / total_count
    return (centre, lax.rsqrt(sum_square / total_count - centre * centre + epsilon))


def whiten_loss(codes, pairing):
    rows_total = codes.shape[0]
    centre = jnp.sum(codes, axis=0) / rows_total
    covariance = jnp.dot(codes.T, codes, precision=lax.Precision.HIGHEST) / rows_total - jnp.outer(
        centre, centre
    )
    covariance = covariance + whiten_floor * jnp.eye(codes.shape[1], dtype=jnp.float32)
    factor = jnp.linalg.cholesky(covariance)
    whitened = lax.linalg.triangular_solve(factor, (codes - centre).T, left_side=True, lower=True).T
    unit_rows = whitened * lax.rsqrt(jnp.sum(whitened * whitened, axis=1, keepdims=True) + epsilon)
    partner_sum = jax.ops.segment_sum(unit_rows, pairing, num_segments=rows_total // 2)
    pair_gap = 2.0 * unit_rows - partner_sum[pairing]
    return jnp.sum(pair_gap * pair_gap) / rows_total


def make_columns(activation):
    images_here, pixel_count, inner_width = activation.shape
    grid_map = activation.reshape(images_here, SIDE, SIDE, inner_width)
    padded = jnp.pad(grid_map, ((0, 0), (1, 1), (1, 1), (0, 0)))
    pieces = [
        padded[:, tap_row : tap_row + SIDE, tap_col : tap_col + SIDE, :]
        for tap_row in range(3)
        for tap_col in range(3)
    ]
    return jnp.concatenate(pieces, axis=3).reshape(images_here * pixel_count, 9 * inner_width)


def fold_columns(columns, images_here, inner_width):
    tap_grads = columns.reshape(images_here, SIDE, SIDE, 9, inner_width)
    padded = jnp.zeros((images_here, SIDE + 2, SIDE + 2, inner_width), jnp.float32)
    for tap_row in range(3):
        for tap_col in range(3):
            padded = padded.at[:, tap_row : tap_row + SIDE, tap_col : tap_col + SIDE, :].add(
                tap_grads[:, :, :, 3 * tap_row + tap_col, :]
            )
    return padded[:, 1 : SIDE + 1, 1 : SIDE + 1, :].reshape(images_here, SIDE * SIDE, inner_width)


def pixel_sums(values, weight):
    return (jnp.sum(values * weight, axis=(0, 1)), jnp.sum(values * values * weight, axis=(0, 1)))


def front(
    masked_low,
    weight,
    counts,
    w_reduce,
    w_spatial,
    w_expand,
    norm_reduce,
    norm_spatial,
    norm_expand,
    known,
):
    images_here, pixel_count, width = masked_low.shape
    inner_width = w_reduce.shape[1]
    rows_here = images_here * pixel_count
    reduced = jnp.dot(
        masked_low.reshape(rows_here, width), w_reduce, preferred_element_type=jnp.float32
    ).reshape(images_here, pixel_count, inner_width)
    if known is None:
        sum_reduce, square_reduce = pixel_sums(reduced, weight)
        sum_reduce, square_reduce, valid_total = lax.psum(
            (sum_reduce, square_reduce, jnp.sum(counts)), ("dp", "sub")
        )
        centre_reduce, scale_reduce = moments(sum_reduce, square_reduce, valid_total)
    else:
        valid_total, centre_reduce, scale_reduce = (known[0], known[1], known[2])
    normed_reduce = (reduced - centre_reduce) * scale_reduce
    level_reduce = norm_reduce[0] * normed_reduce + norm_reduce[1]
    act_reduce = (weight * jax.nn.silu(level_reduce)).astype(jnp.bfloat16)
    columns = make_columns(act_reduce)
    spatial = jnp.dot(
        columns, w_spatial.reshape(9 * inner_width, inner_width), preferred_element_type=jnp.float32
    ).reshape(images_here, pixel_count, inner_width)
    if known is None:
        sum_spatial, square_spatial = pixel_sums(spatial, weight)
        sum_spatial, square_spatial = lax.psum((sum_spatial, square_spatial), ("dp", "sub"))
        centre_spatial, scale_spatial = moments(sum_spatial, square_spatial, valid_total)
    else:
        centre_spatial, scale_spatial = (known[3], known[4])
    normed_spatial = (spatial - centre_spatial) * scale_spatial
    level_spatial = norm_spatial[0] * normed_spatial + norm_spatial[1]
    act_spatial = (weight * jax.nn.silu(level_spatial)).astype(jnp.bfloat16)
    expanded = jnp.dot(
        act_spatial.reshape(rows_here, inner_width), w_expand, preferred_element_type=jnp.float32
    ).reshape(images_here, pixel_count, width)
    if known is None:
        sum_expand, square_expand = pixel_sums(expanded, weight)
        sum_expand, square_expand = lax.psum((sum_expand, square_expand), ("dp", "sub"))
        centre_expand, scale_expand = moments(sum_expand, square_expand, valid_total)
    else:
        centre_expand, scale_expand = (known[5], known[6])
    normed_expand = (expanded - centre_expand) * scale_expand
    summed = masked_low.astype(jnp.float32) + norm_expand[0] * normed_expand + norm_expand[1]
    stats = (
        valid_total,
        centre_reduce,
        scale_reduce,
        centre_spatial,
        scale_spatial,
        centre_expand,
        scale_expand,
    )
    return (
        (
            normed_reduce,
            level_reduce,
            columns,
            normed_spatial,
            level_spatial,
            act_spatial,
            normed_expand,
            summed,
        ),
        stats,
    )


def norm_back(upstream, normed, gain, scale_value, sum_grad, dot_grad, total_count):
    return gain * scale_value * (upstream - (sum_grad + normed * dot_grad) / total_count)


def shards(
    images,
    pixel_mask,
    pairing,
    w_reduce,
    w_spatial,
    w_expand,
    w_project,
    w_code,
    norm_reduce,
    norm_spatial,
    norm_expand,
    norm_project,
):
    images_here, pixel_count, width = images.shape
    inner_width = w_reduce.shape[1]
    images_total = pairing.shape[0]
    rows_here = images_here * pixel_count
    highest = lax.Precision.HIGHEST
    weight = pixel_mask.astype(jnp.float32)[:, :, None]
    counts = jnp.sum(weight, axis=1)
    masked_low = images * weight.astype(jnp.bfloat16)
    project_full = w_project.astype(jnp.float32)
    code_full = w_code.astype(jnp.float32)
    saved, stats = front(
        masked_low,
        weight,
        counts,
        w_reduce,
        w_spatial,
        w_expand,
        norm_reduce,
        norm_spatial,
        norm_expand,
        None,
    )
    output = weight * jax.nn.silu(saved[7])
    pooled = jnp.sum(output, axis=1) / counts
    projected = jnp.dot(pooled, project_full, precision=highest)
    sum_project, square_project = lax.psum(
        (jnp.sum(projected, axis=0), jnp.sum(projected * projected, axis=0)), ("dp", "sub")
    )
    centre_project, scale_project = moments(sum_project, square_project, float(images_total))
    normed_project = (projected - centre_project) * scale_project
    level_project = norm_project[0] * normed_project + norm_project[1]
    hidden = jax.nn.silu(level_project)
    codes = jnp.dot(hidden, code_full, precision=highest)
    all_codes = lax.all_gather(codes, ("dp", "sub"), axis=0, tiled=True)
    loss_value, pullback = jax.vjp(lambda gathered: whiten_loss(gathered, pairing), all_codes)
    code_grads = pullback(jnp.asarray(images_total / 4.0, jnp.float32))[0]
    own_start = lax.axis_index(("dp", "sub")) * images_here
    grad_codes = lax.dynamic_slice_in_dim(code_grads, own_start, images_here, 0)
    grad_w_code = jnp.dot(hidden.T, grad_codes, precision=highest)
    grad_hidden = jnp.dot(grad_codes, code_full.T, precision=highest)
    grad_level_project = grad_hidden * silu_slope(level_project)
    sum_project_grad, dot_project_grad = lax.psum(
        (jnp.sum(grad_level_project, axis=0), jnp.sum(grad_level_project * normed_project, axis=0)),
        ("dp", "sub"),
    )
    grad_norm_project = jnp.stack([dot_project_grad, sum_project_grad])
    grad_projected = norm_back(
        grad_level_project,
        normed_project,
        norm_project[0],
        scale_project,
        sum_project_grad,
        dot_project_grad,
        float(images_total),
    )
    grad_w_project = jnp.dot(pooled.T, grad_projected, precision=highest)
    grad_pooled = jnp.dot(grad_projected, project_full.T, precision=highest)
    again_input, again_stats, grad_pooled = lax.optimization_barrier(
        (masked_low, stats, grad_pooled)
    )
    saved = front(
        again_input,
        weight,
        counts,
        w_reduce,
        w_spatial,
        w_expand,
        norm_reduce,
        norm_spatial,
        norm_expand,
        again_stats,
    )[0]
    (
        normed_reduce,
        level_reduce,
        columns,
        normed_spatial,
        level_spatial,
        act_spatial,
        normed_expand,
        summed,
    ) = saved
    (
        valid_total,
        centre_reduce,
        scale_reduce,
        centre_spatial,
        scale_spatial,
        centre_expand,
        scale_expand,
    ) = stats
    grad_summed = weight * (grad_pooled / counts)[:, None, :] * silu_slope(summed)
    sum_expand_grad, dot_expand_grad = lax.psum(
        (jnp.sum(grad_summed, axis=(0, 1)), jnp.sum(grad_summed * normed_expand, axis=(0, 1))),
        ("dp", "sub"),
    )
    grad_norm_expand = jnp.stack([dot_expand_grad, sum_expand_grad])
    grad_expanded = (
        (
            weight
            * norm_back(
                grad_summed,
                normed_expand,
                norm_expand[0],
                scale_expand,
                sum_expand_grad,
                dot_expand_grad,
                valid_total,
            )
        )
        .astype(jnp.bfloat16)
        .reshape(rows_here, width)
    )
    grad_w_expand = jnp.einsum(
        "rm,rc->mc",
        act_spatial.reshape(rows_here, inner_width),
        grad_expanded,
        preferred_element_type=jnp.float32,
    )
    grad_act_spatial = jnp.einsum(
        "rc,mc->rm", grad_expanded, w_expand, preferred_element_type=jnp.float32
    ).reshape(images_here, pixel_count, inner_width)
    grad_level_spatial = grad_act_spatial * weight * silu_slope(level_spatial)
    sum_spatial_grad, dot_spatial_grad = lax.psum(
        (
            jnp.sum(grad_level_spatial, axis=(0, 1)),
            jnp.sum(grad_level_spatial * normed_spatial, axis=(0, 1)),
        ),
        ("dp", "sub"),
    )
    grad_norm_spatial = jnp.stack([dot_spatial_grad, sum_spatial_grad])
    grad_spatial_out = (
        (
            weight
            * norm_back(
                grad_level_spatial,
                normed_spatial,
                norm_spatial[0],
                scale_spatial,
                sum_spatial_grad,
                dot_spatial_grad,
                valid_total,
            )
        )
        .astype(jnp.bfloat16)
        .reshape(rows_here, inner_width)
    )
    grad_w_spatial = jnp.einsum(
        "rk,rm->km", columns, grad_spatial_out, preferred_element_type=jnp.float32
    ).reshape(3, 3, inner_width, inner_width)
    grad_columns = jnp.einsum(
        "rm,km->rk",
        grad_spatial_out,
        w_spatial.reshape(9 * inner_width, inner_width),
        preferred_element_type=jnp.float32,
    )
    grad_act_reduce = fold_columns(grad_columns, images_here, inner_width)
    grad_level_reduce = grad_act_reduce * weight * silu_slope(level_reduce)
    sum_reduce_grad, dot_reduce_grad = lax.psum(
        (
            jnp.sum(grad_level_reduce, axis=(0, 1)),
            jnp.sum(grad_level_reduce * normed_reduce, axis=(0, 1)),
        ),
        ("dp", "sub"),
    )
    grad_norm_reduce = jnp.stack([dot_reduce_grad, sum_reduce_grad])
    grad_reduced = (
        (
            weight
            * norm_back(
                grad_level_reduce,
                normed_reduce,
                norm_reduce[0],
                scale_reduce,
                sum_reduce_grad,
                dot_reduce_grad,
                valid_total,
            )
        )
        .astype(jnp.bfloat16)
        .reshape(rows_here, inner_width)
    )
    grad_w_reduce = jnp.einsum(
        "rc,rm->cm",
        masked_low.reshape(rows_here, width),
        grad_reduced,
        preferred_element_type=jnp.float32,
    )
    grad_input = jnp.einsum(
        "rm,cm->rc", grad_reduced, w_reduce, preferred_element_type=jnp.float32
    ).reshape(images_here, pixel_count, width)
    grad_images = weight * (grad_summed + grad_input)
    local_grads = (grad_w_reduce, grad_w_spatial, grad_w_expand, grad_w_project, grad_w_code)
    flat_grads = jnp.concatenate([piece_grad.reshape(-1) for piece_grad in local_grads])
    device_count = lax.axis_size(("dp", "sub"))
    share_length = -(-flat_grads.shape[0] // device_count)
    own_share = lax.psum_scatter(
        flat_grads.reshape(device_count, share_length),
        ("dp", "sub"),
        scatter_dimension=0,
        tiled=True,
    )
    whole_grads = lax.all_gather(own_share, ("dp", "sub"), axis=0, tiled=True).reshape(-1)
    results = []
    offset = 0
    for piece_grad in local_grads:
        results.append(whole_grads[offset : offset + piece_grad.size].reshape(piece_grad.shape))
        offset = offset + piece_grad.size
    return (
        loss_value,
        grad_images,
        results[0],
        results[1],
        results[2],
        results[3],
        results[4],
        grad_norm_reduce,
        grad_norm_spatial,
        grad_norm_expand,
        grad_norm_project,
    )


def solution(mesh):
    placed = (
        P(("dp", "sub"), None, None),
        P(("dp", "sub"), None),
        P(),
        P(),
        P(),
        P(),
        P(),
        P(),
        P(),
        P(),
        P(),
        P(),
    )
    return jax.shard_map(
        shards,
        mesh=mesh,
        in_specs=placed,
        out_specs=(P(), P(("dp", "sub"), None, None), P(), P(), P(), P(), P(), P(), P(), P(), P()),
        check_vma=False,
    )
```

profile of v0, /device:TPU:0, one launch (start us, length us, event | category | flops | bytes accessed | tf_op | source)
XLA Modules:
  0.0 1401.6 jit_solution(2436794823706228776)
XLA Ops:
  24.3 42.3 %all-reduce.11 = (f32[512]{0:T(512)S(1)}, f32[]{:T(128)}, f32[512]{0:T(512)S(1)}) all-reduce(f32[512]{0:T(512)S(1)} %get-tuple-element.176, f32[]{:T(128)} %get-tuple-element.188, f32[512]{0:T(512)S(1)} %get-tuple-element.175), channel_id=1, replica_groups=mesh['dp'=16,'sub'=2] {'dp','sub'}, use_global_device_ids=true, to_apply=%region_5.0 | all-reduce | flops 1025 | bytes 8200 | tf_op jit(solution)/shard_map/psum | solution.py:85
  74.8 40.3 %all-reduce.10 = (f32[512]{0:T(512)S(1)}, f32[512]{0:T(512)S(1)}) all-reduce(f32[512]{0:T(512)S(1)} %get-tuple-element.174, f32[512]{0:T(512)S(1)} %get-tuple-element.173), channel_id=1, replica_groups=mesh['dp'=16,'sub'=2] {'dp','sub'}, use_global_device_ids=true, to_apply=%region_9.10 | all-reduce | flops 1024 | bytes 8192 | tf_op jit(solution)/shard_map/psum | solution.py:100
  119.9 50.8 %all-reduce.9 = (f32[2048]{0:T(1024)S(1)}, f32[2048]{0:T(1024)S(1)}) all-reduce(f32[2048]{0:T(1024)S(1)} %get-tuple-element.172, f32[2048]{0:T(1024)S(1)} %get-tuple-element.171), channel_id=1, replica_groups=mesh['dp'=16,'sub'=2] {'dp','sub'}, use_global_device_ids=true, to_apply=%region_11.12 | all-reduce | flops 4096 | bytes 32768 | tf_op jit(solution)/shard_map/psum | solution.py:112
  172.8 4.9 multiply_reduce_fusion.1
  179.5 40.2 %all-reduce.8 = (f32[1024]{0:T(1024)S(1)}, f32[1024]{0:T(1024)S(1)}) all-reduce(f32[1024]{0:T(1024)S(1)} %get-tuple-element.186, f32[1024]{0:T(1024)S(1)} %get-tuple-element.185), channel_id=1, replica_groups=mesh['dp'=16,'sub'=2] {'dp','sub'}, use_global_device_ids=true, to_apply=%region_19.20 | all-reduce | flops 2048 | bytes 16384 | tf_op jit(solution)/shard_map/psum | solution.py:185
  220.0 41.6 %all_gather.6 = f32[256,128]{1,0:T(8,128)S(1)} all-gather(f32[8,128]{1,0:T(8,128)S(1)} %fusion.101), channel_id=1, replica_groups=mesh['dp'=16,'sub'=2] {'dp','sub'}, dimensions={0}, use_global_device_ids=true | all-gather | bytes 135168 | tf_op jit(solution)/shard_map/all_gather | solution.py:193
  262.2 11.7 cholesky.17
  275.3 9.8 custom-call.15
  292.1 9.8 custom-call.19
  304.8 37.0 %all-reduce.7 = (f32[1024]{0:T(1024)S(1)}, f32[1024]{0:T(1024)S(1)}) all-reduce(f32[1024]{0:T(1024)S(1)} %get-tuple-element.184, f32[1024]{0:T(1024)S(1)} %get-tuple-element.183), channel_id=1, replica_groups=mesh['dp'=16,'sub'=2] {'dp','sub'}, use_global_device_ids=true, to_apply=%region_34.36 | all-reduce | flops 2048 | bytes 16384 | tf_op jit(solution)/shard_map/psum | solution.py:201
  342.4 6.5 fusion.99
  368.8 41.5 %all-reduce.6 = (f32[2048]{0:T(1024)S(1)}, f32[2048]{0:T(1024)S(1)}) all-reduce(f32[2048]{0:T(1024)S(1)} %get-tuple-element.170, f32[2048]{0:T(1024)S(1)} %get-tuple-element.169), channel_id=1, replica_groups=mesh['dp'=16,'sub'=2] {'dp','sub'}, use_global_device_ids=true, to_apply=%region_38.40 | all-reduce | flops 4096 | bytes 32768 | tf_op jit(solution)/shard_map/psum | solution.py:252
  410.3 5.0 multiply_convert_fusion
  417.7 39.6 %all-reduce.5 = (f32[512]{0:T(512)S(1)}, f32[512]{0:T(512)S(1)}) all-reduce(f32[512]{0:T(512)S(1)} %get-tuple-element.180, f32[512]{0:T(512)S(1)} %get-tuple-element.179), channel_id=1, replica_groups=mesh['dp'=16,'sub'=2] {'dp','sub'}, use_global_device_ids=true, to_apply=%region_42.44 | all-reduce | flops 1024 | bytes 8192 | tf_op jit(solution)/shard_map/psum | solution.py:283
  461.4 4.9 convolution_bitcast_fusion.3
  466.4 9.1 convolution_bitcast_fusion.2
  484.0 5.2 copy.141
  490.4 5.4 convolution_bitcast_fusion.1
  495.8 9.8 copy.140
  518.1 40.8 %all-reduce.4 = (f32[512]{0:T(512)S(1)}, f32[512]{0:T(512)S(1)}) all-reduce(f32[512]{0:T(512)S(1)} %get-tuple-element.178, f32[512]{0:T(512)S(1)} %get-tuple-element.177), channel_id=1, replica_groups=mesh['dp'=16,'sub'=2] {'dp','sub'}, use_global_device_ids=true, to_apply=%region_47.49 | all-reduce | flops 1024 | bytes 8192 | tf_op jit(solution)/shard_map/psum | solution.py:318
  564.7 5.6 copy.142
  573.9 4.9 constant_dynamic-update-slice_fusion.14
  587.3 27.2 %reshape.655 = f32[32,208896]{1,0:T(8,128)} reshape(f32[6684672]{0:T(1024)} %fusion) | data formatting | bytes 53477376 | tf_op jit(solution)/shard_map/reshape | solution.py:357
  614.6 410.0 %all-reduce.14.cloned.1.call-done = f32[32,208896]{1,0:T(8,128)} async-done(((f32[32,208896]{1,0:T(8,128)}), f32[32,208896]{1,0:T(8,128)}) %all-reduce.14.cloned.1.call-update) | async-done | bytes 26738704
  1040.1 150.9 %all-gather.3.cloned.1.call-done = f32[32,1,208896]{2,1,0:T(1,128)} async-done(((f32[1,1,208896]{2,1,0:T(1,128)}), f32[32,1,208896]{2,1,0:T(1,128)}) %all-gather.3.cloned.1.call-update) | async-done | bytes 26738704 | tf_op jit(solution)/shard_map/all_gather | solution.py:362
  1190.9 78.1 %reduce.33 = f32[32,208896]{1,0:T(8,128)} reduce(f32[32,1,208896]{2,1,0:T(1,128)} %all-gather.3.cloned.1.call-done, f32[]{:T(128)} %constant.412), dimensions={1}, to_apply=%all-gather.reduce_sub_computation | reduce | bytes 53477380 | tf_op jit(solution)/shard_map/all_gather | solution.py:362
  1269.1 30.0 %slice.521 = f32[6528,1024]{1,0:T(8,128)} reshape(f32[32,208896]{1,0:T(8,128)} %reduce.33) | data formatting | bytes 53477376 | tf_op jit(solution)/shard_map/slice | solution.py:366
  1299.1 27.9 %slice.519 = f32[3264,2048]{1,0:T(8,128)} reshape(f32[32,208896]{1,0:T(8,128)} %reduce.33) | data formatting | bytes 53477376 | tf_op jit(solution)/shard_map/slice | solution.py:366
  1326.9 27.2 %slice.516 = f32[13056,512]{1,0:T(8,128)} reshape(f32[32,208896]{1,0:T(8,128)} %reduce.33) | data formatting | bytes 53477376 | tf_op jit(solution)/shard_map/slice | solution.py:366
  1356.0 8.3 slice.546
  1364.3 11.2 reshape.657
  1375.5 8.4 slice.548
  (328 shorter events, 138.4 us)
Async XLA Ops:
  7.2 109.3 %copy-start = (bf16[512,2048]{1,0:T(8,128)(2,1)S(1)}, bf16[512,2048]{1,0:T(8,128)(2,1)}, u32[]{:S(2)}) copy-start(bf16[512,2048]{1,0:T(8,128)(2,1)} %param.37) | copy-start | bytes 6291460
  7.2 1017.4 %all-reduce.14.cloned.1.call-start = ((), (), s32[]{:S(2)}) async-start(), calls=%async_computation.1 | async-start | bytes 53477376
  10.5 167.2 %copy-start.62 = (f32[8]{0:T(128)}, f32[8]{0:T(128)S(1)}, u32[]{:S(2)}) copy-start(f32[8]{0:T(128)S(1)} %get-tuple-element.187) | copy-start | bytes 100
  11.2 161.5 %copy-start.58 = (bf16[8,49]{1,0:T(8,128)(2,1)}, bf16[8,49]{1,0:T(8,128)(2,1)S(1)}, u32[]{:S(2)}) copy-start(bf16[8,49]{1,0:T(8,128)(2,1)S(1)} %get-tuple-element.245) | copy-start | bytes 2356
  12.0 57.1 %copy-start.39 = (f32[1,512]{1,0:T(1,128)}, f32[1,512]{1,0:T(1,128)S(1)}, u32[]{:S(2)}) copy-start(f32[1,512]{1,0:T(1,128)S(1)} %get-tuple-element.246) | copy-start | bytes 6148
  12.0 57.1 %copy-start.51 = (f32[1,512]{1,0:T(1,128)}, f32[1,512]{1,0:T(1,128)S(1)}, u32[]{:S(2)}) copy-start(f32[1,512]{1,0:T(1,128)S(1)} %get-tuple-element.247) | copy-start | bytes 6148
  12.8 103.7 %copy-start.64 = (f32[1,512]{1,0:T(1,128)}, f32[1,512]{1,0:T(1,128)S(1)}, u32[]{:S(2)}) copy-start(f32[1,512]{1,0:T(1,128)S(1)} %get-tuple-element.242) | copy-start | bytes 6148
  12.8 103.7 %copy-start.73 = (f32[1,512]{1,0:T(1,128)}, f32[1,512]{1,0:T(1,128)S(1)}, u32[]{:S(2)}) copy-start(f32[1,512]{1,0:T(1,128)S(1)} %get-tuple-element.243) | copy-start | bytes 6148
  14.2 290.3 %copy-start.37 = (f32[1,1024]{1,0:T(1,128)}, f32[1,1024]{1,0:T(1,128)S(1)}, u32[]{:S(2)}) copy-start(f32[1,1024]{1,0:T(1,128)S(1)} %get-tuple-element.240) | copy-start | bytes 12292
  15.1 157.7 %copy-start.29 = (f32[1,2048]{1,0:T(1,128)}, f32[1,2048]{1,0:T(1,128)S(1)}, u32[]{:S(2)}) copy-start(f32[1,2048]{1,0:T(1,128)S(1)} %get-tuple-element.235) | copy-start | bytes 24580
  15.1 157.7 %copy-start.34 = (f32[1,2048]{1,0:T(1,128)}, f32[1,2048]{1,0:T(1,128)S(1)}, u32[]{:S(2)}) copy-start(f32[1,2048]{1,0:T(1,128)S(1)} %get-tuple-element.236) | copy-start | bytes 24580
  172.8 47.0 %copy-start.19 = (bf16[1024,128]{1,0:T(8,128)(2,1)S(1)}, bf16[1024,128]{1,0:T(8,128)(2,1)}, u32[]{:S(2)}) copy-start(bf16[1024,128]{1,0:T(8,128)(2,1)} %param.39) | copy-start | bytes 786436
  177.7 110.2 %copy-start.20 = (f32[8,2048]{1,0:T(8,128)}, f32[8,2048]{1,0:T(8,128)S(1)}, u32[]{:S(2)}) copy-start(f32[8,2048]{1,0:T(8,128)S(1)} %multiply_reduce_fusion.1) | copy-start | bytes 196612
  219.7 122.1 %copy-start.47 = (f32[1024]{0:T(1024)}, f32[1024]{0:T(1024)S(1)}, u32[]{:S(2)}) copy-start(f32[1024]{0:T(1024)S(1)} %get-tuple-element.237) | copy-start | bytes 12292
  304.5 37.4 %copy-start.41 = (f32[8,128]{1,0:T(8,128)}, f32[8,128]{1,0:T(8,128)S(1)}, u32[]{:S(2)}) copy-start(f32[8,128]{1,0:T(8,128)S(1)} %fusion.92) | copy-start | bytes 12292
  352.9 11.2 copy-start.27
  364.1 46.2 %copy-start.53 = (f32[2048]{0:T(1024)S(1)}, f32[2048]{0:T(1024)}, u32[]{:S(2)}) copy-start(f32[2048]{0:T(1024)} %get-tuple-element.211) | copy-start | bytes 24580
  415.3 42.0 %copy-start.67 = (f32[512]{0:T(512)S(1)}, f32[512]{0:T(512)}, u32[]{:S(2)}) copy-start(f32[512]{0:T(512)} %get-tuple-element.209) | copy-start | bytes 6148
  417.7 43.7 %copy-start.24 = (f32[8,49,512]{2,1,0:T(8,128)S(1)}, f32[8,49,512]{2,1,0:T(8,128)}, u32[]{:S(2)}) copy-start(f32[8,49,512]{2,1,0:T(8,128)} %copy-done.22) | copy-start | bytes 2408452
  466.4 9.7 copy-start.68
  466.4 16.1 %copy-start.12 = (bf16[8,7,7,512]{3,2,1,0:T(8,128)(2,1)S(1)}, bf16[8,7,7,512]{3,2,1,0:T(8,128)(2,1)}, u32[]{:S(2)}) copy-start(bf16[8,7,7,512]{3,2,1,0:T(8,128)(2,1)} %copy.123) | copy-start | bytes 1204228
  495.8 9.8 copy-start.25
  516.0 42.8 %copy-start.66 = (f32[512]{0:T(512)S(1)}, f32[512]{0:T(512)}, u32[]{:S(2)}) copy-start(f32[512]{0:T(512)} %get-tuple-element.206) | copy-start | bytes 6148
  516.2 45.0 %copy-start.59 = (bf16[8,49]{1,0:T(8,128)(2,1)S(1)}, bf16[8,49]{1,0:T(8,128)(2,1)}, u32[]{:S(2)}) copy-start(bf16[8,49]{1,0:T(8,128)(2,1)} %copy-done.58) | copy-start | bytes 2356
  516.3 44.9 %copy-start.7 = (bf16[8,49,2048]{2,0,1:T(8,128)(2,1)S(1)}, bf16[8,49,2048]{2,0,1:T(8,128)(2,1)}, u32[]{:S(2)}) copy-start(bf16[8,49,2048]{2,0,1:T(8,128)(2,1)} %param.32) | copy-start | bytes 4816900
  570.2 11.6 slice-start.5
  614.5 414.3 %copy-start.6 = (bf16[8,49,2048]{2,1,0:T(8,128)(2,1)S(1)}, bf16[8,49,2048]{2,1,0:T(8,128)(2,1)}, u32[]{:S(2)}) copy-start(bf16[8,49,2048]{2,1,0:T(8,128)(2,1)} %copy_multiply_fusion) | copy-start | bytes 4816900
  614.5 414.3 %copy-start.28 = (f32[8,2048]{1,0:T(8,128)S(1)}, f32[8,2048]{1,0:T(8,128)}, u32[]{:S(2)}) copy-start(f32[8,2048]{1,0:T(8,128)} %copy-done.27) | copy-start | bytes 196612
  614.5 414.3 %copy-start.31 = (f32[1,2048]{1,0:T(1,128)S(1)}, f32[1,2048]{1,0:T(1,128)}, u32[]{:S(2)}) copy-start(f32[1,2048]{1,0:T(1,128)} %copy-done.29) | copy-start | bytes 24580
  614.5 414.3 %copy-start.36 = (f32[1,2048]{1,0:T(1,128)S(1)}, f32[1,2048]{1,0:T(1,128)}, u32[]{:S(2)}) copy-start(f32[1,2048]{1,0:T(1,128)} %copy-done.34) | copy-start | bytes 24580
  614.5 576.4 %all-gather.3.cloned.1.call-start = ((), (), s32[]{:S(2)}) async-start(), calls=%async_computation | async-start | bytes 27574272 | tf_op jit(solution)/shard_map/all_gather | solution.py:362
  1383.9 9.5 copy-start.1
  (56 other events, 241.0 us)
Sparse Core Ops, SparseCore 0:
  614.7 409.8 all-reduce.13
  1028.9 162.0 all-gather.2
where the time goes:
time: 1410 us; the launch traced here: 1400 us
  waiting for transfers between devices  561 us (40%)
  blocking collectives  374 us (27%)
  local copies, waits for them, and re-layouts  225 us (16%)
  other arithmetic  155 us (11%)
  matrix products  69.6 us (5%)
  between operations  17.4 us (1%)
    unnamed x3, waiting for transfers between devices  410 us
    all_gather x1, waiting for transfers between devices, shards(): lax.all_gather(own_share, ('dp', 'sub'), axis=0, tiled=True).reshape(-1)  151 us
    slice x8, local copies, waits for them, and re-layouts, shards(): whole_grads[offset:offset + piece_grad.size].reshape(piece_grad.shape)  113 us
    all_gather x1, other arithmetic, shards(): lax.all_gather(own_share, ('dp', 'sub'), axis=0, tiled=True).reshape(-1)  78.1 us
    psum x1, blocking collectives, front(): lax.psum((sum_expand, square_expand), ('dp', 'sub'))  50.8 us
    unnamed x205, local copies, waits for them, and re-layouts  48.8 us
    psum x1, blocking collectives, front(): lax.psum((sum_reduce, square_reduce, jnp.sum(counts)), ('dp', 'sub'))  42.3 us
    all_gather x1, blocking collectives, shards(): all_codes = lax.all_gather(codes, ('dp', 'sub'), axis=0, tiled=True)  41.6 us
  transfers between devices with their start and end apart: 2, of which 2 were waited for; matrix products, arithmetic and copies ran while one was open for 1% of the time, Pallas kernels for 0%

commit v1 on v0

v1 whole, which is shorter than its diff:
```python
import functools

import jax
import jax.numpy as jnp
from jax import lax
from jax.experimental import pallas as pl
from jax.experimental.pallas import tpu as pltpu
from jax.sharding import PartitionSpec as P

MESH = pl.DeviceIdType.MESH
SIDE = 7

def place():
    dp = lax.axis_index("dp")
    sub = lax.axis_index("sub")
    z = dp // 4
    y = lax.rem(dp // 2, 2)
    x = lax.rem(dp, 2)
    ring = 3 * y + x - 2 * x * y
    return dp, sub, z, ring

def ring_dp(z, ring):
    ring = lax.rem(ring + 4, 4)
    y = ring // 2
    odd = lax.rem(ring, 2)
    x = odd + y - 2 * odd * y
    return z * 4 + y * 2 + x

def dev(dp, sub):
    return {"dp": dp, "sub": sub}

def greet_all():
    dp, sub, _, _ = place()
    me = dp * 2 + sub
    total = lax.axis_size("dp") * lax.axis_size("sub")
    barrier = pltpu.get_barrier_semaphore()
    @pl.loop(1, total)
    def _(step):
        other = lax.rem(me + step, total)
        pl.semaphore_signal(barrier, inc=1, device_id=dev(other // 2, lax.rem(other, 2)), device_id_type=MESH)
    pl.semaphore_wait(barrier, total - 1)

def remote(src, dst, send, recv, where):
    return pltpu.make_async_remote_copy(src_ref=src, dst_ref=dst, send_sem=send, recv_sem=recv, device_id=dev(*where), device_id_type=MESH)

def arrived(ref, sem):
    pltpu.make_async_copy(ref, ref, sem).wait()

def add_into(dst, src, rows):
    step = 16 if rows % 16 == 0 else 8
    @pl.loop(0, rows // step)
    def _(k):
        at = pl.ds(pl.multiple_of(k * step, 8), step)
        dst[at, :] = dst[at, :] + src[at, :]

def rows_at(ref, start, size):
    return ref.at[pl.ds(pl.multiple_of(start, 8), size)]

class Line:
    pass

SEMS = 24
def when(cond, body):
    pl.when(cond)(body)

class Job:
    def __init__(self, ring_first, rows, acc, other, out, sbuf, rbuf, send, recv, loc):
        self.__dict__.update(locals())

    def run(self):
        dp, sub, z, q = place()
        rows, acc, out, rbuf, send, recv, loc = self.rows, self.acc, self.out, self.rbuf, self.send, self.recv, self.loc
        nxt, prv = (ring_dp(z, q + 1), sub), (ring_dp(z, q + 3), sub)
        up, dn = (dp + 4, sub), (dp - 4, sub)
        sib = (dp, 1 - sub)
        pending = []
        def go(cond, src, dst, s, r, where):
            def body(): remote(src, dst, send.at[s], recv.at[r], where).start()
            if cond is None: body()
            else: when(cond, body)
            pending.append((cond, src, s))
        def got(cond, ref, r, then=None):
            def body():
                arrived(ref, recv.at[r])
                if then is not None: then()
            if cond is None: body()
            else: when(cond, body)
        go(None, self.other, self.sbuf, 0, 0, sib)
        yield
        got(None, self.sbuf, 0)
        add_into(acc, self.sbuf, rows)
        D = rows
        big = D // 4
        small = D // 16
        def ring_rs(base, block):
            half = block // 2
            r0a = rows_at(rbuf, self.off, half); r0b = rows_at(rbuf, self.off + half, half)
            r1a = rows_at(rbuf, self.off + 2 * half, block); r1b = rows_at(rbuf, self.off + 2 * half + block, block)
            self.off += 2 * half + 2 * block
            blk = lambda k, h=0, n=block: rows_at(acc, base + lax.rem(q + k, 4) * block + h, n)
            go(None, blk(2, 0, half), r0a, 1, 1, nxt)
            go(None, blk(2, half, half), r0b, 2, 2, prv)
            yield
            got(None, r0a, 1); add_into(blk(1, 0, half), r0a, half)
            go(None, blk(1), r1a, 3, 3, nxt)
            got(None, r0b, 2); add_into(blk(3, half, half), r0b, half)
            go(None, blk(3), r1b, 4, 4, prv)
            yield
            got(None, r1a, 3); add_into(blk(0), r1a, block)
            got(None, r1b, 4); add_into(blk(0), r1b, block)
        def line_rs(base, chunk):
            la = [rows_at(rbuf, self.off + k * chunk, chunk) for k in range(3)]
            ra = [rows_at(rbuf, self.off + (3 + k) * chunk, chunk) for k in range(3)]
            self.off += 6 * chunk
            at = lambda j: rows_at(acc, base + jnp.clip(j, 0, 3) * chunk, chunk)
            for t in range(3):
                go(z <= t, at(3 + z - t), la[t], 5 + t, 5 + t, up)
                go(z >= 3 - t, at(z - 3 + t), ra[t], 8 + t, 8 + t, dn)
                yield
                got(jnp.logical_and(z >= 1, z <= t + 1), la[t], 5 + t, lambda: add_into(at(2 + z - t), la[t], chunk))
                got(jnp.logical_and(z <= 2, z >= 2 - t), ra[t], 8 + t, lambda: add_into(at(z - 2 + t), ra[t], chunk))
        def line_ag(base, chunk, first):
            at = lambda j: rows_at(out, base + jnp.clip(j, 0, 3) * chunk, chunk)
            for t in range(3):
                src_r = first if t == 0 and first is not None else at(z - t)
                src_l = first if t == 0 and first is not None else at(z + t)
                go(jnp.logical_and(z <= 2, z >= t), src_r, at(z - t), 11 + t, 11 + t, up)
                go(jnp.logical_and(z >= 1, z <= 3 - t), src_l, at(z + t), 14 + t, 14 + t, dn)
                yield
                got(z >= t + 1, at(z - 1 - t), 11 + t)
                got(z <= 2 - t, at(z + 1 + t), 14 + t)
        def ring_ag(base, block, first, after):
            half = block // 2
            blk = lambda k, h=0, n=block: rows_at(out, base + lax.rem(q + k, 4) * block + h, n)
            src = first if first is not None else blk(0)
            go(None, src, blk(0), 17, 17, nxt)
            go(None, src, blk(0), 18, 18, prv)
            yield
            got(None, blk(3), 17)
            go(None, blk(3, 0, half), blk(3, 0, half), 19, 19, nxt)
            after(blk(3), 21)
            got(None, blk(1), 18)
            go(None, blk(1, half, half), blk(1, half, half), 20, 20, prv)
            after(blk(1), 22)
            yield
            got(None, blk(2, 0, half), 19)
            got(None, blk(2, half, half), 20)
            after(blk(2), 23)
        self.off = 0
        share = lambda ref, s: go(None, ref, ref, s, 21, sib)
        if self.ring_first:
            yield from ring_rs(0, big)
            yield from line_rs(q * big, small)
            mine = rows_at(acc, q * big + z * small, small)
            own = rows_at(out, q * big + z * small, small)
            pltpu.make_async_copy(mine, own, loc).start()
            yield from line_ag(q * big, small, mine)
            pltpu.make_async_copy(mine, own, loc).wait()
            share(rows_at(out, q * big, big), 24)
            yield from ring_ag(0, big, None, share)
        else:
            yield from line_rs(0, big)
            yield from ring_rs(z * big, small)
            mine = rows_at(acc, z * big + q * small, small)
            own = rows_at(out, z * big + q * small, small)
            pltpu.make_async_copy(mine, own, loc).start()
            yield from ring_ag(z * big, small, mine, lambda ref, s: None)
            pltpu.make_async_copy(mine, own, loc).wait()
            share(rows_at(out, z * big, big), 21)
            yield from line_ag(0, big, None)
            for k, s in ((1, 22), (2, 23), (3, 24)):
                share(rows_at(out, lax.rem(z + k, 4) * big, big), s)
        yield
        arrived(self.sib_out, recv.at[21])
        for cond, ref, s in pending:
            def body(ref=ref, s=s): arrived(ref, send.at[s])
            if cond is None: body()
            else: when(cond, body)

SEMS = 25

def rbuf_rows(ring_first, rows):
    big, small = rows // 4, rows // 16
    if ring_first: return big * 3 + 6 * small
    return small * 3 + 6 * big
def plan():
    return [(0, 0, 896, 0, 512, True), (0, 896, 256, 0, 512, False), (0, 1152, 896, 0, 512, True), (0, 2048, 256, 0, 512, False),
            (1, 0, 768, 0, 512, True), (1, 768, 256, 0, 512, False), (2, 0, 256, 0, 1536, True), (2, 0, 256, 1536, 512, False)]
STARTS = [0, 0, 2, 2, 4, 4, 6, 6]
def bulk_kernel(starts, *refs):
    n = 3
    g = refs[:n]; out = refs[n:2 * n]; acc = refs[2 * n:3 * n]; sbuf = refs[3 * n:4 * n]
    jobs_p = plan()
    rb = refs[4 * n:4 * n + len(jobs_p)]
    send, recv, loc, load = refs[4 * n + len(jobs_p):]
    dp, sub, z, q = place()
    half = [r.shape[0] // 2 for r in g]
    for k in range(n):
        pltpu.make_async_copy(g[k].at[pl.ds(pl.multiple_of(sub * half[k], 8), half[k])], acc[k], load.at[k]).start()
    greet_all()
    for k in range(n):
        pltpu.make_async_copy(g[k].at[pl.ds(pl.multiple_of(sub * half[k], 8), half[k])], acc[k], load.at[k]).wait()
    gens = []
    for j, (k, r0, rows, c0, cols, rf) in enumerate(jobs_p):
        cut = lambda ref, base: ref.at[pl.ds(pl.multiple_of(base + r0, 8), rows), pl.ds(c0, cols)]
        job = Job(rf, rows, cut(acc[k], 0), cut(g[k], (1 - sub) * half[k]), cut(out[k], sub * half[k]), cut(sbuf[k], 0), rb[j], send.at[j], recv.at[j], loc.at[j])
        job.sib_out = cut(out[k], (1 - sub) * half[k])
        gens.append(job.run())
    tick = 0
    live = dict(enumerate(gens))
    while live:
        for j in sorted(live):
            if tick >= starts[j]:
                try: next(live[j])
                except StopIteration: live.pop(j)
        tick += 1

def bulk(gs, starts=STARTS, cid=3):
    jobs_p = plan()
    n = 3
    shapes = [x.shape for x in gs]
    scratch = [pltpu.VMEM((s[0] // 2, s[1]), jnp.float32) for s in shapes] * 2
    scratch += [pltpu.VMEM((rbuf_rows(rf, rows), cols), jnp.float32) for (k, r0, rows, c0, cols, rf) in jobs_p]
    scratch += [pltpu.SemaphoreType.DMA((len(jobs_p), SEMS)), pltpu.SemaphoreType.DMA((len(jobs_p), SEMS)), pltpu.SemaphoreType.DMA((len(jobs_p),)), pltpu.SemaphoreType.DMA((n,))]
    return pl.pallas_call(functools.partial(bulk_kernel, starts),
        out_shape=[jax.ShapeDtypeStruct(s, jnp.float32) for s in shapes],
        in_specs=[pl.BlockSpec(memory_space=pl.ANY)] * n, out_specs=[pl.BlockSpec(memory_space=pl.ANY)] * n,
        scratch_shapes=scratch,
        compiler_params=pltpu.CompilerParams(collective_id=cid, has_side_effects=True, vmem_limit_bytes=56 << 20))(*gs)


def sums_kernel(x_ref, o_ref, buf, send, recv):
    dp, sub, _, _ = place()
    me = dp * 2 + sub
    greet_all()
    buf[me] = x_ref[...]
    @pl.loop(1, 32)
    def _(step):
        other = lax.rem(me + step, 32)
        remote(buf.at[me], buf.at[me], send, recv, (other // 2, lax.rem(other, 2))).start()
    many = buf.at[pl.ds(0, 31)]
    arrived(many, recv)
    o_ref[...] = jnp.sum(buf[...], axis=0)
    arrived(many, send)


def sums(parts, ident):
    if lax.axis_size("dp") != 16 or lax.axis_size("sub") != 2:
        return lax.psum(parts, ("dp", "sub"))
    flat = jnp.concatenate([part.reshape(-1) for part in parts])
    rows = -(-flat.shape[0] // 1024) * 8
    flat = jnp.pad(flat, (0, rows * 128 - flat.shape[0])).reshape(rows, 128)
    total = pl.pallas_call(
        sums_kernel,
        out_shape=jax.ShapeDtypeStruct((rows, 128), jnp.float32),
        in_specs=[pl.BlockSpec(memory_space=pltpu.VMEM)],
        out_specs=pl.BlockSpec(memory_space=pltpu.VMEM),
        scratch_shapes=[pltpu.VMEM((32, rows, 128), jnp.float32), pltpu.SemaphoreType.DMA, pltpu.SemaphoreType.DMA],
        compiler_params=pltpu.CompilerParams(collective_id=ident, has_side_effects=True),
    )(flat).reshape(-1)
    results = []
    offset = 0
    for part in parts:
        results.append(total[offset : offset + part.size].reshape(part.shape))
        offset += part.size
    return results


def weight_sums(spatial, reduce, expand):
    if lax.axis_size("dp") != 16 or lax.axis_size("sub") != 2:
        return lax.psum((spatial, reduce, expand), ("dp", "sub"))
    return bulk((spatial, reduce, expand))


def whiten(codes, pairing):
    highest = lax.Precision.HIGHEST
    total = codes.shape[0]
    centre = jnp.sum(codes, axis=0) / total
    moved = codes - centre
    covariance = jnp.dot(moved.T, moved, precision=highest) / total
    covariance = covariance + whiten_floor * jnp.eye(codes.shape[1], dtype=jnp.float32)
    factor = jnp.linalg.cholesky(covariance)
    inverse = lax.linalg.triangular_solve(factor, jnp.eye(codes.shape[1], dtype=jnp.float32), left_side=True, lower=True)
    white = jnp.dot(moved, inverse.T, precision=highest)
    scale = lax.rsqrt(jnp.sum(white * white, axis=1, keepdims=True) + epsilon)
    unit = white * scale
    same = (pairing[:, None] == pairing[None, :]).astype(jnp.float32)
    gap = 2.0 * unit - jnp.dot(same, unit, precision=highest)
    loss_value = jnp.sum(gap * gap) / total
    grad_unit = 0.5 * (2.0 * gap - jnp.dot(same, gap, precision=highest))
    grad_white = scale * grad_unit - white * scale * scale * scale * jnp.sum(white * grad_unit, axis=1, keepdims=True)
    gram = jnp.dot(grad_white.T, white, precision=highest)
    row = lax.broadcasted_iota(jnp.int32, gram.shape, 0)
    column = lax.broadcasted_iota(jnp.int32, gram.shape, 1)
    lower = jnp.where(row > column, gram, jnp.where(row == column, 0.5 * gram, 0.0))
    both = lower + lower.T
    grad_moved = jnp.dot(grad_white - jnp.dot(white, both, precision=highest) / total, inverse, precision=highest)
    return loss_value, grad_moved - jnp.sum(grad_moved, axis=0) / total


epsilon = 1e-05
whiten_floor = 0.001


def silu_slope(values):
    sigmoid_value = jax.nn.sigmoid(values)
    return sigmoid_value * (1.0 + values * (1.0 - sigmoid_value))


def moments(sum_value, sum_square, total_count):
    centre = sum_value / total_count
    return (centre, lax.rsqrt(sum_square / total_count - centre * centre + epsilon))


def make_columns(activation):
    images_here, pixel_count, inner_width = activation.shape
    grid_map = activation.reshape(images_here, SIDE, SIDE, inner_width)
    padded = jnp.pad(grid_map, ((0, 0), (1, 1), (1, 1), (0, 0)))
    pieces = [
        padded[:, tap_row : tap_row + SIDE, tap_col : tap_col + SIDE, :]
        for tap_row in range(3)
        for tap_col in range(3)
    ]
    return jnp.concatenate(pieces, axis=3).reshape(images_here * pixel_count, 9 * inner_width)


def fold_columns(columns, images_here, inner_width):
    tap_grads = columns.reshape(images_here, SIDE, SIDE, 9, inner_width)
    padded = jnp.zeros((images_here, SIDE + 2, SIDE + 2, inner_width), jnp.float32)
    for tap_row in range(3):
        for tap_col in range(3):
            padded = padded.at[:, tap_row : tap_row + SIDE, tap_col : tap_col + SIDE, :].add(
                tap_grads[:, :, :, 3 * tap_row + tap_col, :]
            )
    return padded[:, 1 : SIDE + 1, 1 : SIDE + 1, :].reshape(images_here, SIDE * SIDE, inner_width)


def pixel_sums(values, weight):
    return (jnp.sum(values * weight, axis=(0, 1)), jnp.sum(values * values * weight, axis=(0, 1)))


def front(
    masked_low,
    weight,
    counts,
    w_reduce,
    w_spatial,
    w_expand,
    norm_reduce,
    norm_spatial,
    norm_expand,
):
    images_here, pixel_count, width = masked_low.shape
    inner_width = w_reduce.shape[1]
    rows_here = images_here * pixel_count
    reduced = jnp.dot(
        masked_low.reshape(rows_here, width), w_reduce, preferred_element_type=jnp.float32
    ).reshape(images_here, pixel_count, inner_width)
    sum_reduce, square_reduce = pixel_sums(reduced, weight)
    sum_reduce, square_reduce, valid_total = sums((sum_reduce, square_reduce, jnp.sum(counts)), 10)
    centre_reduce, scale_reduce = moments(sum_reduce, square_reduce, valid_total)
    normed_reduce = (reduced - centre_reduce) * scale_reduce
    level_reduce = norm_reduce[0] * normed_reduce + norm_reduce[1]
    act_reduce = (weight * jax.nn.silu(level_reduce)).astype(jnp.bfloat16)
    columns = make_columns(act_reduce)
    spatial = jnp.dot(
        columns, w_spatial.reshape(9 * inner_width, inner_width), preferred_element_type=jnp.float32
    ).reshape(images_here, pixel_count, inner_width)
    sum_spatial, square_spatial = pixel_sums(spatial, weight)
    sum_spatial, square_spatial = sums((sum_spatial, square_spatial), 11)
    centre_spatial, scale_spatial = moments(sum_spatial, square_spatial, valid_total)
    normed_spatial = (spatial - centre_spatial) * scale_spatial
    level_spatial = norm_spatial[0] * normed_spatial + norm_spatial[1]
    act_spatial = (weight * jax.nn.silu(level_spatial)).astype(jnp.bfloat16)
    expanded = jnp.dot(
        act_spatial.reshape(rows_here, inner_width), w_expand, preferred_element_type=jnp.float32
    ).reshape(images_here, pixel_count, width)
    sum_expand, square_expand = pixel_sums(expanded, weight)
    sum_expand, square_expand = sums((sum_expand, square_expand), 12)
    centre_expand, scale_expand = moments(sum_expand, square_expand, valid_total)
    normed_expand = (expanded - centre_expand) * scale_expand
    summed = masked_low.astype(jnp.float32) + norm_expand[0] * normed_expand + norm_expand[1]
    stats = (
        valid_total,
        centre_reduce,
        scale_reduce,
        centre_spatial,
        scale_spatial,
        centre_expand,
        scale_expand,
    )
    return (
        (
            normed_reduce,
            level_reduce,
            columns,
            normed_spatial,
            level_spatial,
            act_spatial,
            normed_expand,
            summed,
        ),
        stats,
    )


def norm_back(upstream, normed, gain, scale_value, sum_grad, dot_grad, total_count):
    return gain * scale_value * (upstream - (sum_grad + normed * dot_grad) / total_count)


def shards(
    images,
    pixel_mask,
    pairing,
    w_reduce,
    w_spatial,
    w_expand,
    w_project,
    w_code,
    norm_reduce,
    norm_spatial,
    norm_expand,
    norm_project,
):
    images_here, pixel_count, width = images.shape
    inner_width = w_reduce.shape[1]
    images_total = pairing.shape[0]
    rows_here = images_here * pixel_count
    highest = lax.Precision.HIGHEST
    weight = pixel_mask.astype(jnp.float32)[:, :, None]
    counts = jnp.sum(weight, axis=1)
    masked_low = images * weight.astype(jnp.bfloat16)
    project_full = w_project.astype(jnp.float32)
    code_full = w_code.astype(jnp.float32)
    saved, stats = front(
        masked_low,
        weight,
        counts,
        w_reduce,
        w_spatial,
        w_expand,
        norm_reduce,
        norm_spatial,
        norm_expand,
    )
    (
        normed_reduce,
        level_reduce,
        columns,
        normed_spatial,
        level_spatial,
        act_spatial,
        normed_expand,
        summed,
    ) = saved
    (
        valid_total,
        centre_reduce,
        scale_reduce,
        centre_spatial,
        scale_spatial,
        centre_expand,
        scale_expand,
    ) = stats
    output = weight * jax.nn.silu(summed)
    own_pooled = jnp.sum(output, axis=1) / counts
    pooled = lax.all_gather(own_pooled, ("dp", "sub"), axis=0, tiled=True)
    projected = jnp.dot(pooled, project_full, precision=highest)
    centre_project, scale_project = moments(
        jnp.sum(projected, axis=0), jnp.sum(projected * projected, axis=0), float(images_total)
    )
    normed_project = (projected - centre_project) * scale_project
    level_project = norm_project[0] * normed_project + norm_project[1]
    hidden = jax.nn.silu(level_project)
    codes = jnp.dot(hidden, code_full, precision=highest)
    loss_value, grad_codes = whiten(codes, pairing)
    grad_w_code = jnp.dot(hidden.T, grad_codes, precision=highest)
    grad_hidden = jnp.dot(grad_codes, code_full.T, precision=highest)
    grad_level_project = grad_hidden * silu_slope(level_project)
    sum_project_grad = jnp.sum(grad_level_project, axis=0)
    dot_project_grad = jnp.sum(grad_level_project * normed_project, axis=0)
    grad_norm_project = jnp.stack([dot_project_grad, sum_project_grad])
    grad_projected = norm_back(
        grad_level_project,
        normed_project,
        norm_project[0],
        scale_project,
        sum_project_grad,
        dot_project_grad,
        float(images_total),
    )
    grad_w_project = jnp.dot(pooled.T, grad_projected, precision=highest)
    own_start = lax.axis_index(("dp", "sub")) * images_here
    own_projected = lax.dynamic_slice_in_dim(grad_projected, own_start, images_here, 0)
    grad_pooled = jnp.dot(own_projected, project_full.T, precision=highest)
    grad_summed = weight * (grad_pooled / counts)[:, None, :] * silu_slope(summed)
    sum_expand_grad, dot_expand_grad = sums(
        (jnp.sum(grad_summed, axis=(0, 1)), jnp.sum(grad_summed * normed_expand, axis=(0, 1))), 13
    )
    grad_norm_expand = jnp.stack([dot_expand_grad, sum_expand_grad])
    grad_expanded = (
        (
            weight
            * norm_back(
                grad_summed,
                normed_expand,
                norm_expand[0],
                scale_expand,
                sum_expand_grad,
                dot_expand_grad,
                valid_total,
            )
        )
        .astype(jnp.bfloat16)
        .reshape(rows_here, width)
    )
    grad_w_expand = jnp.einsum(
        "rm,rc->mc",
        act_spatial.reshape(rows_here, inner_width),
        grad_expanded,
        preferred_element_type=jnp.float32,
    )
    grad_act_spatial = jnp.einsum(
        "rc,mc->rm", grad_expanded, w_expand, preferred_element_type=jnp.float32
    ).reshape(images_here, pixel_count, inner_width)
    grad_level_spatial = grad_act_spatial * weight * silu_slope(level_spatial)
    sum_spatial_grad, dot_spatial_grad = sums(
        (
            jnp.sum(grad_level_spatial, axis=(0, 1)),
            jnp.sum(grad_level_spatial * normed_spatial, axis=(0, 1)),
        ),
        14,
    )
    grad_norm_spatial = jnp.stack([dot_spatial_grad, sum_spatial_grad])
    grad_spatial_out = (
        (
            weight
            * norm_back(
                grad_level_spatial,
                normed_spatial,
                norm_spatial[0],
                scale_spatial,
                sum_spatial_grad,
                dot_spatial_grad,
                valid_total,
            )
        )
        .astype(jnp.bfloat16)
        .reshape(rows_here, inner_width)
    )
    grad_w_spatial = jnp.einsum(
        "rk,rm->km", columns, grad_spatial_out, preferred_element_type=jnp.float32
    ).reshape(3, 3, inner_width, inner_width)
    grad_columns = jnp.einsum(
        "rm,km->rk",
        grad_spatial_out,
        w_spatial.reshape(9 * inner_width, inner_width),
        preferred_element_type=jnp.float32,
    )
    grad_act_reduce = fold_columns(grad_columns, images_here, inner_width)
    grad_level_reduce = grad_act_reduce * weight * silu_slope(level_reduce)
    sum_reduce_grad, dot_reduce_grad = sums(
        (
            jnp.sum(grad_level_reduce, axis=(0, 1)),
            jnp.sum(grad_level_reduce * normed_reduce, axis=(0, 1)),
        ),
        15,
    )
    grad_norm_reduce = jnp.stack([dot_reduce_grad, sum_reduce_grad])
    grad_reduced = (
        (
            weight
            * norm_back(
                grad_level_reduce,
                normed_reduce,
                norm_reduce[0],
                scale_reduce,
                sum_reduce_grad,
                dot_reduce_grad,
                valid_total,
            )
        )
        .astype(jnp.bfloat16)
        .reshape(rows_here, inner_width)
    )
    grad_w_reduce = jnp.einsum(
        "rc,rm->cm",
        masked_low.reshape(rows_here, width),
        grad_reduced,
        preferred_element_type=jnp.float32,
    )
    grad_input = jnp.einsum(
        "rm,cm->rc", grad_reduced, w_reduce, preferred_element_type=jnp.float32
    ).reshape(images_here, pixel_count, width)
    grad_images = weight * (grad_summed + grad_input)
    grad_w_spatial, grad_w_reduce, grad_w_expand = weight_sums(
        grad_w_spatial.reshape(9 * inner_width, inner_width), grad_w_reduce, grad_w_expand
    )
    return (
        loss_value,
        grad_images,
        grad_w_reduce,
        grad_w_spatial.reshape(3, 3, inner_width, inner_width),
        grad_w_expand,
        grad_w_project,
        grad_w_code,
        grad_norm_reduce,
        grad_norm_spatial,
        grad_norm_expand,
        grad_norm_project,
    )


def solution(mesh):
    placed = (
        P(("dp", "sub"), None, None),
        P(("dp", "sub"), None),
        P(),
        P(),
        P(),
        P(),
        P(),
        P(),
        P(),
        P(),
        P(),
        P(),
    )
    return jax.shard_map(
        shards,
        mesh=mesh,
        in_specs=placed,
        out_specs=(P(), P(("dp", "sub"), None, None), P(), P(), P(), P(), P(), P(), P(), P(), P()),
        check_vma=False,
    )
```

time: 1410 us -> 470 us (0.33)
  waiting for transfers between devices: 561 us -> 17.6 us
  blocking collectives: 374 us -> 0 us
  Pallas kernels: 0 us -> 229 us
  local copies, waits for them, and re-layouts: 225 us -> 63.5 us
  other arithmetic: 155 us -> 68.5 us
    unnamed x3 -> x1, waiting for transfers between devices: 410 us -> 0.02 us
    psum x8 -> x0, blocking collectives: 332 us -> none  [the longest x1 50.8 us: front(): lax.psum((sum_expand, square_expand), ('dp', 'sub'))]
    pallas_call x0 -> x7, Pallas kernels: none -> 229 us  [the longest x1 153 us: bulk(): pl.pallas_call(functools.partial(bulk_kernel, starts), out_shape=[jax.Sha...]
    all_gather x1, waiting for transfers between devices: 151 us -> 17.6 us  [shards(): pooled = lax.all_gather(own_pooled, ('dp', 'sub'), axis=0, tiled=True)]
    slice x9 -> x4, local copies, waits for them, and re-layouts: 114 us -> 3.52 us  [sums(): results.append(total[offset:offset + part.size].reshape(part.shape))]
    all_gather x1 -> x0, other arithmetic: 78.1 us -> none  [shards(): lax.all_gather(own_share, ('dp', 'sub'), axis=0, tiled=True).reshape(-1)]
    all_gather x1 -> x0, blocking collectives: 41.6 us -> none  [shards(): all_codes = lax.all_gather(codes, ('dp', 'sub'), axis=0, tiled=True)]
    reshape x2 -> x0, local copies, waits for them, and re-layouts: 38.4 us -> none  [the longest x1 27.2 us: shards(): flat_grads.reshape(device_count, share_length)]
  transfers between devices with their start and end apart: 2 -> 1, of which waited for: 2 -> 1; matrix products, arithmetic and copies ran while one was open for 1% -> 9% of each run, Pallas kernels for 0% -> 0%
where the time goes in v1:
time: 470 us; the launch traced here: 465 us
  Pallas kernels  229 us (49%)
  matrix products  69.2 us (15%)
  other arithmetic  68.5 us (15%)
  local copies, waits for them, and re-layouts  63.5 us (14%)
  waiting for transfers between devices  17.6 us (4%)
  between operations  17.1 us (4%)
    pallas_call x1, Pallas kernels, bulk(): pl.pallas_call(functools.partial(bulk_kernel, starts), out_shape=[jax.Sha...  153 us
    pallas_call x6, Pallas kernels, sums(): pl.pallas_call(sums_kernel, out_shape=jax.ShapeDtypeStruct((rows, 128), j...  76.4 us
    unnamed x149, local copies, waits for them, and re-layouts  26.4 us
    all_gather x1, waiting for transfers between devices, shards(): pooled = lax.all_gather(own_pooled, ('dp', 'sub'), axis=0, tiled=True)  17.6 us
    slice x9, local copies, waits for them, and re-layouts, make_columns(): padded[:, tap_row:tap_row + SIDE, tap_col:tap_col + SIDE, :]  15.6 us
    concatenate x11, local copies, waits for them, and re-layouts, make_columns(): jnp.concatenate(pieces, axis=3)  15.2 us
    another operation x3, other arithmetic, whiten(): factor = jnp.linalg.cholesky(covariance)  12.4 us
    another operation x2, other arithmetic, whiten(): lax.linalg.triangular_solve(factor, jnp.eye(codes.shape[1], dtype=jnp.flo...  10.5 us
  transfers between devices with their start and end apart: 1, of which 1 were waited for; matrix products, arithmetic and copies ran while one was open for 9% of the time, Pallas kernels for 0%

profile of v1, /device:TPU:0, one launch (start us, length us, event | category | flops | bytes accessed | tf_op | source)
XLA Modules:
  0.0 465.3 jit_solution(15220158738463662449)
XLA Ops:
  10.2 4.8 %multiply_reduce_fusion.11 = (f32[512]{0:T(512)S(1)}, f32[512]{0:T(512)S(1)}, f32[8,49,512]{2,1,0:T(8,128)S(1)}) fusion(f32[8,49]{1,0:T(8,128)S(1)} %get-tuple-element.205, bf16[2048,512]{1,0:T(8,128)(2,1)} %param.33, bf16[8,49,2048]{2,0,1:T(8,128)(2,1)} %param.30, bf16[8,49]{1,0:T(8,128)(2,1)S(1)} %get-tuple-element.204), kind=kOutput, calls=%fused_computation.62 | convolution fusion | flops 823888896 | bytes 4512048 | tf_op jit(solution)/shard_map/dot_general | solution.py:356
  16.3 13.4 %shard_map.203 = f32[16,128]{1,0:T(8,128)} custom-call(f32[16,128]{1,0:T(8,128)} %fusion.65.x_ref), custom_call_target="tpu_custom_call" | custom-call | tf_op jit(solution)/shard_map/pallas_call | solution.py:253
  38.5 3.3 multiply_reduce_fusion.9
  42.5 10.9 %shard_map.204 = f32[8,128]{1,0:T(8,128)} custom-call(f32[8,128]{1,0:T(8,128)} %pad_maximum_fusion.4.x_ref), custom_call_target="tpu_custom_call" | custom-call | tf_op jit(solution)/shard_map/pallas_call | solution.py:253
  56.7 4.6 multiply_reduce_fusion.3
  61.9 16.0 %shard_map.205 = f32[32,128]{1,0:T(8,128)} custom-call(f32[32,128]{1,0:T(8,128)} %pad_maximum_fusion.x_ref), custom_call_target="tpu_custom_call" | custom-call | tf_op jit(solution)/shard_map/pallas_call | solution.py:253
  80.6 4.9 %multiply_reduce_fusion.1 = f32[8,2048]{1,0:T(8,128)S(1)} fusion(f32[8,49]{1,0:T(8,128)S(1)} %get-tuple-element.205, f32[2048]{0:T(1024)S(1)} %bitcast.254, f32[2048]{0:T(1024)S(1)} %fusion.67, f32[8,49,2048]{2,1,0:T(8,128)} %get-tuple-element.214, f32[2048]{0:T(1024)S(1)} %get-tuple-element.169, f32[2048]{0:T(1024)S(1)} %bitcast.252, ...), kind=kLoop, calls=%fused_computation.4 | loop fusion | flops 10420224 | bytes 4917552 | tf_op jit(solution)/shard_map/reduce_sum | solution.py:466
  128.8 17.6 %all-gather.2.cloned.1.call-done = f32[256,2048]{1,0:T(8,128)} async-done(((f32[8,2048]{1,0:T(8,128)}), f32[256,2048]{1,0:T(8,128)}) %all-gather.2.cloned.1.call-update) | async-done | bytes 2097168 | tf_op jit(solution)/shard_map/all_gather | solution.py:467
  146.4 6.6 %fusion.83 = (f32[1024]{0:T(1024)S(1)}, f32[1024]{0:T(1024)S(1)}, f32[256,1024]{1,0:T(8,128)S(1)}) fusion(f32[256,2048]{1,0:T(8,128)} %all-gather.2.cloned.1.call-done, bf16[2048,1024]{1,0:T(8,128)(2,1)} %param.36), kind=kOutput, calls=%fused_computation.209 | convolution fusion | flops 6443235328 | bytes 7348224 | tf_op jit(solution)/shard_map/dot_general | solution.py:468
  155.4 11.7 %cholesky.18 = f32[128,128]{1,0:T(8,128)S(1)} custom-call(f32[128,128]{1,0:T(8,128)S(1)} %add_multiply_fusion.1), custom_call_target="Cholesky" | custom-call | tf_op jit(solution)/shard_map/jit(cholesky)/cholesky | solution.py:282
  168.5 9.8 %custom-call.6 = f32[1,128,128]{1,2,0:T(8,128)S(1)} custom-call(f32[1,128,128]{2,1,0:T(8,128)S(1)} %fusion.45), custom_call_target="InvertDiagBlocksLowerTriangular" | custom-call | tf_op jit(solution)/shard_map/triangular_solve | solution.py:283
  182.9 2.5 fusion.82
  185.9 3.5 convolution_divide_fusion
  189.4 6.2 %fusion.81 = (f32[2048]{0:T(1024)S(1)}, f32[2048]{0:T(1024)S(1)}, f32[8,49,2048]{2,1,0:T(8,128)}) fusion(f32[2048]{0:T(1024)S(1)} %fusion.67, f32[8,49,2048]{2,1,0:T(8,128)S(1)} %copy-done.2, f32[2048]{0:T(1024)S(1)} %get-tuple-element.169, f32[2048]{0:T(1024)S(1)} %bitcast.255, f32[2048]{0:T(1024)S(1)} %bitcast.253, ...), kind=kLoop, calls=%fused_computation.207 | loop fusion | flops 15249408 | bytes 8145200 | tf_op jit(solution)/shard_map/reduce_sum | solution.py:498
  196.2 13.4 %shard_map.206 = f32[32,128]{1,0:T(8,128)} custom-call(f32[32,128]{1,0:T(8,128)} %pad_maximum_fusion.1.x_ref), custom_call_target="tpu_custom_call" | custom-call | tf_op jit(solution)/shard_map/pallas_call | solution.py:253
  210.4 5.0 %multiply_convert_fusion = bf16[8,49,2048]{2,1,0:T(8,128)(2,1)S(1)} fusion(f32[8,49,2048]{2,1,0:T(8,128)} %get-tuple-element.170, f32[8,49,2048]{2,1,0:T(8,128)} %get-tuple-element.214, f32[]{:T(128)} %bitcast.8, f32[2048]{0:T(1024)S(1)} %get-tuple-element.181, f32[2048]{0:T(1024)S(1)} %get-tuple-element.180, f32[2048]{0:T(1024)S(1)} %get-tuple-element.168, ...), kind=kLoop, calls=%fused_computation.1 | loop fusion | flops 7225344 | bytes 8070692 | tf_op jit(solution)/shard_map/convert_element_type | solution.py:514
  215.5 2.4 fusion.85
  218.5 12.7 %shard_map.207 = f32[8,128]{1,0:T(8,128)} custom-call(f32[8,128]{1,0:T(8,128)} %pad_maximum_fusion.5.x_ref), custom_call_target="tpu_custom_call" | custom-call | tf_op jit(solution)/shard_map/pallas_call | solution.py:253
  232.0 2.4 multiply_convert_fusion.2
  234.7 4.4 fusion.97
  245.5 10.0 %shard_map.208 = f32[8,128]{1,0:T(8,128)} custom-call(f32[8,128]{1,0:T(8,128)} %pad_maximum_fusion.6.x_ref), custom_call_target="tpu_custom_call" | custom-call | tf_op jit(solution)/shard_map/pallas_call | solution.py:253
  257.4 3.4 add_multiply_fusion
  260.8 4.3 convolution_bitcast_fusion.1.refs_1_
  265.1 3.5 convolution_bitcast_fusion.refs_2_
  268.6 2.8 fusion.37
  271.3 3.5 copy.67
  274.9 7.3 %fusion.98.refs_0_ = f32[4608,512]{1,0:T(8,128)} fusion(bf16[392,4608]{1,0:T(8,128)(2,1)} %constant_dynamic-update-slice_fusion.1, bf16[392,512]{1,0:T(8,128)(2,1)S(1)} %reshape.722), kind=kOutput, calls=%fused_computation.223 | convolution fusion | flops 1849688064 | bytes 13451264 | tf_op jit(solution)/shard_map/rk,rm->km/dot_general | solution.py:551
  282.2 152.9 %shard_map.209 = (f32[4608,512]{1,0:T(8,128)}, f32[2048,512]{1,0:T(8,128)}, f32[512,2048]{1,0:T(8,128)}) custom-call(f32[4608,512]{1,0:T(8,128)} %fusion.98.refs_0_, f32[2048,512]{1,0:T(8,128)} %convolution_bitcast_fusion.1.refs_1_, f32[512,2048]{1,0:T(8,128)} %convolution_bitcast_fusion.refs_2_), custom_call_target="tpu_custom_call" | custom-call | tf_op jit(solution)/shard_map/pallas_call | solution.py:225
  437.6 10.2 %fusion.99 = f32[2048,1024]{1,0:T(8,128)} fusion(f32[256,2048]{1,0:T(8,128)S(1)} %copy-done.5, f32[256,1024]{1,0:T(8,128)} %copy-done.6), kind=kOutput, calls=%fused_computation.224 | convolution fusion | flops 6442450944 | bytes 11534336 | tf_op jit(solution)/shard_map/dot_general | solution.py:492
  447.7 2.0 copy.127
  449.8 4.8 %copy.128 = f32[3,3,512,512]{3,2,1,0:T(8,128)} copy(f32[3,3,512,512]{3,2,1,0:T(8,128)S(1)} %bitcast.238) | data formatting | bytes 18874368
  455.0 2.0 copy.129
  (237 shorter events, 85.5 us)
Async XLA Ops:
  7.2 49.5 %copy-start = (bf16[512,2048]{1,0:T(8,128)(2,1)S(1)}, bf16[512,2048]{1,0:T(8,128)(2,1)}, u32[]{:S(2)}) copy-start(bf16[512,2048]{1,0:T(8,128)(2,1)} %param.35) | copy-start | bytes 6291460
  7.2 139.2 %all-gather.2.cloned.1.call-start = ((), (), s32[]{:S(2)}) async-start(), calls=%async_computation | async-start | bytes 2162688 | tf_op jit(solution)/shard_map/all_gather | solution.py:467
  9.4 76.1 %copy-start.46 = (f32[8]{0:T(128)}, f32[8]{0:T(128)S(1)}, u32[]{:S(2)}) copy-start(f32[8]{0:T(128)S(1)} %get-tuple-element.163) | copy-start | bytes 100
  10.2 20.7 %copy-start.49 = (f32[2,512]{1,0:T(2,128)S(1)}, f32[2,512]{1,0:T(2,128)}, u32[]{:S(2)}) copy-start(f32[2,512]{1,0:T(2,128)} %param.38) | copy-start | bytes 12292
  36.0 20.7 %copy-start.38 = (f32[1,512]{1,0:T(1,128)}, f32[1,512]{1,0:T(1,128)S(1)}, u32[]{:S(2)}) copy-start(f32[1,512]{1,0:T(1,128)S(1)} %get-tuple-element.200) | copy-start | bytes 6148
  36.1 20.6 %copy-start.55 = (f32[1,512]{1,0:T(1,128)}, f32[1,512]{1,0:T(1,128)S(1)}, u32[]{:S(2)}) copy-start(f32[1,512]{1,0:T(1,128)S(1)} %get-tuple-element.201) | copy-start | bytes 6148
  54.7 6.7 %copy-start.40 = (f32[512]{0:T(512)}, f32[512]{0:T(512)S(1)}, u32[]{:S(2)}) copy-start(f32[512]{0:T(512)S(1)} %divide_bitcast_fusion.1) | copy-start | bytes 6148
  94.8 7.7 %copy-start.21 = (bf16[8,7,7,512]{3,2,1,0:T(8,128)(2,1)S(1)}, bf16[8,7,7,512]{3,2,1,0:T(8,128)(2,1)}, u32[]{:S(2)}) copy-start(bf16[8,7,7,512]{3,2,1,0:T(8,128)(2,1)} %copy.59) | copy-start | bytes 1204228
  100.6 16.5 %copy-start.57 = (s32[4]{0:T(128)S(1)}, s32[4]{0:T(128)}, u32[]{:S(2)}) copy-start(s32[4]{0:T(128)} %constant.361.clone.1) | copy-start | bytes 52
  103.4 7.7 %copy-start.22 = (bf16[8,7,7,512]{3,2,1,0:T(8,128)(2,1)S(1)}, bf16[8,7,7,512]{3,2,1,0:T(8,128)(2,1)}, u32[]{:S(2)}) copy-start(bf16[8,7,7,512]{3,2,1,0:T(8,128)(2,1)} %copy.64) | copy-start | bytes 1204228
  112.0 12.9 %copy-start.23 = (bf16[392,512]{1,0:T(8,128)(2,1)S(1)}, bf16[392,512]{1,0:T(8,128)(2,1)}, u32[]{:S(2)}) copy-start(bf16[392,512]{1,0:T(8,128)(2,1)} %concatenate.140) | copy-start | bytes 1204228
  115.9 9.8 %copy-start.27 = (bf16[392,512]{1,0:T(8,128)(2,1)S(1)}, bf16[392,512]{1,0:T(8,128)(2,1)}, u32[]{:S(2)}) copy-start(bf16[392,512]{1,0:T(8,128)(2,1)} %concatenate.141) | copy-start | bytes 1204228
  115.9 10.6 %copy-start.26 = (bf16[392,512]{1,0:T(8,128)(2,1)S(1)}, bf16[392,512]{1,0:T(8,128)(2,1)}, u32[]{:S(2)}) copy-start(bf16[392,512]{1,0:T(8,128)(2,1)} %concatenate.142) | copy-start | bytes 1204228
  115.9 11.4 %copy-start.25 = (bf16[392,512]{1,0:T(8,128)(2,1)S(1)}, bf16[392,512]{1,0:T(8,128)(2,1)}, u32[]{:S(2)}) copy-start(bf16[392,512]{1,0:T(8,128)(2,1)} %concatenate.143) | copy-start | bytes 1204228
  115.9 12.1 %copy-start.24 = (bf16[392,512]{1,0:T(8,128)(2,1)S(1)}, bf16[392,512]{1,0:T(8,128)(2,1)}, u32[]{:S(2)}) copy-start(bf16[392,512]{1,0:T(8,128)(2,1)} %concatenate.144) | copy-start | bytes 1204228
  128.8 24.2 %copy-start.37 = (f32[2,1024]{1,0:T(2,128)S(1)}, f32[2,1024]{1,0:T(2,128)}, u32[]{:S(2)}) copy-start(f32[2,1024]{1,0:T(2,128)} %param.41) | copy-start | bytes 24580
  146.4 7.6 %copy-start.59 = (bf16[1024,128]{1,0:T(8,128)(2,1)S(1)}, bf16[1024,128]{1,0:T(8,128)(2,1)}, u32[]{:S(2)}) copy-start(bf16[1024,128]{1,0:T(8,128)(2,1)} %param.37) | copy-start | bytes 786436
  153.0 25.9 %copy-start.48 = (s32[256]{0:T(256)S(1)}, s32[256]{0:T(256)}, u32[]{:S(2)}) copy-start(s32[256]{0:T(256)} %param.32) | copy-start | bytes 3076
  185.9 9.7 %copy-start.6 = (f32[256,1024]{1,0:T(8,128)}, f32[256,1024]{1,0:T(8,128)S(1)}, u32[]{:S(2)}) copy-start(f32[256,1024]{1,0:T(8,128)S(1)} %subtract_multiply_fusion.1) | copy-start | bytes 3145732
  210.3 5.1 %copy-start.31 = (f32[8,49,512]{2,1,0:T(8,128)S(1)}, f32[8,49,512]{2,1,0:T(8,128)}, u32[]{:S(2)}) copy-start(f32[8,49,512]{2,1,0:T(8,128)} %get-tuple-element.213) | copy-start | bytes 2408452
  210.4 5.1 %copy-start.39 = (f32[1,512]{1,0:T(1,128)S(1)}, f32[1,512]{1,0:T(1,128)}, u32[]{:S(2)}) copy-start(f32[1,512]{1,0:T(1,128)} %copy-done.38) | copy-start | bytes 6148
  210.4 5.1 %copy-start.41 = (f32[512]{0:T(512)S(1)}, f32[512]{0:T(512)}, u32[]{:S(2)}) copy-start(f32[512]{0:T(512)} %copy-done.40) | copy-start | bytes 6148
  210.4 5.1 %copy-start.44 = (f32[512]{0:T(512)S(1)}, f32[512]{0:T(512)}, u32[]{:S(2)}) copy-start(f32[512]{0:T(512)} %copy-done.43) | copy-start | bytes 6148
  210.4 5.1 %copy-start.56 = (f32[1,512]{1,0:T(1,128)S(1)}, f32[1,512]{1,0:T(1,128)}, u32[]{:S(2)}) copy-start(f32[1,512]{1,0:T(1,128)} %copy-done.55) | copy-start | bytes 6148
  215.5 16.5 %copy-start.45 = (f32[512]{0:T(512)S(1)}, f32[512]{0:T(512)}, u32[]{:S(2)}) copy-start(f32[512]{0:T(512)} %get-tuple-element.196) | copy-start | bytes 6148
  243.8 12.6 %copy-start.42 = (f32[512]{0:T(512)S(1)}, f32[512]{0:T(512)}, u32[]{:S(2)}) copy-start(f32[512]{0:T(512)} %get-tuple-element.165) | copy-start | bytes 6148
  282.2 155.4 %copy-start.5 = (f32[256,2048]{1,0:T(8,128)S(1)}, f32[256,2048]{1,0:T(8,128)}, u32[]{:S(2)}) copy-start(f32[256,2048]{1,0:T(8,128)} %all-gather.2.cloned.1.call-done) | copy-start | bytes 6291460
  437.6 10.2 %copy-start.9 = (f32[2048,512]{1,0:T(8,128)S(1)}, f32[2048,512]{1,0:T(8,128)}, u32[]{:S(2)}) copy-start(f32[2048,512]{1,0:T(8,128)} %get-tuple-element.243) | copy-start | bytes 12582916
  437.6 12.2 %slice-start = ((s8[9437184]{0:T(1024)(128)(4,1)}), s8[4194304]{0:T(1024)(128)(4,1)S(1)}, s32[]{:S(2)}) async-start(s8[9437184]{0:T(1024)(128)(4,1)} %bitcast.236), calls=%async_computation.1 | async-start | bytes 8388608
  437.6 12.2 %slice-start.1 = ((s8[9437184]{0:T(1024)(128)(4,1)}), s8[4194304]{0:T(1024)(128)(4,1)S(1)}, s32[]{:S(2)}) async-start(s8[9437184]{0:T(1024)(128)(4,1)} %bitcast.236), calls=%async_computation.2 | async-start | bytes 8388608
  449.8 5.2 %copy-start.8 = (f32[512,2048]{1,0:T(8,128)S(1)}, f32[512,2048]{1,0:T(8,128)}, u32[]{:S(2)}) copy-start(f32[512,2048]{1,0:T(8,128)} %get-tuple-element.245) | copy-start | bytes 12582916
  449.8 7.2 %copy-start.1 = (bf16[512,2048]{1,0:T(8,128)(2,1)S(1)}, bf16[512,2048]{1,0:T(8,128)(2,1)}, u32[]{:S(2)}) copy-start(bf16[512,2048]{1,0:T(8,128)(2,1)} %param.35) | copy-start | bytes 6291460
  (34 other events, 85.9 us)
Sparse Core Ops, SparseCore 0:
  86.4 59.9 all-gather.1

commit v2 on v0

v2 whole, which is shorter than its diff:
```python
import jax
import jax.numpy as jnp
from jax import lax
from jax.experimental import pallas as pl
from jax.experimental.pallas import tpu as pltpu
from jax.sharding import PartitionSpec as P

MESH = pl.DeviceIdType.MESH
SIDE = 7
SLOTS = 56
ROWS = 448
epsilon = 1e-05
whiten_floor = 0.001
f32 = jnp.float32
bf16 = jnp.bfloat16


def place():
    dp = lax.axis_index("dp")
    sub = lax.axis_index("sub")
    z = dp // 4
    y = lax.rem(dp // 2, 2)
    x = lax.rem(dp, 2)
    ring = 3 * y + x - 2 * x * y
    return dp, sub, z, ring


def plane_of(ring):
    ring = lax.rem(ring + 4, 4)
    y = ring // 2
    odd = lax.rem(ring, 2)
    return y * 2 + odd + y - 2 * odd * y


def ring_dp(z, ring):
    return z * 4 + plane_of(ring)


def dev(dp, sub):
    return {"dp": dp, "sub": sub}


def greet_start():
    dp, sub, _, _ = place()
    me = dp * 2 + sub
    barrier = pltpu.get_barrier_semaphore()

    @pl.loop(1, 32)
    def _(step):
        other = lax.rem(me + step, 32)
        pl.semaphore_signal(
            barrier, inc=1, device_id=dev(other // 2, lax.rem(other, 2)), device_id_type=MESH
        )


def greet_wait():
    pl.semaphore_wait(pltpu.get_barrier_semaphore(), 31)


def remote(src, dst, send, recv, where):
    return pltpu.make_async_remote_copy(
        src_ref=src,
        dst_ref=dst,
        send_sem=send,
        recv_sem=recv,
        device_id=dev(*where),
        device_id_type=MESH,
    )


def arrived(ref, sem):
    pltpu.make_async_copy(ref, ref, sem).wait()


def direct_start(buf, send, recv):
    dp, sub, _, _ = place()
    me = dp * 2 + sub

    @pl.loop(1, 32)
    def _(step):
        other = lax.rem(me + step, 32)
        remote(buf.at[me], buf.at[me], send, recv, (other // 2, lax.rem(other, 2))).start()


def direct_finish(buf, send, recv):
    many = buf.at[pl.ds(0, 31)]
    arrived(many, recv)
    total = jnp.sum(buf[...], axis=0)
    arrived(many, send)
    return total


def tree_sums(value, pair, plane, line, send, recv, base=3):
    dp, sub, z, _ = place()
    w = lax.rem(dp, 4)
    if value is not None:
        pair[sub] = value
    remote(pair.at[sub], pair.at[sub], send.at[base + 0], recv.at[base + 0], (dp, 1 - sub)).start()
    arrived(pair.at[0], recv.at[base + 0])
    plane[w] = pair[0] + pair[1]
    for k in range(1, 4):
        remote(
            plane.at[w], plane.at[w], send.at[base + 1], recv.at[base + 1], (z * 4 + lax.rem(w + k, 4), sub)
        ).start()
    arrived(plane.at[pl.ds(0, 3)], recv.at[base + 1])
    line[z] = (plane[0] + plane[1]) + (plane[2] + plane[3])
    for k in range(1, 4):
        remote(
            line.at[z], line.at[z], send.at[base + 2], recv.at[base + 2], (lax.rem(z + k, 4) * 4 + w, sub)
        ).start()
    arrived(line.at[pl.ds(0, 3)], recv.at[base + 2])
    total = (line[0] + line[1]) + (line[2] + line[3])
    arrived(pair.at[0], send.at[base + 0])
    arrived(plane.at[pl.ds(0, 3)], send.at[base + 1])
    arrived(line.at[pl.ds(0, 3)], send.at[base + 2])
    return total


class Mover:
    def __init__(self, send, recv):
        self.send, self.recv, self.pending = send, recv, []

    def go(self, cond, src, dst, s, r, where):
        def body():
            remote(src, dst, self.send.at[s], self.recv.at[r], where).start()

        if cond is None:
            body()
        else:
            pl.when(cond)(body)
        self.pending.append((cond, src, s))

    def got(self, cond, ref, r, then=None):
        def body():
            arrived(ref, self.recv.at[r])
            if then is not None:
                then()

        if cond is None:
            body()
        else:
            pl.when(cond)(body)

    def drain(self):
        for cond, ref, s in self.pending:

            def body(ref=ref, s=s):
                arrived(ref, self.send.at[s])

            if cond is None:
                body()
            else:
                pl.when(cond)(body)
        self.pending = []

    def line_gather(self, at, first, base):
        dp, sub, z, _ = place()
        up, down = (dp + 4, sub), (dp - 4, sub)
        hold = lambda j: at(jnp.clip(j, 0, 3))
        for t in range(3):
            from_up = first if t == 0 and first is not None else hold(z - t)
            from_down = first if t == 0 and first is not None else hold(z + t)
            self.go(jnp.logical_and(z <= 2, z >= t), from_up, hold(z - t), base + t, base + t, up)
            self.go(
                jnp.logical_and(z >= 1, z <= 3 - t),
                from_down,
                hold(z + t),
                base + 3 + t,
                base + 3 + t,
                down,
            )
            yield
            self.got(z >= t + 1, hold(z - 1 - t), base + t)
            self.got(z <= 2 - t, hold(z + 1 + t), base + 3 + t)

    def ring_gather(self, blk, first, base, after):
        dp, sub, z, q = place()
        after_me, before_me = (ring_dp(z, q + 1), sub), (ring_dp(z, q + 3), sub)
        src = first if first is not None else blk(0, None)
        self.go(None, src, blk(0, None), base, base, after_me)
        self.go(None, src, blk(0, None), base + 1, base + 1, before_me)
        yield
        self.got(None, blk(3, None), base)
        self.go(None, blk(3, 0), blk(3, 0), base + 2, base + 2, after_me)
        after(blk(3, None), 0)
        self.got(None, blk(1, None), base + 1)
        self.go(None, blk(1, 1), blk(1, 1), base + 3, base + 3, before_me)
        after(blk(1, None), 1)
        yield
        self.got(None, blk(2, 0), base + 2)
        self.got(None, blk(2, 1), base + 3)
        after(blk(2, None), 2)


def run_all(gens, starts=None):
    live = dict(enumerate(gens))
    tick = 0
    while live:
        for j in sorted(live):
            if starts is None or tick >= starts[j]:
                try:
                    next(live[j])
                except StopIteration:
                    live.pop(j)
        tick += 1


def gather_pooled(own, out, send, recv, split):
    dp, sub, z, q = place()
    width = out.shape[-1]
    sib = (dp, 1 - sub)

    def first_line():
        cols = pl.ds(0, split)
        mover = Mover(send.at[0], recv.at[0])
        at = lambda j: out.at[j, plane_of(q), sub, :, cols]

        def blk(k, h):
            ring = plane_of(q + k)
            if h is None:
                return out.at[:, ring, sub, :, cols]
            return out.at[pl.ds(2 * h, 2), ring, sub, :, cols]

        def share(ref, s):
            mover.go(None, ref, ref, 10 + s, 10, sib)

        yield from mover.line_gather(at, own.at[:, cols], 0)
        share(blk(0, None), 3)
        yield from mover.ring_gather(blk, None, 6, share)
        yield
        arrived(out.at[:, :, 1 - sub, :, cols], recv.at[0, 10])
        mover.drain()

    def first_ring():
        cols = pl.ds(split, width - split)
        mid = (width - split) // 2
        mover = Mover(send.at[1], recv.at[1])

        def blk(k, h):
            ring = plane_of(q + k)
            if h is None:
                return out.at[z, ring, sub, :, cols]
            return out.at[z, ring, sub, :, pl.ds(split + h * mid, mid)]

        at = lambda j: out.at[j, :, sub, :, cols]

        def share(ref, s):
            mover.go(None, ref, ref, 10 + s, 10, sib)

        yield from mover.ring_gather(blk, own.at[:, cols], 0, lambda ref, s: None)
        share(at(z), 3)
        yield from mover.line_gather(at, None, 4)
        for k in range(1, 4):
            share(at(lax.rem(z + k, 4)), k - 1)
        yield
        arrived(out.at[:, :, 1 - sub, :, cols], recv.at[1, 10])
        mover.drain()

    return [first_line(), first_ring()]


def mm(a, b):
    return jnp.dot(a, b, preferred_element_type=f32)


def mm_nt(a, b):
    return lax.dot_general(a, b, (((1,), (1,)), ((), ())), preferred_element_type=f32)


def mm_tn(a, b):
    return lax.dot_general(a, b, (((0,), (0,)), ((), ())), preferred_element_type=f32)


def sigmoid(v):
    return 0.5 + 0.5 * jnp.tanh(0.5 * v)


def split(v):
    high = v.astype(bf16)
    return high, (v - high.astype(f32)).astype(bf16)


def exact(a, b, dims):
    return lax.dot_general(
        a, b, (dims, ((), ())), precision=lax.Precision.HIGHEST, preferred_element_type=f32
    )


def factor_inverse(cov, block=8):
    size = cov.shape[0]
    tiles = size // 8
    row = lax.broadcasted_iota(jnp.int32, (8, size), 0)
    column = lax.broadcasted_iota(jnp.int32, (8, size), 1)
    left = [cov[8 * t : 8 * t + 8, :] for t in range(tiles)]
    right = [jnp.where(row + 8 * t == column, 1.0, 0.0) for t in range(tiles)]
    wide = lambda v: jnp.broadcast_to(v, (8, size))
    for j in range(0, size, block):
        t0, s = j // 8, j % 8
        columns = [[wide(left[t][:, j + k : j + k + 1]) for k in range(block)] for t in range(t0, tiles)]
        lefts = [wide(left[t0][s + k : s + k + 1, :]) for k in range(block)]
        rights = [wide(right[t0][s + k : s + k + 1, :]) for k in range(block)]
        entry = [[wide(columns[0][k][s + m : s + m + 1, :]) for k in range(m + 1)] for m in range(block)]
        lower = [[None] * block for _ in range(block)]
        inverses = []
        for k in range(block):
            inverse = 1.0 / entry[k][k]
            inverses.append(inverse)
            for m in range(k + 1, block):
                lower[m][k] = entry[m][k] * inverse
            for m in range(k + 1, block):
                for n in range(k + 1, m + 1):
                    entry[m][n] = entry[m][n] - lower[m][k] * entry[n][k]
        for m in range(block):
            for k in range(m):
                lefts[m] = lefts[m] - lower[m][k] * lefts[k]
                rights[m] = rights[m] - lower[m][k] * rights[k]
        scaled_left = [a * b for a, b in zip(lefts, inverses)]
        scaled_right = [a * b for a, b in zip(rights, inverses)]
        for t in range(t0, tiles):
            if t == t0 and s + block == 8 and block == 1:
                continue
            own = columns[t - t0]
            for m in range(block):
                for k in range(m):
                    own[m] = own[m] - lower[m][k] * own[k]
            for m in range(block):
                factor = own[m]
                if t == t0:
                    factor = jnp.where(row > s + m, factor, 0.0)
                left[t] = left[t] - factor * scaled_left[m]
                right[t] = right[t] - factor * scaled_right[m]
    out = []
    for t in range(tiles):
        pivots = jnp.sum(jnp.where(row + 8 * t == column, left[t], 0.0), axis=1, keepdims=True)
        out.append(right[t] * lax.rsqrt(pivots))
    return jnp.concatenate(out, axis=0)


def fold8(v):
    rows, cols = v.shape
    return jnp.sum(v.reshape(rows // 8, 8, cols), axis=0)


def columns_of(mask, cols):
    return jnp.concatenate([mask] * (cols // 128), axis=1)


def fwd_kernel(
    images, pixel_mask, pair_column, pair_row, w_reduce, w_spatial, w_expand, w_project, w_code,
    norm_reduce, norm_spatial, norm_expand, norm_project,
    pooled_out, hidden_out, dprojected_out, dcodes_out, loss_out, grad_norm_out, upstream,
    masked_out, reduced_out, act1_out, spatial_out, act2_out, normed_out, slope_out, mask, stats, sums_out,
    img, masked, wr, ws, we, wp, wc, reduced, wide, shifted, spatial, act2, normed, slope, own,
    pooled_all, pool_high, pool_low, level, normal, hidden, dproj, counts,
    counts_buf, buf1, buf2, pair, plane, line,
    load, save, send, recv, gsend, grecv,
):
    dp, sub, z, q = place()
    me = dp * 2 + sub
    inner = wr.shape[1]
    width = wr.shape[0]
    loads = [pltpu.make_async_copy(a, b, load.at[k]) for k, (a, b) in enumerate(
        [(images, img), (w_reduce, wr), (w_spatial, ws), (w_expand, we), (w_project, wp), (w_code, wc)])]
    for copy in loads:
        copy.start()
    greet_start()
    here = pixel_mask[...].astype(f32)
    counts[...] = jnp.broadcast_to(jnp.sum(here, axis=1, keepdims=True), (8, 128))
    for slot in range(SLOTS):
        r, c = slot // 8, slot % 8
        if c == SIDE:
            value = jnp.zeros((8, 128), f32)
        else:
            value = jnp.broadcast_to(here[:, SIDE * r + c : SIDE * r + c + 1], (8, 128))
        mask[pl.ds(8 * slot, 8), :] = value
    wide[pl.ds(0, 8), :] = jnp.zeros((8, inner), f32)
    wide[pl.ds(ROWS + 8, 8), :] = jnp.zeros((8, inner), f32)
    for b in range(3):
        shifted[b, pl.ds(0, 64), :] = jnp.zeros((64, inner), bf16)
        shifted[b, pl.ds(512, 64), :] = jnp.zeros((64, inner), bf16)
    greet_wait()
    counts_buf[me] = counts[...]
    direct_start(counts_buf, send.at[0], recv.at[0])
    loads[0].wait()
    gap = jnp.zeros((8, 256), f32)

    @pl.loop(0, width // 256)
    def _(n):
        cols = pl.ds(pl.multiple_of(n * 256, 256), 256)
        for r in range(SIDE):
            rows = img[pl.ds(SIDE * r, SIDE), :, cols].astype(f32).reshape(SIDE * 8, 256)
            rows = rows * columns_of(mask[pl.ds(64 * r, 56), :], 256)
            masked[pl.ds(64 * r, 64), cols] = jnp.concatenate([rows, gap], axis=0).astype(bf16)

    saves = []

    def keep(a, b):
        copy = pltpu.make_async_copy(a, b, save.at[len(saves)])
        copy.start()
        saves.append(copy)

    keep(masked, masked_out)
    loads[1].wait()

    @pl.loop(0, inner // 256)
    def _(n):
        cols = pl.ds(pl.multiple_of(n * 256, 256), 256)
        got = mm(masked[...], wr[:, cols])
        reduced[:, cols] = got
        buf1[me, pl.ds(0, 1), cols] = jnp.sum(got, axis=0, keepdims=True)
        buf1[me, pl.ds(1, 1), cols] = jnp.sum(got * got, axis=0, keepdims=True)

    direct_start(buf1, send.at[1], recv.at[1])
    keep(reduced, reduced_out)
    valid = jnp.sum(direct_finish(counts_buf, send.at[0], recv.at[0]), axis=0, keepdims=True)[:, 0:1]
    inverse_valid = 1.0 / valid

    def moments(total):
        centre = total[0:1] * inverse_valid
        return centre, lax.rsqrt(total[1:2] * inverse_valid - centre * centre + epsilon)

    def activate(src, norm, centre, scale, store):
        gain = norm[0:1, :] * scale
        bias = norm[1:2, :] - centre * gain

        @pl.loop(0, ROWS // 32)
        def _(k):
            rows = pl.ds(pl.multiple_of(k * 32, 32), 32)
            level = src[rows, :] * gain + bias
            store(k, columns_of(mask[rows, :], inner) * (level * sigmoid(level)))

    centre1, scale1 = moments(direct_finish(buf1, send.at[1], recv.at[1]))
    stats[pl.ds(0, 1), pl.ds(0, inner)] = centre1
    stats[pl.ds(1, 1), pl.ds(0, inner)] = scale1

    def store_wide(k, value):
        wide[pl.ds(pl.multiple_of(k * 32 + 8, 8), 32), :] = value
        shifted[1, pl.ds(pl.multiple_of(k * 32 + 64, 32), 32), :] = value.astype(bf16)

    activate(reduced, norm_reduce, centre1, scale1, store_wide)

    @pl.loop(0, ROWS // 32)
    def _(k):
        for b in (0, 2):
            rows = wide[pl.ds(pl.multiple_of(k * 32 + 8 * b, 8), 32), :]
            shifted[b, pl.ds(pl.multiple_of(k * 32 + 64, 32), 32), :] = rows.astype(bf16)

    keep(shifted.at[1, pl.ds(64, ROWS)], act1_out)
    loads[2].wait()

    @pl.loop(0, inner // 256)
    def _(n):
        cols = pl.ds(pl.multiple_of(n * 256, 256), 256)

        def taps(a, total):
            for b in range(3):
                left = shifted[b, pl.ds(pl.multiple_of(a * 64, 64), ROWS), :]
                right = ws[pl.ds(pl.multiple_of((a * 3 + b) * inner, inner), inner), cols]
                total = total + mm(left, right)
            return total

        spatial[:, cols] = taps(0, jnp.zeros((ROWS, 256), f32))
        spatial[:, cols] = taps(1, spatial[:, cols])
        got = taps(2, spatial[:, cols]) * columns_of(mask[...], 256)
        spatial[:, cols] = got
        buf2[me, pl.ds(0, 1), cols] = jnp.sum(got, axis=0, keepdims=True)
        buf2[me, pl.ds(1, 1), cols] = jnp.sum(got * got, axis=0, keepdims=True)

    direct_start(buf2, send.at[2], recv.at[2])
    keep(spatial, spatial_out)
    centre2, scale2 = moments(direct_finish(buf2, send.at[2], recv.at[2]))
    stats[pl.ds(2, 1), pl.ds(0, inner)] = centre2
    stats[pl.ds(3, 1), pl.ds(0, inner)] = scale2

    def store_act2(k, value):
        act2[pl.ds(pl.multiple_of(k * 32, 32), 32), :] = value.astype(bf16)

    activate(spatial, norm_spatial, centre2, scale2, store_act2)
    keep(act2, act2_out)
    loads[3].wait()

    @pl.loop(0, width // 256)
    def _(n):
        cols = pl.ds(pl.multiple_of(n * 256, 256), 256)
        got = mm(act2[...], we[:, cols])
        normed[:, cols] = got
        pair[sub, pl.ds(0, 1), cols] = jnp.sum(got, axis=0, keepdims=True)
        pair[sub, pl.ds(1, 1), cols] = jnp.sum(got * got, axis=0, keepdims=True)

    centre3, scale3 = moments(tree_sums(None, pair, plane, line, send, recv))
    stats[pl.ds(4, 1), :] = centre3
    stats[pl.ds(5, 1), :] = scale3
    stats[pl.ds(6, 1), :] = jnp.broadcast_to(valid, (1, width))
    stats[pl.ds(7, 1), :] = jnp.zeros((1, width), f32)
    inverse_counts = 1.0 / counts[...]

    @pl.loop(0, width // 256)
    def _(n):
        cols = pl.ds(pl.multiple_of(n * 256, 256), 256)
        centre, scale = stats[pl.ds(4, 1), cols], stats[pl.ds(5, 1), cols]
        gain, bias = norm_expand[pl.ds(0, 1), cols], norm_expand[pl.ds(1, 1), cols]

        def block(k, carry):
            pool, s1, s2 = carry
            rows = pl.ds(pl.multiple_of(k * 64, 64), 64)
            here = columns_of(mask[rows, :], 256)
            n3 = (normed[rows, cols] - centre) * scale
            total = masked[rows, cols].astype(f32) + gain * n3 + bias
            sig = sigmoid(total)
            out = total * sig
            slope3 = here * (sig + out * (1.0 - sig))
            normed[rows, cols] = n3
            slope[rows, cols] = slope3
            return pool + fold8(here * out), s1 + fold8(slope3), s2 + fold8(slope3 * n3)

        zero = jnp.zeros((8, 256), f32)
        pool, s1, s2 = lax.fori_loop(0, ROWS // 64, block, (zero, zero, zero))
        own[:, cols] = pool * columns_of(inverse_counts, 256)
        sums_out[pl.ds(0, 8), cols] = s1
        sums_out[pl.ds(8, 8), cols] = s2

    keep(normed, normed_out)
    keep(slope, slope_out)
    movers = gather_pooled(own, pooled_all, gsend, grecv, 1536)
    for mover in movers:
        next(mover)
    pooled_all[z, lax.rem(dp, 4), sub] = own[...]
    run_all(movers)
    rows_all = 256
    keep(pooled_all, pooled_out)
    loads[4].wait()
    loads[5].wait()

    @pl.loop(0, rows_all // 8)
    def _(k):
        value = pooled_all[k // 8, lax.rem(k // 2, 4), lax.rem(k, 2)]
        level[pl.ds(pl.multiple_of(k * 8, 8), 8), :] = value

    @pl.loop(0, rows_all // 32)
    def _(k):
        rows = pl.ds(pl.multiple_of(k * 32, 32), 32)
        high, low = split(level[rows, :])
        pool_high[rows, :] = high
        pool_low[rows, :] = low

    proj = hidden.shape[1]
    share = 1.0 / rows_all

    @pl.loop(0, proj // 256)
    def _(n):
        cols = pl.ds(pl.multiple_of(n * 256, 256), 256)
        right = wp[:, cols]
        value = mm(pool_high[...], right) + mm(pool_low[...], right)
        centre = jnp.sum(value, axis=0, keepdims=True) * share
        square = jnp.sum(value * value, axis=0, keepdims=True) * share
        scale = lax.rsqrt(square - centre * centre + epsilon)
        normal_here = (value - centre) * scale
        level_here = norm_project[pl.ds(0, 1), cols] * normal_here + norm_project[pl.ds(1, 1), cols]
        normal[:, cols] = normal_here
        level[:, cols] = level_here
        hidden[:, cols] = level_here * sigmoid(level_here)
        upstream[pl.ds(0, 1), cols] = scale * norm_project[pl.ds(0, 1), cols]

    keep(hidden, hidden_out)
    high, low = split(hidden[...])
    codes = mm(high, wc[...]) + mm(low, wc[...])

    centre = jnp.sum(codes, axis=0, keepdims=True) * share
    moved = codes - centre
    cov = exact(moved, moved, ((0,), (0,))) * share
    size = cov.shape[0]
    row = lax.broadcasted_iota(jnp.int32, (size, size), 0)
    column = lax.broadcasted_iota(jnp.int32, (size, size), 1)
    inverse = factor_inverse(cov + jnp.where(row == column, whiten_floor, 0.0))
    white = exact(moved, inverse, ((1,), (1,)))
    unit_scale = lax.rsqrt(jnp.sum(white * white, axis=1, keepdims=True) + epsilon)
    unit = white * unit_scale
    same = (pair_column[...] == pair_row[...]).astype(f32)
    gap = 2.0 * unit - exact(same, unit, ((1,), (0,)))
    loss_out[...] = jnp.broadcast_to(jnp.sum(jnp.sum(gap * gap, axis=1, keepdims=True), axis=0, keepdims=True) * share, (8, 128))
    grad_white = unit_scale * (gap - unit * jnp.sum(unit * gap, axis=1, keepdims=True))
    gram = exact(grad_white, white, ((0,), (0,)))
    half = jnp.where(row > column, gram, jnp.where(row == column, 0.5 * gram, 0.0))
    both = half + jnp.transpose(half)
    grad_moved = exact(grad_white - exact(white, both, ((1,), (0,))) * share, inverse, ((1,), (0,)))
    dcodes = grad_moved - jnp.sum(grad_moved, axis=0, keepdims=True) * share
    dcodes_out[...] = dcodes

    high, low = split(dcodes)

    @pl.loop(0, proj // 256)
    def _(n):
        cols = pl.ds(pl.multiple_of(n * 256, 256), 256)
        right = wc[cols, :]
        grad = mm_nt(high, right) + mm_nt(low, right)
        level_here = level[:, cols]
        sig = sigmoid(level_here)
        grad = grad * (sig * (1.0 + level_here * (1.0 - sig)))
        normal_here = normal[:, cols]
        total = jnp.sum(grad, axis=0, keepdims=True)
        dot = jnp.sum(grad * normal_here, axis=0, keepdims=True)
        grad_norm_out[pl.ds(0, 1), cols] = dot
        grad_norm_out[pl.ds(1, 1), cols] = total
        dproj[:, cols] = upstream[pl.ds(0, 1), cols] * (grad - (total + normal_here * dot) * share)

    keep(dproj, dprojected_out)
    mine = dproj[pl.ds(pl.multiple_of(me * 8, 8), 8), :]
    high = mine.astype(bf16).astype(f32)
    both_terms = jnp.concatenate([high, mine - high], axis=0).astype(bf16)

    @pl.loop(0, width // 256)
    def _(n):
        cols = pl.ds(pl.multiple_of(n * 256, 256), 256)
        value = mm_nt(both_terms, wp[cols, :])
        upstream[:, cols] = (value[0:8] + value[8:16]) * columns_of(inverse_counts, 256)

    for copy in saves:
        copy.wait()


def forward(
    images, pixel_mask, pair_column, pair_row, w_reduce, w_spatial, w_expand, w_project, w_code,
    norm_reduce, norm_spatial, norm_expand, norm_project,
):
    width, inner = w_reduce.shape
    proj, code = w_code.shape
    hbm = pl.BlockSpec(memory_space=pl.ANY)
    vmem = pl.BlockSpec(memory_space=pltpu.VMEM)
    shape = jax.ShapeDtypeStruct
    return pl.pallas_call(
        fwd_kernel,
        out_shape=[
            shape((4, 4, 2, 8, width), f32),
            shape((256, proj), f32),
            shape((256, proj), f32),
            shape((256, code), f32),
            shape((8, 128), f32),
            shape((2, proj), f32),
            shape((8, width), f32),
            shape((ROWS, width), bf16),
            shape((ROWS, inner), f32),
            shape((ROWS, inner), bf16),
            shape((ROWS, inner), f32),
            shape((ROWS, inner), bf16),
            shape((ROWS, width), f32),
            shape((ROWS, width), f32),
            shape((ROWS, 128), f32),
            shape((8, width), f32),
            shape((16, width), f32),
        ],
        in_specs=[hbm, vmem, vmem, vmem, hbm, hbm, hbm, hbm, hbm, vmem, vmem, vmem, vmem],
        out_specs=[hbm, hbm, hbm, vmem, vmem, vmem, vmem] + [hbm] * 7 + [vmem] * 3,
        scratch_shapes=[
            pltpu.VMEM((49, 8, width), bf16),
            pltpu.VMEM((ROWS, width), bf16),
            pltpu.VMEM((width, inner), bf16),
            pltpu.VMEM((9 * inner, inner), bf16),
            pltpu.VMEM((inner, width), bf16),
            pltpu.VMEM((width, proj), bf16),
            pltpu.VMEM((proj, code), bf16),
            pltpu.VMEM((ROWS, inner), f32),
            pltpu.VMEM((ROWS + 16, inner), f32),
            pltpu.VMEM((3, ROWS + 128, inner), bf16),
            pltpu.VMEM((ROWS, inner), f32),
            pltpu.VMEM((ROWS, inner), bf16),
            pltpu.VMEM((ROWS, width), f32),
            pltpu.VMEM((ROWS, width), f32),
            pltpu.VMEM((8, width), f32),
            pltpu.VMEM((4, 4, 2, 8, width), f32),
            pltpu.VMEM((256, width), bf16),
            pltpu.VMEM((256, width), bf16),
            pltpu.VMEM((256, width), f32),
            pltpu.VMEM((256, proj), f32),
            pltpu.VMEM((256, proj), f32),
            pltpu.VMEM((256, proj), f32),
            pltpu.VMEM((8, 128), f32),
            pltpu.VMEM((32, 8, 128), f32),
            pltpu.VMEM((32, 2, inner), f32),
            pltpu.VMEM((32, 2, inner), f32),
            pltpu.VMEM((2, 2, width), f32),
            pltpu.VMEM((4, 2, width), f32),
            pltpu.VMEM((4, 2, width), f32),
            pltpu.SemaphoreType.DMA((6,)),
            pltpu.SemaphoreType.DMA((10,)),
            pltpu.SemaphoreType.DMA((6,)),
            pltpu.SemaphoreType.DMA((6,)),
            pltpu.SemaphoreType.DMA((2, 14)),
            pltpu.SemaphoreType.DMA((2, 14)),
        ],
        compiler_params=pltpu.CompilerParams(
            collective_id=20, has_side_effects=True, vmem_limit_bytes=58 << 20
        ),
    )(
        images, pixel_mask, pair_column, pair_row, w_reduce, w_spatial, w_expand, w_project, w_code,
        norm_reduce, norm_spatial, norm_expand, norm_project,
    )


class Job:
    def __init__(self, ring_first, rows, acc, other, out, sib_out, land, scratch, send, recv, loc):
        self.ring_first, self.rows, self.acc, self.other = ring_first, rows, acc, other
        self.out, self.sib_out, self.land, self.scratch = out, sib_out, land, scratch
        self.mover = Mover(send, recv)
        self.loc = loc
        self.taken = 0

    def take(self, rows):
        ref = rows_at(self.scratch, self.taken, rows)
        self.taken += rows
        return ref

    def start(self):
        dp, sub, _, _ = place()
        self.mover.go(None, self.other, self.land, 0, 0, (dp, 1 - sub))

    def ring_reduce(self, base, block):
        dp, sub, z, q = place()
        go, got = self.mover.go, self.mover.got
        after_me, before_me = (ring_dp(z, q + 1), sub), (ring_dp(z, q + 3), sub)
        half = block // 2
        r0a, r0b, r1a, r1b = self.take(half), self.take(half), self.take(block), self.take(block)

        def blk(k, h=0, n=block):
            return rows_at(self.acc, base + lax.rem(q + k, 4) * block + h, n)

        go(None, blk(2, 0, half), r0a, 1, 1, after_me)
        go(None, blk(2, half, half), r0b, 2, 2, before_me)
        yield
        got(None, r0a, 1)
        add_into(blk(1, 0, half), r0a, half)
        go(None, blk(1), r1a, 3, 3, after_me)
        got(None, r0b, 2)
        add_into(blk(3, half, half), r0b, half)
        go(None, blk(3), r1b, 4, 4, before_me)
        yield
        got(None, r1a, 3)
        add_into(blk(0), r1a, block)
        got(None, r1b, 4)
        add_into(blk(0), r1b, block)

    def line_reduce(self, base, chunk):
        dp, sub, z, _ = place()
        go, got = self.mover.go, self.mover.got
        up, down = (dp + 4, sub), (dp - 4, sub)
        low = [self.take(chunk) for _ in range(3)]
        high = [self.take(chunk) for _ in range(3)]

        def at(j):
            return rows_at(self.acc, base + jnp.clip(j, 0, 3) * chunk, chunk)

        for t in range(3):
            go(z <= t, at(3 + z - t), low[t], 5 + t, 5 + t, up)
            go(z >= 3 - t, at(z - 3 + t), high[t], 8 + t, 8 + t, down)
            yield
            got(
                jnp.logical_and(z >= 1, z <= t + 1),
                low[t],
                5 + t,
                lambda: add_into(at(2 + z - t), low[t], chunk),
            )
            got(
                jnp.logical_and(z <= 2, z >= 2 - t),
                high[t],
                8 + t,
                lambda: add_into(at(z - 2 + t), high[t], chunk),
            )

    def run(self):
        dp, sub, z, q = place()
        sib = (dp, 1 - sub)
        mover, out, rows = self.mover, self.out, self.rows
        self.start()
        yield
        mover.got(None, self.land, 0)
        add_into(self.acc, self.land, rows)
        big, small = rows // 4, rows // 16
        half_small = small // 2
        half_big = big // 2

        def share(ref, k):
            mover.go(None, ref, ref, 21 + k, 21, sib)

        if self.ring_first:
            yield from self.ring_reduce(0, big)
            yield from self.line_reduce(q * big, small)
            mine = rows_at(self.acc, q * big + z * small, small)
            own = rows_at(out, q * big + z * small, small)
            local = pltpu.make_async_copy(mine, own, self.loc)
            local.start()
            at = lambda j: rows_at(out, q * big + j * small, small)
            yield from mover.line_gather(at, mine, 11)
            local.wait()
            share(rows_at(out, q * big, big), 3)

            def blk(k, h):
                start = lax.rem(q + k, 4) * big
                if h is None:
                    return rows_at(out, start, big)
                return rows_at(out, start + h * half_big, half_big)

            yield from mover.ring_gather(blk, None, 17, share)
        else:
            yield from self.line_reduce(0, big)
            yield from self.ring_reduce(z * big, small)
            mine = rows_at(self.acc, z * big + q * small, small)
            own = rows_at(out, z * big + q * small, small)
            local = pltpu.make_async_copy(mine, own, self.loc)
            local.start()

            def blk(k, h):
                start = z * big + lax.rem(q + k, 4) * small
                if h is None:
                    return rows_at(out, start, small)
                return rows_at(out, start + h * half_small, half_small)

            yield from mover.ring_gather(blk, mine, 17, lambda ref, k: None)
            local.wait()
            share(rows_at(out, z * big, big), 3)
            at = lambda j: rows_at(out, j * big, big)
            yield from mover.line_gather(at, None, 11)
            for k in range(1, 4):
                share(rows_at(out, lax.rem(z + k, 4) * big, big), k - 1)
        yield
        arrived(self.sib_out, mover.recv.at[21])
        mover.drain()


JOB_SEMS = 25


def add_into(dst, src, rows):
    step = 16 if rows % 16 == 0 else 8

    @pl.loop(0, rows // step)
    def _(k):
        at = pl.ds(pl.multiple_of(k * step, 8), step)
        dst[at, :] = dst[at, :] + src[at, :]


def rows_at(ref, start, size):
    return ref.at[pl.ds(pl.multiple_of(start, 8), size)]


def landing_rows(ring_first, rows):
    big, small = rows // 4, rows // 16
    return 3 * big + 6 * small if ring_first else 3 * small + 6 * big


JOBS = (
    (2, 0, 256, 0, 1536, True),
    (2, 0, 256, 1536, 512, False),
    (0, 0, 896, 0, 512, True),
    (0, 896, 256, 0, 512, False),
    (0, 1152, 896, 0, 512, True),
    (0, 2048, 256, 0, 512, False),
    (1, 0, 768, 0, 512, True),
    (1, 768, 256, 0, 512, False),
)


def tree_gen(pair, plane, line, send, recv, result):
    dp, sub, z, _ = place()
    w = lax.rem(dp, 4)
    remote(pair.at[sub], pair.at[sub], send.at[0], recv.at[0], (dp, 1 - sub)).start()
    yield
    arrived(pair.at[0], recv.at[0])
    plane[w] = pair[0] + pair[1]
    for k in range(1, 4):
        where = (z * 4 + lax.rem(w + k, 4), sub)
        remote(plane.at[w], plane.at[w], send.at[1], recv.at[1], where).start()
    yield
    arrived(plane.at[pl.ds(0, 3)], recv.at[1])
    line[z] = (plane[0] + plane[1]) + (plane[2] + plane[3])
    for k in range(1, 4):
        where = (lax.rem(z + k, 4) * 4 + w, sub)
        remote(line.at[z], line.at[z], send.at[2], recv.at[2], where).start()
    yield
    arrived(line.at[pl.ds(0, 3)], recv.at[2])
    result[...] = (line[0] + line[1]) + (line[2] + line[3])
    arrived(pair.at[0], send.at[0])
    arrived(plane.at[pl.ds(0, 3)], send.at[1])
    arrived(line.at[pl.ds(0, 3)], send.at[2])


def back_kernel(
    upstream, masked_in, reduced_in, act1_in, spatial_in, act2_in, normed_in, slope_in, mask, stats, sums_in,
    w_reduce, w_spatial, w_expand, norm_reduce, norm_spatial, norm_expand,
    grad_images, grad_spatial, grad_reduce, grad_expand, grad_norm_reduce, grad_norm_spatial, grad_norm_expand,
    wr, ws, we, masked, reduced, act1, spatial, act2, big, dsum, dexp, level, wide, shifted, dred,
    gs, gr, land_s, land_r, land_e, *rest,
):
    scratches = rest[: len(JOBS)]
    buf5, buf6, pair, plane, line, load, send, recv, jsend, jrecv, jloc, osem = rest[len(JOBS) :]
    dp, sub, z, q = place()
    me = dp * 2 + sub
    width, inner = wr.shape
    normed = big.at[pl.ds(0, ROWS)]
    loads = {}
    for k, (name, a, b) in enumerate(
        [
            ("slope", slope_in, dsum),
            ("normed", normed_in, normed),
            ("we", w_expand, we),
            ("act2", act2_in, act2),
            ("spatial", spatial_in, spatial),
            ("ws", w_spatial, ws),
            ("act1", act1_in, act1),
            ("reduced", reduced_in, reduced),
            ("masked", masked_in, masked),
            ("wr", w_reduce, wr),
        ]
    ):
        loads[name] = pltpu.make_async_copy(a, b, load.at[k])
        loads[name].start()
    greet_start()

    @pl.loop(0, width // 512)
    def _(n):
        cols = pl.ds(pl.multiple_of(n * 512, 512), 512)
        up = upstream[:, cols]
        pair[sub, pl.ds(0, 1), cols] = jnp.sum(up * sums_in[pl.ds(0, 8), cols], axis=0, keepdims=True)
        pair[sub, pl.ds(1, 1), cols] = jnp.sum(up * sums_in[pl.ds(8, 8), cols], axis=0, keepdims=True)

    wide[pl.ds(0, 8), :] = jnp.zeros((8, inner), f32)
    wide[pl.ds(ROWS + 8, 8), :] = jnp.zeros((8, inner), f32)
    for b in range(3):
        shifted[b, pl.ds(0, 64), :] = jnp.zeros((64, inner), bf16)
        shifted[b, pl.ds(512, 64), :] = jnp.zeros((64, inner), bf16)
    greet_wait()
    third = tree_gen(pair, plane, line, send, recv, grad_norm_expand)
    next(third)
    loads["slope"].wait()

    def scale_slope(lo, hi):
        @pl.loop(lo, hi)
        def _(n):
            cols = pl.ds(pl.multiple_of(n * 256, 256), 256)
            up = upstream[:, cols]
            for k in range(SLOTS // 8):
                rows = pl.ds(64 * k, 64)
                value = dsum[rows, cols].reshape(8, 8, 256) * up[None]
                dsum[rows, cols] = value.reshape(64, 256)

    parts = width // 256
    scale_slope(0, parts // 4)
    next(third)
    scale_slope(parts // 4, parts * 5 // 8)
    next(third)
    scale_slope(parts * 5 // 8, parts)
    loads["normed"].wait()
    loads["we"].wait()
    loads["act2"].wait()
    next(third, None)
    share = 1.0 / stats[pl.ds(6, 1), :]
    plane[0, pl.ds(0, 1), :] = grad_norm_expand[pl.ds(0, 1), :] * share
    plane[0, pl.ds(1, 1), :] = grad_norm_expand[pl.ds(1, 1), :] * share
    plane[1, pl.ds(0, 1), :] = norm_expand[pl.ds(0, 1), :] * stats[pl.ds(5, 1), :]
    first_row = grad_norm_expand[pl.ds(0, 1), :]
    grad_norm_expand[pl.ds(0, 1), :] = grad_norm_expand[pl.ds(1, 1), :]
    grad_norm_expand[pl.ds(1, 1), :] = first_row

    @pl.loop(0, width // 256)
    def _(n):
        cols = pl.ds(pl.multiple_of(n * 256, 256), 256)
        total, dot, gain = plane[0, pl.ds(0, 1), cols], plane[0, pl.ds(1, 1), cols], plane[1, pl.ds(0, 1), cols]
        for k in range(SLOTS // 8):
            rows = pl.ds(64 * k, 64)
            value = dsum[rows, cols] - total - normed[rows, cols] * dot
            dexp[rows, cols] = (columns_of(mask[rows, :], 256) * (value * gain)).astype(bf16)


    small_share = share[:, 0:1]
    loads["spatial"].wait()

    def slope_pass(values, source, norm, at, buf):
        centre, scale = stats[pl.ds(at, 1), pl.ds(0, inner)], stats[pl.ds(at + 1, 1), pl.ds(0, inner)]

        def block(k, carry):
            s1, s2 = carry
            rows = pl.ds(pl.multiple_of(k * 32, 32), 32)
            normal = (source[rows, :] - centre) * scale
            point = norm[pl.ds(0, 1), :] * normal + norm[pl.ds(1, 1), :]
            sig = sigmoid(point)
            value = columns_of(mask[rows, :], inner) * values[rows, :] * (sig * (1.0 + point * (1.0 - sig)))
            values[rows, :] = value
            return s1 + fold8(value), s2 + fold8(value * normal)

        zero = jnp.zeros((8, inner), f32)
        s1, s2 = lax.fori_loop(0, ROWS // 32, block, (zero, zero))
        buf[me, pl.ds(0, 1), :] = jnp.sum(s1, axis=0, keepdims=True)
        buf[me, pl.ds(1, 1), :] = jnp.sum(s2, axis=0, keepdims=True)

    def norm_pass(values, source, norm, at, total, grad_norm, store):
        centre, scale = stats[pl.ds(at, 1), pl.ds(0, inner)], stats[pl.ds(at + 1, 1), pl.ds(0, inner)]
        grad_norm[pl.ds(0, 1), :] = total[1:2]
        grad_norm[pl.ds(1, 1), :] = total[0:1]
        gain = norm[pl.ds(0, 1), :] * scale
        mean, dot = total[0:1] * small_share, total[1:2] * small_share

        @pl.loop(0, ROWS // 32)
        def _(k):
            rows = pl.ds(pl.multiple_of(k * 32, 32), 32)
            normal = (source[rows, :] - centre) * scale
            value = values[rows, :] - mean - normal * dot
            store(k, columns_of(mask[rows, :], inner) * (value * gain))

    @pl.loop(0, inner // 256)
    def _(n):
        cols = pl.ds(pl.multiple_of(n * 256, 256), 256)
        level[:, cols] = mm_nt(dexp[...], we[cols, :])

    slope_pass(level, spatial, norm_spatial, 2, buf5)
    direct_start(buf5, send.at[3], recv.at[3])

    @pl.loop(0, width // 256)
    def _(n):
        cols = pl.ds(pl.multiple_of(n * 256, 256), 256)
        big[:, cols] = mm_tn(act2[...], dexp[:, cols])

    grads = (gs, gr, big)
    outs = (grad_spatial, grad_reduce, grad_expand)
    lands = (land_s, land_r, land_e)

    def make_job(j):
        k, r0, rows, c0, cols, ring_first = JOBS[j]
        half = grads[k].shape[0] // 2

        def cut(ref, base):
            return ref.at[pl.ds(pl.multiple_of(base + r0, 8), rows), pl.ds(c0, cols)]

        return Job(
            ring_first,
            rows,
            cut(grads[k], sub * half),
            cut(grads[k], (1 - sub) * half),
            cut(outs[k], sub * half),
            cut(outs[k], (1 - sub) * half),
            cut(lands[k], 0),
            scratches[j],
            jsend.at[j],
            jrecv.at[j],
            jloc.at[j],
        ).run()

    live = {}

    def begin(*which):
        for j in which:
            live[j] = make_job(j)
            next(live[j])

    def turn():
        for j in sorted(live):
            try:
                next(live[j])
            except StopIteration:
                live.pop(j)

    begin(0, 1)
    total = direct_finish(buf5, send.at[3], recv.at[3])
    turn()

    def store_spatial(k, value):
        wide[pl.ds(pl.multiple_of(k * 32 + 8, 8), 32), :] = value
        shifted[1, pl.ds(pl.multiple_of(k * 32 + 64, 32), 32), :] = value.astype(bf16)

    norm_pass(level, spatial, norm_spatial, 2, total, grad_norm_spatial, store_spatial)

    @pl.loop(0, ROWS // 32)
    def _(k):
        for b in (0, 2):
            rows = wide[pl.ds(pl.multiple_of(k * 32 + 16 - 8 * b, 8), 32), :]
            shifted[b, pl.ds(pl.multiple_of(k * 32 + 64, 32), 32), :] = rows.astype(bf16)

    turn()
    loads["ws"].wait()
    loads["reduced"].wait()
    loads["act1"].wait()

    @pl.loop(0, inner // 256)
    def _(n):
        cols = pl.ds(pl.multiple_of(n * 256, 256), 256)

        def taps(a, total):
            for b in range(3):
                left = shifted[b, pl.ds(128 - 64 * a, ROWS), :]
                right = ws[pl.ds(pl.multiple_of((a * 3 + b) * inner + n * 256, 256), 256), :]
                total = total + mm_nt(left, right)
            return total

        level[:, cols] = taps(0, jnp.zeros((ROWS, 256), f32))
        level[:, cols] = taps(1, level[:, cols])
        level[:, cols] = taps(2, level[:, cols])

    turn()
    slope_pass(level, reduced, norm_reduce, 0, buf6)
    direct_start(buf6, send.at[4], recv.at[4])

    @pl.loop(0, 9)
    def _(tap):
        right = shifted[lax.rem(tap, 3), pl.ds(pl.multiple_of(128 - 64 * (tap // 3), 64), ROWS), :]
        gs[pl.ds(pl.multiple_of(tap * inner, inner), inner), :] = mm_tn(act1[...], right)

    begin(2, 3, 4, 5)
    total = direct_finish(buf6, send.at[4], recv.at[4])

    def store_reduce(k, value):
        dred[pl.ds(pl.multiple_of(k * 32, 32), 32), :] = value.astype(bf16)

    norm_pass(level, reduced, norm_reduce, 0, total, grad_norm_reduce, store_reduce)
    turn()
    loads["masked"].wait()

    @pl.loop(0, width // 256)
    def _(n):
        cols = pl.ds(pl.multiple_of(n * 256, 256), 256)
        gr[cols, :] = mm_tn(masked[:, cols], dred[...])

    begin(6, 7)
    turn()
    loads["wr"].wait()

    @pl.loop(0, width // 256)
    def _(n):
        cols = pl.ds(pl.multiple_of(n * 256, 256), 256)
        value = dsum[:, cols] + mm_nt(dred[...], wr[cols, :])
        dsum[:, cols] = value * columns_of(mask[...], 256)

    images_out = [
        pltpu.make_async_copy(dsum.at[pl.ds(64 * r, 56)], grad_images.at[pl.ds(56 * r, 56)], osem.at[r])
        for r in range(SIDE)
    ]
    for copy in images_out:
        copy.start()
    while live:
        turn()
    for copy in images_out:
        copy.wait()


def backward(
    upstream, masked, reduced, act1, spatial, act2, normed, slope, mask, stats, sums,
    w_reduce, w_spatial, w_expand, norm_reduce, norm_spatial, norm_expand,
):
    width, inner = w_reduce.shape
    hbm = pl.BlockSpec(memory_space=pl.ANY)
    vmem = pl.BlockSpec(memory_space=pltpu.VMEM)
    shape = jax.ShapeDtypeStruct
    landings = [
        pltpu.VMEM((landing_rows(ring_first, rows), cols), f32) for _, _, rows, _, cols, ring_first in JOBS
    ]
    return pl.pallas_call(
        back_kernel,
        out_shape=[
            shape((392, width), f32),
            shape((9 * inner, inner), f32),
            shape((width, inner), f32),
            shape((inner, width), f32),
            shape((2, inner), f32),
            shape((2, inner), f32),
            shape((2, width), f32),
        ],
        in_specs=[vmem] + [hbm] * 7 + [vmem] * 3 + [hbm] * 3 + [vmem] * 3,
        out_specs=[hbm] * 4 + [vmem] * 3,
        scratch_shapes=[
            pltpu.VMEM((width, inner), bf16),
            pltpu.VMEM((9 * inner, inner), bf16),
            pltpu.VMEM((inner, width), bf16),
            pltpu.VMEM((ROWS, width), bf16),
            pltpu.VMEM((ROWS, inner), f32),
            pltpu.VMEM((ROWS, inner), bf16),
            pltpu.VMEM((ROWS, inner), f32),
            pltpu.VMEM((ROWS, inner), bf16),
            pltpu.VMEM((inner, width), f32),
            pltpu.VMEM((ROWS, width), f32),
            pltpu.VMEM((ROWS, width), bf16),
            pltpu.VMEM((ROWS, inner), f32),
            pltpu.VMEM((ROWS + 16, inner), f32),
            pltpu.VMEM((3, ROWS + 128, inner), bf16),
            pltpu.VMEM((ROWS, inner), bf16),
            pltpu.VMEM((9 * inner, inner), f32),
            pltpu.VMEM((width, inner), f32),
            pltpu.VMEM((9 * inner // 2, inner), f32),
            pltpu.VMEM((width // 2, inner), f32),
            pltpu.VMEM((inner // 2, width), f32),
            *landings,
            pltpu.VMEM((32, 2, inner), f32),
            pltpu.VMEM((32, 2, inner), f32),
            pltpu.VMEM((2, 2, width), f32),
            pltpu.VMEM((4, 2, width), f32),
            pltpu.VMEM((4, 2, width), f32),
            pltpu.SemaphoreType.DMA((10,)),
            pltpu.SemaphoreType.DMA((5,)),
            pltpu.SemaphoreType.DMA((5,)),
            pltpu.SemaphoreType.DMA((len(JOBS), JOB_SEMS)),
            pltpu.SemaphoreType.DMA((len(JOBS), JOB_SEMS)),
            pltpu.SemaphoreType.DMA((len(JOBS),)),
            pltpu.SemaphoreType.DMA((SIDE,)),
        ],
        compiler_params=pltpu.CompilerParams(
            collective_id=21, has_side_effects=True, vmem_limit_bytes=63 << 20
        ),
    )(
        upstream, masked, reduced, act1, spatial, act2, normed, slope, mask, stats, sums,
        w_reduce, w_spatial, w_expand, norm_reduce, norm_spatial, norm_expand,
    )


def whiten(codes, pairing):
    highest = lax.Precision.HIGHEST
    total = codes.shape[0]
    centre = jnp.sum(codes, axis=0) / total
    moved = codes - centre
    covariance = jnp.dot(moved.T, moved, precision=highest) / total
    covariance = covariance + whiten_floor * jnp.eye(codes.shape[1], dtype=jnp.float32)
    factor = jnp.linalg.cholesky(covariance)
    inverse = lax.linalg.triangular_solve(factor, jnp.eye(codes.shape[1], dtype=jnp.float32), left_side=True, lower=True)
    white = jnp.dot(moved, inverse.T, precision=highest)
    scale = lax.rsqrt(jnp.sum(white * white, axis=1, keepdims=True) + epsilon)
    unit = white * scale
    same = (pairing[:, None] == pairing[None, :]).astype(jnp.float32)
    gap = 2.0 * unit - jnp.dot(same, unit, precision=highest)
    loss_value = jnp.sum(gap * gap) / total
    grad_unit = 0.5 * (2.0 * gap - jnp.dot(same, gap, precision=highest))
    grad_white = scale * grad_unit - white * scale * scale * scale * jnp.sum(white * grad_unit, axis=1, keepdims=True)
    gram = jnp.dot(grad_white.T, white, precision=highest)
    row = lax.broadcasted_iota(jnp.int32, gram.shape, 0)
    column = lax.broadcasted_iota(jnp.int32, gram.shape, 1)
    lower = jnp.where(row > column, gram, jnp.where(row == column, 0.5 * gram, 0.0))
    both = lower + lower.T
    grad_moved = jnp.dot(grad_white - jnp.dot(white, both, precision=highest) / total, inverse, precision=highest)
    return loss_value, grad_moved - jnp.sum(grad_moved, axis=0) / total


def silu_slope(values):
    sigmoid_value = jax.nn.sigmoid(values)
    return sigmoid_value * (1.0 + values * (1.0 - sigmoid_value))


def moments(sum_value, sum_square, total_count):
    centre = sum_value / total_count
    return (centre, lax.rsqrt(sum_square / total_count - centre * centre + epsilon))


def make_columns(activation):
    images_here, pixel_count, inner_width = activation.shape
    grid_map = activation.reshape(images_here, SIDE, SIDE, inner_width)
    padded = jnp.pad(grid_map, ((0, 0), (1, 1), (1, 1), (0, 0)))
    pieces = [
        padded[:, tap_row : tap_row + SIDE, tap_col : tap_col + SIDE, :]
        for tap_row in range(3)
        for tap_col in range(3)
    ]
    return jnp.concatenate(pieces, axis=3).reshape(images_here * pixel_count, 9 * inner_width)


def fold_columns(columns, images_here, inner_width):
    tap_grads = columns.reshape(images_here, SIDE, SIDE, 9, inner_width)
    padded = jnp.zeros((images_here, SIDE + 2, SIDE + 2, inner_width), jnp.float32)
    for tap_row in range(3):
        for tap_col in range(3):
            padded = padded.at[:, tap_row : tap_row + SIDE, tap_col : tap_col + SIDE, :].add(
                tap_grads[:, :, :, 3 * tap_row + tap_col, :]
            )
    return padded[:, 1 : SIDE + 1, 1 : SIDE + 1, :].reshape(images_here, SIDE * SIDE, inner_width)


def pixel_sums(values, weight):
    return (jnp.sum(values * weight, axis=(0, 1)), jnp.sum(values * values * weight, axis=(0, 1)))


def front(
    masked_low,
    weight,
    counts,
    w_reduce,
    w_spatial,
    w_expand,
    norm_reduce,
    norm_spatial,
    norm_expand,
):
    images_here, pixel_count, width = masked_low.shape
    inner_width = w_reduce.shape[1]
    rows_here = images_here * pixel_count
    reduced = jnp.dot(
        masked_low.reshape(rows_here, width), w_reduce, preferred_element_type=jnp.float32
    ).reshape(images_here, pixel_count, inner_width)
    sum_reduce, square_reduce = pixel_sums(reduced, weight)
    sum_reduce, square_reduce, valid_total = lax.psum((sum_reduce, square_reduce, jnp.sum(counts)), ("dp", "sub"))
    centre_reduce, scale_reduce = moments(sum_reduce, square_reduce, valid_total)
    normed_reduce = (reduced - centre_reduce) * scale_reduce
    level_reduce = norm_reduce[0] * normed_reduce + norm_reduce[1]
    act_reduce = (weight * jax.nn.silu(level_reduce)).astype(jnp.bfloat16)
    columns = make_columns(act_reduce)
    spatial = jnp.dot(
        columns, w_spatial.reshape(9 * inner_width, inner_width), preferred_element_type=jnp.float32
    ).reshape(images_here, pixel_count, inner_width)
    sum_spatial, square_spatial = pixel_sums(spatial, weight)
    sum_spatial, square_spatial = lax.psum((sum_spatial, square_spatial), ("dp", "sub"))
    centre_spatial, scale_spatial = moments(sum_spatial, square_spatial, valid_total)
    normed_spatial = (spatial - centre_spatial) * scale_spatial
    level_spatial = norm_spatial[0] * normed_spatial + norm_spatial[1]
    act_spatial = (weight * jax.nn.silu(level_spatial)).astype(jnp.bfloat16)
    expanded = jnp.dot(
        act_spatial.reshape(rows_here, inner_width), w_expand, preferred_element_type=jnp.float32
    ).reshape(images_here, pixel_count, width)
    sum_expand, square_expand = pixel_sums(expanded, weight)
    sum_expand, square_expand = lax.psum((sum_expand, square_expand), ("dp", "sub"))
    centre_expand, scale_expand = moments(sum_expand, square_expand, valid_total)
    normed_expand = (expanded - centre_expand) * scale_expand
    summed = masked_low.astype(jnp.float32) + norm_expand[0] * normed_expand + norm_expand[1]
    stats = (
        valid_total,
        centre_reduce,
        scale_reduce,
        centre_spatial,
        scale_spatial,
        centre_expand,
        scale_expand,
    )
    return (
        (
            normed_reduce,
            level_reduce,
            columns,
            normed_spatial,
            level_spatial,
            act_spatial,
            normed_expand,
            summed,
        ),
        stats,
    )


def norm_back(upstream, normed, gain, scale_value, sum_grad, dot_grad, total_count):
    return gain * scale_value * (upstream - (sum_grad + normed * dot_grad) / total_count)


def plain_shards(
    images,
    pixel_mask,
    pairing,
    w_reduce,
    w_spatial,
    w_expand,
    w_project,
    w_code,
    norm_reduce,
    norm_spatial,
    norm_expand,
    norm_project,
):
    images_here, pixel_count, width = images.shape
    inner_width = w_reduce.shape[1]
    images_total = pairing.shape[0]
    rows_here = images_here * pixel_count
    highest = lax.Precision.HIGHEST
    weight = pixel_mask.astype(jnp.float32)[:, :, None]
    counts = jnp.sum(weight, axis=1)
    masked_low = images * weight.astype(jnp.bfloat16)
    project_full = w_project.astype(jnp.float32)
    code_full = w_code.astype(jnp.float32)
    saved, stats = front(
        masked_low,
        weight,
        counts,
        w_reduce,
        w_spatial,
        w_expand,
        norm_reduce,
        norm_spatial,
        norm_expand,
    )
    (
        normed_reduce,
        level_reduce,
        columns,
        normed_spatial,
        level_spatial,
        act_spatial,
        normed_expand,
        summed,
    ) = saved
    (
        valid_total,
        centre_reduce,
        scale_reduce,
        centre_spatial,
        scale_spatial,
        centre_expand,
        scale_expand,
    ) = stats
    output = weight * jax.nn.silu(summed)
    own_pooled = jnp.sum(output, axis=1) / counts
    pooled = lax.all_gather(own_pooled, ("dp", "sub"), axis=0, tiled=True)
    projected = jnp.dot(pooled, project_full, precision=highest)
    centre_project, scale_project = moments(
        jnp.sum(projected, axis=0), jnp.sum(projected * projected, axis=0), float(images_total)
    )
    normed_project = (projected - centre_project) * scale_project
    level_project = norm_project[0] * normed_project + norm_project[1]
    hidden = jax.nn.silu(level_project)
    codes = jnp.dot(hidden, code_full, precision=highest)
    loss_value, grad_codes = whiten(codes, pairing)
    grad_w_code = jnp.dot(hidden.T, grad_codes, precision=highest)
    grad_hidden = jnp.dot(grad_codes, code_full.T, precision=highest)
    grad_level_project = grad_hidden * silu_slope(level_project)
    sum_project_grad = jnp.sum(grad_level_project, axis=0)
    dot_project_grad = jnp.sum(grad_level_project * normed_project, axis=0)
    grad_norm_project = jnp.stack([dot_project_grad, sum_project_grad])
    grad_projected = norm_back(
        grad_level_project,
        normed_project,
        norm_project[0],
        scale_project,
        sum_project_grad,
        dot_project_grad,
        float(images_total),
    )
    grad_w_project = jnp.dot(pooled.T, grad_projected, precision=highest)
    own_start = lax.axis_index(("dp", "sub")) * images_here
    own_projected = lax.dynamic_slice_in_dim(grad_projected, own_start, images_here, 0)
    grad_pooled = jnp.dot(own_projected, project_full.T, precision=highest)
    grad_summed = weight * (grad_pooled / counts)[:, None, :] * silu_slope(summed)
    sum_expand_grad, dot_expand_grad = lax.psum(
        (jnp.sum(grad_summed, axis=(0, 1)), jnp.sum(grad_summed * normed_expand, axis=(0, 1))), ("dp", "sub")
    )
    grad_norm_expand = jnp.stack([dot_expand_grad, sum_expand_grad])
    grad_expanded = (
        (
            weight
            * norm_back(
                grad_summed,
                normed_expand,
                norm_expand[0],
                scale_expand,
                sum_expand_grad,
                dot_expand_grad,
                valid_total,
            )
        )
        .astype(jnp.bfloat16)
        .reshape(rows_here, width)
    )
    grad_w_expand = jnp.einsum(
        "rm,rc->mc",
        act_spatial.reshape(rows_here, inner_width),
        grad_expanded,
        preferred_element_type=jnp.float32,
    )
    grad_act_spatial = jnp.einsum(
        "rc,mc->rm", grad_expanded, w_expand, preferred_element_type=jnp.float32
    ).reshape(images_here, pixel_count, inner_width)
    grad_level_spatial = grad_act_spatial * weight * silu_slope(level_spatial)
    sum_spatial_grad, dot_spatial_grad = lax.psum(
        (
            jnp.sum(grad_level_spatial, axis=(0, 1)),
            jnp.sum(grad_level_spatial * normed_spatial, axis=(0, 1)),
        ),
        ("dp", "sub"),
    )
    grad_norm_spatial = jnp.stack([dot_spatial_grad, sum_spatial_grad])
    grad_spatial_out = (
        (
            weight
            * norm_back(
                grad_level_spatial,
                normed_spatial,
                norm_spatial[0],
                scale_spatial,
                sum_spatial_grad,
                dot_spatial_grad,
                valid_total,
            )
        )
        .astype(jnp.bfloat16)
        .reshape(rows_here, inner_width)
    )
    grad_w_spatial = jnp.einsum(
        "rk,rm->km", columns, grad_spatial_out, preferred_element_type=jnp.float32
    ).reshape(3, 3, inner_width, inner_width)
    grad_columns = jnp.einsum(
        "rm,km->rk",
        grad_spatial_out,
        w_spatial.reshape(9 * inner_width, inner_width),
        preferred_element_type=jnp.float32,
    )
    grad_act_reduce = fold_columns(grad_columns, images_here, inner_width)
    grad_level_reduce = grad_act_reduce * weight * silu_slope(level_reduce)
    sum_reduce_grad, dot_reduce_grad = lax.psum(
        (
            jnp.sum(grad_level_reduce, axis=(0, 1)),
            jnp.sum(grad_level_reduce * normed_reduce, axis=(0, 1)),
        ),
        ("dp", "sub"),
    )
    grad_norm_reduce = jnp.stack([dot_reduce_grad, sum_reduce_grad])
    grad_reduced = (
        (
            weight
            * norm_back(
                grad_level_reduce,
                normed_reduce,
                norm_reduce[0],
                scale_reduce,
                sum_reduce_grad,
                dot_reduce_grad,
                valid_total,
            )
        )
        .astype(jnp.bfloat16)
        .reshape(rows_here, inner_width)
    )
    grad_w_reduce = jnp.einsum(
        "rc,rm->cm",
        masked_low.reshape(rows_here, width),
        grad_reduced,
        preferred_element_type=jnp.float32,
    )
    grad_input = jnp.einsum(
        "rm,cm->rc", grad_reduced, w_reduce, preferred_element_type=jnp.float32
    ).reshape(images_here, pixel_count, width)
    grad_images = weight * (grad_summed + grad_input)
    grad_w_spatial, grad_w_reduce, grad_w_expand = lax.psum(
        (grad_w_spatial, grad_w_reduce, grad_w_expand), ("dp", "sub")
    )
    return (
        loss_value,
        grad_images,
        grad_w_reduce,
        grad_w_spatial.reshape(3, 3, inner_width, inner_width),
        grad_w_expand,
        grad_w_project,
        grad_w_code,
        grad_norm_reduce,
        grad_norm_spatial,
        grad_norm_expand,
        grad_norm_project,
    )


def shards(
    images,
    pixel_mask,
    pairing,
    w_reduce,
    w_spatial,
    w_expand,
    w_project,
    w_code,
    norm_reduce,
    norm_spatial,
    norm_expand,
    norm_project,
):
    width, inner = w_reduce.shape
    highest = lax.Precision.HIGHEST
    taps = w_spatial.reshape(9 * inner, inner)
    (
        pooled, hidden, dprojected, dcodes, loss, grad_norm_project, upstream,
        masked, reduced, act1, spatial, act2, normed, slope, mask, stats, sums,
    ) = forward(
        jnp.transpose(images, (1, 0, 2)),
        pixel_mask,
        pairing.reshape(256, 1),
        pairing.reshape(1, 256),
        w_reduce,
        taps,
        w_expand,
        w_project,
        w_code,
        norm_reduce,
        norm_spatial,
        norm_expand,
        norm_project,
    )
    (
        grad_images, grad_spatial, grad_reduce, grad_expand,
        grad_norm_reduce, grad_norm_spatial, grad_norm_expand,
    ) = backward(
        upstream, masked, reduced, act1, spatial, act2, normed, slope, mask, stats, sums,
        w_reduce, taps, w_expand, norm_reduce, norm_spatial, norm_expand,
    )
    grad_project = jnp.dot(pooled.reshape(256, width).T, dprojected, precision=highest)
    grad_code = jnp.dot(hidden.T, dcodes, precision=highest)
    return (
        loss[0, 0],
        jnp.transpose(grad_images.reshape(49, 8, width), (1, 0, 2)),
        grad_reduce,
        grad_spatial.reshape(w_spatial.shape),
        grad_expand,
        grad_project,
        grad_code,
        grad_norm_reduce,
        grad_norm_spatial,
        grad_norm_expand,
        grad_norm_project,
    )


def solution(mesh):
    fits = mesh.shape["dp"] == 16 and mesh.shape["sub"] == 2
    placed = (P(("dp", "sub"), None, None), P(("dp", "sub"), None)) + (P(),) * 10
    return jax.shard_map(
        shards if fits else plain_shards,
        mesh=mesh,
        in_specs=placed,
        out_specs=(P(), P(("dp", "sub"), None, None)) + (P(),) * 9,
        check_vma=False,
    )
```

time: 1410 us -> 288 us (0.20)
  waiting for transfers between devices: 561 us -> 0 us
  blocking collectives: 374 us -> 0 us
  Pallas kernels: 0 us -> 258 us
  local copies, waits for them, and re-layouts: 225 us -> 16.1 us
  other arithmetic: 155 us -> 0.01 us
  matrix products: 69.6 us -> 13.4 us
  between operations: 17.4 us -> 0.73 us
    unnamed x3 -> x0, waiting for transfers between devices: 410 us -> none
    psum x8 -> x0, blocking collectives: 332 us -> none  [the longest x1 50.8 us: front(): lax.psum((sum_expand, square_expand), ('dp', 'sub'))]
    pallas_call x0 -> x2, Pallas kernels: none -> 258 us  [the longest x1 183 us: backward(): pl.pallas_call(back_kernel, out_shape=[shape((392, width), f32), shape((9...]
    all_gather x1 -> x0, waiting for transfers between devices: 151 us -> none  [shards(): lax.all_gather(own_share, ('dp', 'sub'), axis=0, tiled=True).reshape(-1)]
    slice x23 -> x1, local copies, waits for them, and re-layouts: 124 us -> 1.19 us  [shards(): loss[0, 0]]
    all_gather x1 -> x0, other arithmetic: 78.1 us -> none  [shards(): lax.all_gather(own_share, ('dp', 'sub'), axis=0, tiled=True).reshape(-1)]
    dot_general x23 -> x2, matrix products: 68.1 us -> 13.4 us  [the longest x1 10.7 us: shards(): jnp.dot(pooled.reshape(256, width).T, dprojected, precision=highest)]
    all_gather x1 -> x0, blocking collectives: 41.6 us -> none  [shards(): all_codes = lax.all_gather(codes, ('dp', 'sub'), axis=0, tiled=True)]
  transfers between devices with their start and end apart: 2 -> 0, of which waited for: 2 -> 0; matrix products, arithmetic and copies ran while one was open for 1% -> 0% of each run, Pallas kernels for 0% -> 0%
where the time goes in v2:
time: 288 us
  Pallas kernels  258 us (90%)
  local copies, waits for them, and re-layouts  16.1 us (6%)
  matrix products  13.4 us (5%)
    pallas_call x1, Pallas kernels, backward(): pl.pallas_call(back_kernel, out_shape=[shape((392, width), f32), shape((9...  183 us
    pallas_call x1, Pallas kernels, forward(): pl.pallas_call(fwd_kernel, out_shape=[shape((4, 4, 2, 8, width), f32), sh...  75.2 us
    unnamed x32, local copies, waits for them, and re-layouts  13.4 us
    dot_general x1, matrix products, shards(): jnp.dot(pooled.reshape(256, width).T, dprojected, precision=highest)  10.7 us

profile of v2, /device:TPU:0, one launch (start us, length us, event | category | flops | bytes accessed | tf_op | source)
XLA Modules:
  0.0 288.1 jit_solution(3761557933280218036)
XLA Ops:
  0.6 1.5 copy.23.pair_column
  2.1 75.2 %shard_map.203 = (f32[4,4,2,8,2048]{4,3,2,1,0:T(8,128)}, f32[256,1024]{1,0:T(8,128)}, f32[256,1024]{1,0:T(8,128)}, f32[256,128]{1,0:T(8,128)}, f32[8,128]{1,0:T(...) custom-call(bf16[49,8,2048]{2,1,0:T(8,128)(2,1)} %bitcast.21, ...), custom_call_target="tpu_custom_call" | custom-call | tf_op jit(solution)/shard_map/pallas_call | solution.py:630
  77.3 1.2 slice.3
  78.5 182.7 %shard_map.204 = (f32[392,2048]{1,0:T(8,128)}, f32[4608,512]{1,0:T(8,128)}, f32[2048,512]{1,0:T(8,128)}, f32[512,2048]{1,0:T(8,128)}, f32[2,512]{1,0:T(2,128)}, /*index=5*/f32[2,512]{1,0:T(2,128)}, f32[2,2048]{1,0:T(2,128)}) custom-call(f32[8,2048]{1,0:T(8,128)} %get-tuple-element.36.upstream, bf16[448,2048]{1,0:T(8,128)(2,1)} %get-tuple-element.37.masked_in, ...), custom_call_target="tpu_custom_call" | custom-call | tf_op jit(solution)/shard_map/pallas_call | solution.py:1152
  261.2 0.0 copy-start.3
  261.2 0.0 copy-start.4
  261.2 0.0 copy-start.2
  261.2 0.0 slice-start
  261.2 0.0 slice-start.1
  261.3 10.7 %fusion = f32[2048,1024]{1,0:T(8,128)} fusion(f32[256,2048]{1,0:T(8,128)} %bitcast.19, f32[256,1024]{1,0:T(8,128)} %get-tuple-element.52), kind=kOutput, calls=%fused_computation | convolution fusion | flops 6442450944 | bytes 11534336 | tf_op jit(solution)/shard_map/dot_general | solution.py:1586
  272.0 0.0 copy-done.3
  272.0 0.0 copy-done.4
  272.0 2.6 fusion.1
  274.6 0.0 copy-done.2
  274.6 1.7 copy.32
  276.3 0.0 copy-done.1
  276.3 2.0 copy.33
  278.3 0.0 slice-done
  278.3 0.0 slice-done.1
  278.4 0.0 slice-done.2
  278.4 0.0 copy-start
  278.4 4.6 %copy.34 = f32[3,3,512,512]{3,2,1,0:T(8,128)} copy(f32[3,3,512,512]{3,2,1,0:T(8,128)S(1)} %bitcast.18) | data formatting | bytes 18874368
  283.0 0.6 copy-done
  283.6 2.0 copy.35
  285.7 0.0 copy-done.8
  285.7 0.6 copy.36
  286.2 0.0 copy-done.7
  286.3 0.6 copy.37
  286.8 0.0 copy-done.5
  286.8 0.6 copy.38
  287.5 0.0 copy-done.6
  287.5 0.6 copy.39
  (7 shorter events, 0.0 us)
Async XLA Ops:
  261.2 10.8 %copy-start.3 = (f32[256,1024]{1,0:T(8,128)S(1)}, f32[256,1024]{1,0:T(8,128)}, u32[]{:S(2)}) copy-start(f32[256,1024]{1,0:T(8,128)} %get-tuple-element.53) | copy-start | bytes 3145732
  261.2 10.8 %copy-start.4 = (f32[256,128]{1,0:T(8,128)S(1)}, f32[256,128]{1,0:T(8,128)}, u32[]{:S(2)}) copy-start(f32[256,128]{1,0:T(8,128)} %get-tuple-element.54) | copy-start | bytes 393220
  261.2 13.4 %copy-start.2 = (f32[392,2048]{1,0:T(8,128)S(1)}, f32[392,2048]{1,0:T(8,128)}, u32[]{:S(2)}) copy-start(f32[392,2048]{1,0:T(8,128)} %get-tuple-element.47) | copy-start | bytes 9633796
  261.2 17.1 %slice-start = ((s8[9437184]{0:T(1024)(128)(4,1)}), s8[4194304]{0:T(1024)(128)(4,1)S(1)}, s32[]{:S(2)}) async-start(s8[9437184]{0:T(1024)(128)(4,1)} %bitcast.16), calls=%async_computation | async-start | bytes 8388608
  261.2 17.1 %slice-start.1 = ((s8[9437184]{0:T(1024)(128)(4,1)}), s8[4194304]{0:T(1024)(128)(4,1)S(1)}, s32[]{:S(2)}) async-start(s8[9437184]{0:T(1024)(128)(4,1)} %bitcast.16), calls=%async_computation.1 | async-start | bytes 8388608
  272.0 4.3 %copy-start.1 = (f32[2048,512]{1,0:T(8,128)S(1)}, f32[2048,512]{1,0:T(8,128)}, u32[]{:S(2)}) copy-start(f32[2048,512]{1,0:T(8,128)} %get-tuple-element.72) | copy-start | bytes 12582916
  274.6 3.7 %slice-start.2 = ((s8[9437184]{0:T(1024)(128)(4,1)}), s8[1048576]{0:T(1024)(128)(4,1)S(1)}, s32[]{:S(2)}) async-start(s8[9437184]{0:T(1024)(128)(4,1)} %bitcast.16), calls=%async_computation.2 | async-start | bytes 2097152
  278.4 5.3 %copy-start = (f32[512,2048]{1,0:T(8,128)S(1)}, f32[512,2048]{1,0:T(8,128)}, u32[]{:S(2)}) copy-start(f32[512,2048]{1,0:T(8,128)} %get-tuple-element.74) | copy-start | bytes 12582916
  283.6 2.0 copy-start.8
  283.6 2.6 copy-start.7
  283.6 3.2 %copy-start.5 = (f32[2,2048]{1,0:T(2,128)S(1)}, f32[2,2048]{1,0:T(2,128)}, u32[]{:S(2)}) copy-start(f32[2,2048]{1,0:T(2,128)} %get-tuple-element.79) | copy-start | bytes 49156
  283.6 3.8 %copy-start.6 = (f32[2,1024]{1,0:T(2,128)S(1)}, f32[2,1024]{1,0:T(2,128)}, u32[]{:S(2)}) copy-start(f32[2,1024]{1,0:T(2,128)} %get-tuple-element.80) | copy-start | bytes 24580

commit v3 on v2

--- a/solution.py
+++ b/solution.py
@@ -90,30 +90,28 @@
     return total
 
 
-def tree_sums(value, pair, plane, line, send, recv, base=3):
+def tree_gen(pair, plane, line, send, recv, result):
     dp, sub, z, _ = place()
     w = lax.rem(dp, 4)
-    if value is not None:
-        pair[sub] = value
-    remote(pair.at[sub], pair.at[sub], send.at[base + 0], recv.at[base + 0], (dp, 1 - sub)).start()
-    arrived(pair.at[0], recv.at[base + 0])
+    remote(pair.at[sub], pair.at[sub], send.at[0], recv.at[0], (dp, 1 - sub)).start()
+    yield
+    arrived(pair.at[0], recv.at[0])
     plane[w] = pair[0] + pair[1]
     for k in range(1, 4):
-        remote(
-            plane.at[w], plane.at[w], send.at[base + 1], recv.at[base + 1], (z * 4 + lax.rem(w + k, 4), sub)
-        ).start()
-    arrived(plane.at[pl.ds(0, 3)], recv.at[base + 1])
+        where = (z * 4 + lax.rem(w + k, 4), sub)
+        remote(plane.at[w], plane.at[w], send.at[1], recv.at[1], where).start()
+    yield
+    arrived(plane.at[pl.ds(0, 3)], recv.at[1])
     line[z] = (plane[0] + plane[1]) + (plane[2] + plane[3])
     for k in range(1, 4):
-        remote(
-            line.at[z], line.at[z], send.at[base + 2], recv.at[base + 2], (lax.rem(z + k, 4) * 4 + w, sub)
-        ).start()
-    arrived(line.at[pl.ds(0, 3)], recv.at[base + 2])
-    total = (line[0] + line[1]) + (line[2] + line[3])
-    arrived(pair.at[0], send.at[base + 0])
-    arrived(plane.at[pl.ds(0, 3)], send.at[base + 1])
-    arrived(line.at[pl.ds(0, 3)], send.at[base + 2])
-    return total
+        where = (lax.rem(z + k, 4) * 4 + w, sub)
+        remote(line.at[z], line.at[z], send.at[2], recv.at[2], where).start()
+    yield
+    arrived(line.at[pl.ds(0, 3)], recv.at[2])
+    result[...] = (line[0] + line[1]) + (line[2] + line[3])
+    arrived(pair.at[0], send.at[0])
+    arrived(plane.at[pl.ds(0, 3)], send.at[1])
+    arrived(line.at[pl.ds(0, 3)], send.at[2])
 
 
 class Mover:
@@ -152,6 +150,12 @@
             else:
                 pl.when(cond)(body)
         self.pending = []
+
+    def settle(self, s):
+        for cond, ref, other in self.pending:
+            if other == s:
+                arrived(ref, self.send.at[s])
+        self.pending = [item for item in self.pending if item[2] != s]
 
     def line_gather(self, at, first, base):
         dp, sub, z, _ = place()
@@ -173,6 +177,26 @@
             self.got(z >= t + 1, hold(z - 1 - t), base + t)
             self.got(z <= 2 - t, hold(z + 1 + t), base + 3 + t)
 
+    def line_direct(self, at, first, base):
+        dp, sub, z, _ = place()
+        w = lax.rem(dp, 4)
+        for k in range(1, 4):
+            where = (lax.rem(z + k, 4) * 4 + w, sub)
+            self.go(None, first, at(z), base + k - 1, base + k - 1, where)
+        yield
+        for k in range(1, 4):
+            self.got(None, at(lax.rem(z + 4 - k, 4)), base + k - 1)
+
+    def ring_direct(self, blk, first, base, after):
+        dp, sub, z, q = place()
+        src = first if first is not None else blk(0, None)
+        for k in range(1, 4):
+            self.go(None, src, blk(0, None), base + k - 1, base + k - 1, (ring_dp(z, q + k), sub))
+        yield
+        for k in range(1, 4):
+            self.got(None, blk(4 - k, None), base + k - 1)
+            after(blk(4 - k, None), 3 - k)
+
     def ring_gather(self, blk, first, base, after):
         dp, sub, z, q = place()
         after_me, before_me = (ring_dp(z, q + 1), sub), (ring_dp(z, q + 3), sub)
@@ -205,13 +229,14 @@
         tick += 1
 
 
-def gather_pooled(own, out, send, recv, split):
+def gather_rows(own, out, send, recv, split, direct=(1, 0, 1, 1)):
     dp, sub, z, q = place()
     width = out.shape[-1]
     sib = (dp, 1 - sub)
 
     def first_line():
         cols = pl.ds(0, split)
+        mid = split // 2
         mover = Mover(send.at[0], recv.at[0])
         at = lambda j: out.at[j, plane_of(q), sub, :, cols]
 
@@ -224,9 +249,11 @@
         def share(ref, s):
             mover.go(None, ref, ref, 10 + s, 10, sib)
 
-        yield from mover.line_gather(at, own.at[:, cols], 0)
+        line = mover.line_direct if direct[0] else mover.line_gather
+        yield from line(at, own.at[:, cols], 0)
         share(blk(0, None), 3)
-        yield from mover.ring_gather(blk, None, 6, share)
+        ring = mover.ring_direct if direct[1] else mover.ring_gather
+        yield from ring(blk, None, 6, share)
         yield
         arrived(out.at[:, :, 1 - sub, :, cols], recv.at[0, 10])
         mover.drain()
@@ -247,9 +274,11 @@
         def share(ref, s):
             mover.go(None, ref, ref, 10 + s, 10, sib)
 
-        yield from mover.ring_gather(blk, own.at[:, cols], 0, lambda ref, s: None)
+        ring = mover.ring_direct if direct[2] else mover.ring_gather
+        yield from ring(blk, own.at[:, cols], 0, lambda ref, s: None)
         share(at(z), 3)
-        yield from mover.line_gather(at, None, 4)
+        line = mover.line_direct if direct[3] else mover.line_gather
+        yield from line(at, at(z), 4)
         for k in range(1, 4):
             share(at(lax.rem(z + k, 4)), k - 1)
         yield
@@ -346,14 +375,14 @@
 
 
 def fwd_kernel(
-    images, pixel_mask, pair_column, pair_row, w_reduce, w_spatial, w_expand, w_project, w_code,
+    images, pixel_mask, pair_row, w_reduce, w_spatial, w_expand, w_project, w_code,
     norm_reduce, norm_spatial, norm_expand, norm_project,
     pooled_out, hidden_out, dprojected_out, dcodes_out, loss_out, grad_norm_out, upstream,
     masked_out, reduced_out, act1_out, spatial_out, act2_out, normed_out, slope_out, mask, stats, sums_out,
     img, masked, wr, ws, we, wp, wc, reduced, wide, shifted, spatial, act2, normed, slope, own,
-    pooled_all, pool_high, pool_low, level, normal, hidden, dproj, counts,
+    own_proj, proj_all, same, totals, act1_turned, act2_turned, level, normal, hidden, dproj, counts,
     counts_buf, buf1, buf2, pair, plane, line,
-    load, save, send, recv, gsend, grecv,
+    load, save, send, recv, gsend, grecv, hsend, hrecv,
 ):
     dp, sub, z, q = place()
     me = dp * 2 + sub
@@ -361,8 +390,8 @@
     width = wr.shape[0]
     loads = [pltpu.make_async_copy(a, b, load.at[k]) for k, (a, b) in enumerate(
         [(images, img), (w_reduce, wr), (w_spatial, ws), (w_expand, we), (w_project, wp), (w_code, wc)])]
-    for copy in loads:
-        copy.start()
+    loads[0].start()
+    loads[1].start()
     greet_start()
     here = pixel_mask[...].astype(f32)
     counts[...] = jnp.broadcast_to(jnp.sum(here, axis=1, keepdims=True), (8, 128))
@@ -375,13 +404,14 @@
         mask[pl.ds(8 * slot, 8), :] = value
     wide[pl.ds(0, 8), :] = jnp.zeros((8, inner), f32)
     wide[pl.ds(ROWS + 8, 8), :] = jnp.zeros((8, inner), f32)
-    for b in range(3):
-        shifted[b, pl.ds(0, 64), :] = jnp.zeros((64, inner), bf16)
-        shifted[b, pl.ds(512, 64), :] = jnp.zeros((64, inner), bf16)
+    shifted[pl.ds(0, 64), :] = jnp.zeros((64, 3 * inner), bf16)
+    shifted[pl.ds(512, 64), :] = jnp.zeros((64, 3 * inner), bf16)
     greet_wait()
     counts_buf[me] = counts[...]
     direct_start(counts_buf, send.at[0], recv.at[0])
     loads[0].wait()
+    for copy in loads[2:]:
+        copy.start()
     gap = jnp.zeros((8, 256), f32)
 
     @pl.loop(0, width // 256)
@@ -412,6 +442,8 @@
 
     direct_start(buf1, send.at[1], recv.at[1])
     keep(reduced, reduced_out)
+    pairs = jnp.broadcast_to(pair_row[...].astype(f32), (256, 256))
+    same[...] = (pairs == jnp.transpose(pairs)).astype(f32)
     valid = jnp.sum(direct_finish(counts_buf, send.at[0], recv.at[0]), axis=0, keepdims=True)[:, 0:1]
     inverse_valid = 1.0 / valid
 
@@ -435,7 +467,7 @@
 
     def store_wide(k, value):
         wide[pl.ds(pl.multiple_of(k * 32 + 8, 8), 32), :] = value
-        shifted[1, pl.ds(pl.multiple_of(k * 32 + 64, 32), 32), :] = value.astype(bf16)
+        shifted[pl.ds(pl.multiple_of(k * 32 + 64, 32), 32), pl.ds(inner, inner)] = value.astype(bf16)
 
     activate(reduced, norm_reduce, centre1, scale1, store_wide)
 
@@ -443,40 +475,33 @@
     def _(k):
         for b in (0, 2):
             rows = wide[pl.ds(pl.multiple_of(k * 32 + 8 * b, 8), 32), :]
-            shifted[b, pl.ds(pl.multiple_of(k * 32 + 64, 32), 32), :] = rows.astype(bf16)
-
-    keep(shifted.at[1, pl.ds(64, ROWS)], act1_out)
+            shifted[pl.ds(pl.multiple_of(k * 32 + 64, 32), 32), pl.ds(b * inner, inner)] = rows.astype(bf16)
+
     loads[2].wait()
 
     @pl.loop(0, inner // 256)
     def _(n):
         cols = pl.ds(pl.multiple_of(n * 256, 256), 256)
 
-        def taps(a, total):
-            for b in range(3):
-                left = shifted[b, pl.ds(pl.multiple_of(a * 64, 64), ROWS), :]
-                right = ws[pl.ds(pl.multiple_of((a * 3 + b) * inner, inner), inner), cols]
-                total = total + mm(left, right)
-            return total
-
-        spatial[:, cols] = taps(0, jnp.zeros((ROWS, 256), f32))
-        spatial[:, cols] = taps(1, spatial[:, cols])
-        got = taps(2, spatial[:, cols]) * columns_of(mask[...], 256)
+        left = jnp.concatenate([shifted[pl.ds(64 * a, ROWS), :] for a in range(3)], axis=1)
+        got = mm(left, ws[:, cols]) * columns_of(mask[...], 256)
         spatial[:, cols] = got
         buf2[me, pl.ds(0, 1), cols] = jnp.sum(got, axis=0, keepdims=True)
         buf2[me, pl.ds(1, 1), cols] = jnp.sum(got * got, axis=0, keepdims=True)
 
     direct_start(buf2, send.at[2], recv.at[2])
     keep(spatial, spatial_out)
+    act1_turned[...] = jnp.transpose(wide[pl.ds(8, ROWS), :]).astype(bf16)
+    keep(act1_turned, act1_out)
     centre2, scale2 = moments(direct_finish(buf2, send.at[2], recv.at[2]))
     stats[pl.ds(2, 1), pl.ds(0, inner)] = centre2
     stats[pl.ds(3, 1), pl.ds(0, inner)] = scale2
 
     def store_act2(k, value):
+        wide[pl.ds(pl.multiple_of(k * 32 + 8, 8), 32), :] = value
         act2[pl.ds(pl.multiple_of(k * 32, 32), 32), :] = value.astype(bf16)
 
     activate(spatial, norm_spatial, centre2, scale2, store_act2)
-    keep(act2, act2_out)
     loads[3].wait()
 
     @pl.loop(0, width // 256)
@@ -487,70 +512,95 @@
         pair[sub, pl.ds(0, 1), cols] = jnp.sum(got, axis=0, keepdims=True)
         pair[sub, pl.ds(1, 1), cols] = jnp.sum(got * got, axis=0, keepdims=True)
 
-    centre3, scale3 = moments(tree_sums(None, pair, plane, line, send, recv))
+    third = tree_gen(pair, plane, line, send.at[pl.ds(3, 3)], recv.at[pl.ds(3, 3)], totals)
+    next(third)
+    next(third)
+    act2_turned[...] = jnp.transpose(wide[pl.ds(8, ROWS), :]).astype(bf16)
+    keep(act2_turned, act2_out)
+    next(third)
+    next(third, None)
+    centre3, scale3 = moments(totals[...])
     stats[pl.ds(4, 1), :] = centre3
     stats[pl.ds(5, 1), :] = scale3
     stats[pl.ds(6, 1), :] = jnp.broadcast_to(valid, (1, width))
     stats[pl.ds(7, 1), :] = jnp.zeros((1, width), f32)
     inverse_counts = 1.0 / counts[...]
 
+    def last_norm(cols, rows):
+        gain, bias = norm_expand[pl.ds(0, 1), cols], norm_expand[pl.ds(1, 1), cols]
+        n3 = (normed[rows, cols] - stats[pl.ds(4, 1), cols]) * stats[pl.ds(5, 1), cols]
+        total = masked[rows, cols].astype(f32) + gain * n3 + bias
+        sig = sigmoid(total)
+        return n3, sig, total * sig
+
     @pl.loop(0, width // 256)
     def _(n):
         cols = pl.ds(pl.multiple_of(n * 256, 256), 256)
-        centre, scale = stats[pl.ds(4, 1), cols], stats[pl.ds(5, 1), cols]
-        gain, bias = norm_expand[pl.ds(0, 1), cols], norm_expand[pl.ds(1, 1), cols]
-
-        def block(k, carry):
-            pool, s1, s2 = carry
-            rows = pl.ds(pl.multiple_of(k * 64, 64), 64)
-            here = columns_of(mask[rows, :], 256)
-            n3 = (normed[rows, cols] - centre) * scale
-            total = masked[rows, cols].astype(f32) + gain * n3 + bias
-            sig = sigmoid(total)
-            out = total * sig
-            slope3 = here * (sig + out * (1.0 - sig))
-            normed[rows, cols] = n3
-            slope[rows, cols] = slope3
-            return pool + fold8(here * out), s1 + fold8(slope3), s2 + fold8(slope3 * n3)
-
-        zero = jnp.zeros((8, 256), f32)
-        pool, s1, s2 = lax.fori_loop(0, ROWS // 64, block, (zero, zero, zero))
+        pool = jnp.zeros((8, 256), f32)
+        for k in range(SIDE):
+            rows = pl.ds(64 * k, 64)
+            _, _, out = last_norm(cols, rows)
+            pool = pool + fold8(columns_of(mask[rows, :], 256) * out)
         own[:, cols] = pool * columns_of(inverse_counts, 256)
-        sums_out[pl.ds(0, 8), cols] = s1
-        sums_out[pl.ds(8, 8), cols] = s2
-
-    keep(normed, normed_out)
-    keep(slope, slope_out)
-    movers = gather_pooled(own, pooled_all, gsend, grecv, 1536)
-    for mover in movers:
-        next(mover)
-    pooled_all[z, lax.rem(dp, 4), sub] = own[...]
-    run_all(movers)
+
+    def slopes(lo, hi):
+        @pl.loop(lo, hi)
+        def _(n):
+            cols = pl.ds(pl.multiple_of(n * 256, 256), 256)
+            s1 = s2 = jnp.zeros((8, 256), f32)
+            for k in range(SIDE):
+                rows = pl.ds(64 * k, 64)
+                n3, sig, out = last_norm(cols, rows)
+                slope3 = columns_of(mask[rows, :], 256) * (sig + out * (1.0 - sig))
+                normed[rows, cols] = n3
+                slope[rows, cols] = slope3
+                s1, s2 = s1 + fold8(slope3), s2 + fold8(slope3 * n3)
+            sums_out[pl.ds(0, 8), cols] = s1
+            sums_out[pl.ds(8, 8), cols] = s2
+
     rows_all = 256
-    keep(pooled_all, pooled_out)
     loads[4].wait()
     loads[5].wait()
-
-    @pl.loop(0, rows_all // 8)
-    def _(k):
-        value = pooled_all[k // 8, lax.rem(k // 2, 4), lax.rem(k, 2)]
-        level[pl.ds(pl.multiple_of(k * 8, 8), 8), :] = value
-
-    @pl.loop(0, rows_all // 32)
-    def _(k):
-        rows = pl.ds(pl.multiple_of(k * 32, 32), 32)
-        high, low = split(level[rows, :])
-        pool_high[rows, :] = high
-        pool_low[rows, :] = low
-
+    high = own[...].astype(bf16).astype(f32)
+    both_terms = jnp.concatenate([high, own[...] - high], axis=0).astype(bf16)
     proj = hidden.shape[1]
-    share = 1.0 / rows_all
 
     @pl.loop(0, proj // 256)
     def _(n):
         cols = pl.ds(pl.multiple_of(n * 256, 256), 256)
-        right = wp[:, cols]
-        value = mm(pool_high[...], right) + mm(pool_low[...], right)
+        value = mm(both_terms, wp[:, cols])
+        own_proj[:, cols] = value[0:8] + value[8:16]
+
+    proj_all[z, lax.rem(dp, 4), sub] = own_proj[...]
+    proj_movers = gather_rows(own_proj, proj_all, gsend, grecv, proj * 3 // 4, (1, 1, 1, 1))
+    pool_movers = gather_rows(own, pooled_out, hsend, hrecv, 1536, (1, 0, 1, 1))
+
+    def move(movers):
+        for mover in movers:
+            next(mover, None)
+
+    mine = pltpu.make_async_copy(own, pooled_out.at[z, lax.rem(dp, 4), sub], load.at[0])
+    mine.start()
+    move(proj_movers)
+    slopes(0, 3)
+    move(proj_movers)
+    move(pool_movers)
+    slopes(3, 6)
+    move(proj_movers)
+    slopes(6, 8)
+    keep(normed, normed_out)
+    keep(slope, slope_out)
+    mine.wait()
+    move(proj_movers)
+    move(proj_movers)
+    move(pool_movers)
+
+    share = 1.0 / rows_all
+
+    @pl.loop(0, proj // 256)
+    def _(n):
+        cols = pl.ds(pl.multiple_of(n * 256, 256), 256)
+        value = proj_all[:, :, :, :, cols].reshape(rows_all, 256)
         centre = jnp.sum(value, axis=0, keepdims=True) * share
         square = jnp.sum(value * value, axis=0, keepdims=True) * share
         scale = lax.rsqrt(square - centre * centre + epsilon)
@@ -572,11 +622,11 @@
     row = lax.broadcasted_iota(jnp.int32, (size, size), 0)
     column = lax.broadcasted_iota(jnp.int32, (size, size), 1)
     inverse = factor_inverse(cov + jnp.where(row == column, whiten_floor, 0.0))
+    move(pool_movers)
     white = exact(moved, inverse, ((1,), (1,)))
     unit_scale = lax.rsqrt(jnp.sum(white * white, axis=1, keepdims=True) + epsilon)
     unit = white * unit_scale
-    same = (pair_column[...] == pair_row[...]).astype(f32)
-    gap = 2.0 * unit - exact(same, unit, ((1,), (0,)))
+    gap = 2.0 * unit - exact(same[...], unit, ((1,), (0,)))
     loss_out[...] = jnp.broadcast_to(jnp.sum(jnp.sum(gap * gap, axis=1, keepdims=True), axis=0, keepdims=True) * share, (8, 128))
     grad_white = unit_scale * (gap - unit * jnp.sum(unit * gap, axis=1, keepdims=True))
     gram = exact(grad_white, white, ((0,), (0,)))
@@ -586,6 +636,7 @@
     dcodes = grad_moved - jnp.sum(grad_moved, axis=0, keepdims=True) * share
     dcodes_out[...] = dcodes
 
+    move(pool_movers)
     high, low = split(dcodes)
 
     @pl.loop(0, proj // 256)
@@ -604,6 +655,9 @@
         dproj[:, cols] = upstream[pl.ds(0, 1), cols] * (grad - (total + normal_here * dot) * share)
 
     keep(dproj, dprojected_out)
+    for mover in pool_movers:
+        for _ in mover:
+            pass
     mine = dproj[pl.ds(pl.multiple_of(me * 8, 8), 8), :]
     high = mine.astype(bf16).astype(f32)
     both_terms = jnp.concatenate([high, mine - high], axis=0).astype(bf16)
@@ -619,7 +673,7 @@
 
 
 def forward(
-    images, pixel_mask, pair_column, pair_row, w_reduce, w_spatial, w_expand, w_project, w_code,
+    images, pixel_mask, pair_row, w_reduce, w_spatial, w_expand, w_project, w_code,
     norm_reduce, norm_spatial, norm_expand, norm_project,
 ):
     width, inner = w_reduce.shape
@@ -639,16 +693,16 @@
             shape((8, width), f32),
             shape((ROWS, width), bf16),
             shape((ROWS, inner), f32),
-            shape((ROWS, inner), bf16),
+            shape((inner, ROWS), bf16),
             shape((ROWS, inner), f32),
-            shape((ROWS, inner), bf16),
+            shape((inner, ROWS), bf16),
             shape((ROWS, width), f32),
             shape((ROWS, width), f32),
             shape((ROWS, 128), f32),
             shape((8, width), f32),
             shape((16, width), f32),
         ],
-        in_specs=[hbm, vmem, vmem, vmem, hbm, hbm, hbm, hbm, hbm, vmem, vmem, vmem, vmem],
+        in_specs=[hbm, vmem, vmem, hbm, hbm, hbm, hbm, hbm, vmem, vmem, vmem, vmem],
         out_specs=[hbm, hbm, hbm, vmem, vmem, vmem, vmem] + [hbm] * 7 + [vmem] * 3,
         scratch_shapes=[
             pltpu.VMEM((49, 8, width), bf16),
@@ -660,16 +714,19 @@
             pltpu.VMEM((proj, code), bf16),
             pltpu.VMEM((ROWS, inner), f32),
             pltpu.VMEM((ROWS + 16, inner), f32),
-            pltpu.VMEM((3, ROWS + 128, inner), bf16),
+            pltpu.VMEM((ROWS + 128, 3 * inner), bf16),
             pltpu.VMEM((ROWS, inner), f32),
             pltpu.VMEM((ROWS, inner), bf16),
             pltpu.VMEM((ROWS, width), f32),
             pltpu.VMEM((ROWS, width), f32),
             pltpu.VMEM((8, width), f32),
-            pltpu.VMEM((4, 4, 2, 8, width), f32),
-            pltpu.VMEM((256, width), bf16),
-            pltpu.VMEM((256, width), bf16),
-            pltpu.VMEM((256, width), f32),
+            pltpu.VMEM((8, proj), f32),
+            pltpu.VMEM((4, 4, 2, 8, proj), f32),
+            pltpu.VMEM((256, 256), f32),
+            pltpu.VMEM((2, width), f32),
+            pltpu.VMEM((inner, ROWS), bf16),
+            pltpu.VMEM((inner, ROWS), bf16),
+            pltpu.VMEM((256, proj), f32),
             pltpu.VMEM((256, proj), f32),
             pltpu.VMEM((256, proj), f32),
             pltpu.VMEM((256, proj), f32),
@@ -686,22 +743,28 @@
             pltpu.SemaphoreType.DMA((6,)),
             pltpu.SemaphoreType.DMA((2, 14)),
             pltpu.SemaphoreType.DMA((2, 14)),
+            pltpu.SemaphoreType.DMA((2, 14)),
+            pltpu.SemaphoreType.DMA((2, 14)),
         ],
         compiler_params=pltpu.CompilerParams(
             collective_id=20, has_side_effects=True, vmem_limit_bytes=58 << 20
         ),
     )(
-        images, pixel_mask, pair_column, pair_row, w_reduce, w_spatial, w_expand, w_project, w_code,
+        images, pixel_mask, pair_row, w_reduce, w_spatial, w_expand, w_project, w_code,
         norm_reduce, norm_spatial, norm_expand, norm_project,
     )
 
 
+def halves(ref, h):
+    cols = ref.shape[1] // 2
+    return ref.at[:, pl.ds(h * cols, cols)]
+
+
 class Job:
-    def __init__(self, ring_first, rows, acc, other, out, sib_out, land, scratch, send, recv, loc):
+    def __init__(self, ring_first, rows, acc, other, land, scratch, send, recv, free):
         self.ring_first, self.rows, self.acc, self.other = ring_first, rows, acc, other
-        self.out, self.sib_out, self.land, self.scratch = out, sib_out, land, scratch
+        self.land, self.scratch, self.free = land, scratch, free
         self.mover = Mover(send, recv)
-        self.loc = loc
         self.taken = 0
 
     def take(self, rows):
@@ -709,34 +772,29 @@
         self.taken += rows
         return ref
 
-    def start(self):
-        dp, sub, _, _ = place()
-        self.mover.go(None, self.other, self.land, 0, 0, (dp, 1 - sub))
-
     def ring_reduce(self, base, block):
         dp, sub, z, q = place()
         go, got = self.mover.go, self.mover.got
         after_me, before_me = (ring_dp(z, q + 1), sub), (ring_dp(z, q + 3), sub)
-        half = block // 2
-        r0a, r0b, r1a, r1b = self.take(half), self.take(half), self.take(block), self.take(block)
-
-        def blk(k, h=0, n=block):
-            return rows_at(self.acc, base + lax.rem(q + k, 4) * block + h, n)
-
-        go(None, blk(2, 0, half), r0a, 1, 1, after_me)
-        go(None, blk(2, half, half), r0b, 2, 2, before_me)
+        r0 = self.take(block)
+        r1a, r1b = self.take(block), self.take(block)
+
+        def blk(k):
+            return rows_at(self.land, base + lax.rem(q + k, 4) * block, block)
+
+        go(None, halves(blk(2), 0), halves(r0, 0), 1, 1, after_me)
+        go(None, halves(blk(2), 1), halves(r0, 1), 2, 2, before_me)
         yield
-        got(None, r0a, 1)
-        add_into(blk(1, 0, half), r0a, half)
+        got(None, halves(r0, 0), 1)
+        add_into(halves(blk(1), 0), halves(r0, 0), block)
         go(None, blk(1), r1a, 3, 3, after_me)
-        got(None, r0b, 2)
-        add_into(blk(3, half, half), r0b, half)
+        got(None, halves(r0, 1), 2)
+        add_into(halves(blk(3), 1), halves(r0, 1), block)
         go(None, blk(3), r1b, 4, 4, before_me)
         yield
         got(None, r1a, 3)
-        add_into(blk(0), r1a, block)
         got(None, r1b, 4)
-        add_into(blk(0), r1b, block)
+        add_into(blk(0), r1a, block, r1b)
 
     def line_reduce(self, base, chunk):
         dp, sub, z, _ = place()
@@ -746,7 +804,7 @@
         high = [self.take(chunk) for _ in range(3)]
 
         def at(j):
-            return rows_at(self.acc, base + jnp.clip(j, 0, 3) * chunk, chunk)
+            return rows_at(self.land, base + jnp.clip(j, 0, 3) * chunk, chunk)
 
         for t in range(3):
             go(z <= t, at(3 + z - t), low[t], 5 + t, 5 + t, up)
@@ -768,73 +826,78 @@
     def run(self):
         dp, sub, z, q = place()
         sib = (dp, 1 - sub)
-        mover, out, rows = self.mover, self.out, self.rows
-        self.start()
+        mover, acc, rows = self.mover, self.acc, self.rows
+        mover.go(None, self.other, self.land, 0, 0, sib)
         yield
         mover.got(None, self.land, 0)
-        add_into(self.acc, self.land, rows)
+        add_into(self.land, acc, rows)
         big, small = rows // 4, rows // 16
-        half_small = small // 2
-        half_big = big // 2
+
+        def hand_over():
+            mover.settle(0)
+            pl.semaphore_signal(self.free, inc=1, device_id=dev(*sib), device_id_type=MESH)
+
+        def total(start):
+            copy_into(rows_at(acc, start, small), rows_at(self.land, start, small), small)
 
         def share(ref, k):
             mover.go(None, ref, ref, 21 + k, 21, sib)
 
         if self.ring_first:
             yield from self.ring_reduce(0, big)
+            hand_over()
             yield from self.line_reduce(q * big, small)
-            mine = rows_at(self.acc, q * big + z * small, small)
-            own = rows_at(out, q * big + z * small, small)
-            local = pltpu.make_async_copy(mine, own, self.loc)
-            local.start()
-            at = lambda j: rows_at(out, q * big + j * small, small)
-            yield from mover.line_gather(at, mine, 11)
-            local.wait()
-            share(rows_at(out, q * big, big), 3)
+            total(q * big + z * small)
+            at = lambda j: rows_at(acc, q * big + j * small, small)
+            yield from mover.line_gather(at, None, 11)
+            pl.semaphore_wait(self.free, 1)
+            share(rows_at(acc, q * big, big), 3)
 
             def blk(k, h):
-                start = lax.rem(q + k, 4) * big
-                if h is None:
-                    return rows_at(out, start, big)
-                return rows_at(out, start + h * half_big, half_big)
+                ref = rows_at(acc, lax.rem(q + k, 4) * big, big)
+                return ref if h is None else halves(ref, h)
 
             yield from mover.ring_gather(blk, None, 17, share)
         else:
             yield from self.line_reduce(0, big)
+            hand_over()
             yield from self.ring_reduce(z * big, small)
-            mine = rows_at(self.acc, z * big + q * small, small)
-            own = rows_at(out, z * big + q * small, small)
-            local = pltpu.make_async_copy(mine, own, self.loc)
-            local.start()
+            total(z * big + q * small)
 
             def blk(k, h):
-                start = z * big + lax.rem(q + k, 4) * small
-                if h is None:
-                    return rows_at(out, start, small)
-                return rows_at(out, start + h * half_small, half_small)
-
-            yield from mover.ring_gather(blk, mine, 17, lambda ref, k: None)
-            local.wait()
-            share(rows_at(out, z * big, big), 3)
-            at = lambda j: rows_at(out, j * big, big)
+                ref = rows_at(acc, z * big + lax.rem(q + k, 4) * small, small)
+                return ref if h is None else halves(ref, h)
+
+            yield from mover.ring_gather(blk, None, 17, lambda ref, k: None)
+            pl.semaphore_wait(self.free, 1)
+            share(rows_at(acc, z * big, big), 3)
+            at = lambda j: rows_at(acc, j * big, big)
             yield from mover.line_gather(at, None, 11)
             for k in range(1, 4):
-                share(rows_at(out, lax.rem(z + k, 4) * big, big), k - 1)
+                share(rows_at(acc, lax.rem(z + k, 4) * big, big), k - 1)
         yield
-        arrived(self.sib_out, mover.recv.at[21])
+        arrived(self.other, mover.recv.at[21])
         mover.drain()
 
 
 JOB_SEMS = 25
 
 
-def add_into(dst, src, rows):
+def add_into(dst, src, rows, more=None):
     step = 16 if rows % 16 == 0 else 8
 
     @pl.loop(0, rows // step)
     def _(k):
         at = pl.ds(pl.multiple_of(k * step, 8), step)
-        dst[at, :] = dst[at, :] + src[at, :]
+        value = dst[at, :] + src[at, :]
+        dst[at, :] = value if more is None else value + more[at, :]
+
+
+def copy_into(dst, src, rows):
+    @pl.loop(0, rows // 8)
+    def _(k):
+        at = pl.ds(pl.multiple_of(k * 8, 8), 8)
+        dst[at, :] = src[at, :]
 
 
 def rows_at(ref, start, size):
@@ -847,50 +910,46 @@
 
 
 JOBS = (
-    (2, 0, 256, 0, 1536, True),
-    (2, 0, 256, 1536, 512, False),
-    (0, 0, 896, 0, 512, True),
-    (0, 896, 256, 0, 512, False),
-    (0, 1152, 896, 0, 512, True),
+    (2, 0, 256, 0, 768, True),
+    (2, 0, 256, 768, 256, False),
+    (2, 0, 256, 1024, 768, True),
+    (2, 0, 256, 1792, 256, False),
+    (0, 0, 512, 0, 512, True),
+    (0, 512, 256, 0, 512, False),
+    (0, 768, 512, 0, 512, True),
+    (0, 1280, 256, 0, 512, False),
+    (0, 1536, 512, 0, 512, True),
     (0, 2048, 256, 0, 512, False),
-    (1, 0, 768, 0, 512, True),
-    (1, 768, 256, 0, 512, False),
+    (1, 0, 384, 0, 512, True),
+    (1, 384, 128, 0, 512, False),
+    (1, 512, 384, 0, 512, True),
+    (1, 896, 128, 0, 512, False),
 )
 
-
-def tree_gen(pair, plane, line, send, recv, result):
-    dp, sub, z, _ = place()
-    w = lax.rem(dp, 4)
-    remote(pair.at[sub], pair.at[sub], send.at[0], recv.at[0], (dp, 1 - sub)).start()
-    yield
-    arrived(pair.at[0], recv.at[0])
-    plane[w] = pair[0] + pair[1]
-    for k in range(1, 4):
-        where = (z * 4 + lax.rem(w + k, 4), sub)
-        remote(plane.at[w], plane.at[w], send.at[1], recv.at[1], where).start()
-    yield
-    arrived(plane.at[pl.ds(0, 3)], recv.at[1])
-    line[z] = (plane[0] + plane[1]) + (plane[2] + plane[3])
-    for k in range(1, 4):
-        where = (lax.rem(z + k, 4) * 4 + w, sub)
-        remote(line.at[z], line.at[z], send.at[2], recv.at[2], where).start()
-    yield
-    arrived(line.at[pl.ds(0, 3)], recv.at[2])
-    result[...] = (line[0] + line[1]) + (line[2] + line[3])
-    arrived(pair.at[0], send.at[0])
-    arrived(plane.at[pl.ds(0, 3)], send.at[1])
-    arrived(line.at[pl.ds(0, 3)], send.at[2])
+ORDER = (
+    -1, -2, 1, 0, -3, 1, 3, 2, 0, 3, 1, 2, 3, 0, -4, 1, 3, -5, 9, 0, 1, 8, 2, 0,
+    5, 9, 4, 8, 7, 3, 5, 1, 0, 4, 9, -6, 1, 8, 5, 2, 6, 3, 9, 2, 1, 0, 4, 5,
+    -7, -8, 2, 13, 0, 6, 12, 1, 10, 4, 5, 2, 3, 12, 7, 0, 1, 4, 5, 2, 10, 13, 11, 7,
+    5, 12, 3, 1, 2, 9, 13, 5, 4, 7, 0, 10, 9, 4, 12, 6, 5, 4, 13, 0, 12, 11, 3, 8,
+    7, 5, 13, 4, 12, 3, 5, 11, 6, 2, 12, 3, 10, 8, 13, 4, 11, 12, 7, 6, 10, 2, 8, 12,
+    1, 6, 10, 9, 11, 8, 13, 6, 7, 4, 10, 9, 8, 7, 6, 13, 11, 12, 10, 8, 11, 6, 5, 7,
+    9, 8, 11, 6, 12, 9, 10, 7, 10, 13, 8, 11, 9, 9, 2, 0, 11, 11, 6, 1, 13, 4, 7, 9,
+    -9, 10, 13, 3, 12, 8, 6, 8, 7, 11, 6, 10, 2, 13, 12, 0, 10, 4, 13, 11, 7, 3, 5,
+)
+
+
+VM = 42
 
 
 def back_kernel(
     upstream, masked_in, reduced_in, act1_in, spatial_in, act2_in, normed_in, slope_in, mask, stats, sums_in,
     w_reduce, w_spatial, w_expand, norm_reduce, norm_spatial, norm_expand,
-    grad_images, grad_spatial, grad_reduce, grad_expand, grad_norm_reduce, grad_norm_spatial, grad_norm_expand,
-    wr, ws, we, masked, reduced, act1, spatial, act2, big, dsum, dexp, level, wide, shifted, dred,
-    gs, gr, land_s, land_r, land_e, *rest,
+    dsum, gs, gr, big, grad_norm_reduce, grad_norm_spatial, grad_norm_expand,
+    wr, ws, we, masked, reduced, act1, spatial, act2, dexp, level, wide, shifted, dred,
+    land_s, land_r, land_e, *rest,
 ):
     scratches = rest[: len(JOBS)]
-    buf5, buf6, pair, plane, line, load, send, recv, jsend, jrecv, jloc, osem = rest[len(JOBS) :]
+    buf5, buf6, pair, plane, line, load, send, recv, jsend, jrecv, jfree = rest[len(JOBS) :]
     dp, sub, z, q = place()
     me = dp * 2 + sub
     width, inner = wr.shape
@@ -914,63 +973,60 @@
         loads[name].start()
     greet_start()
 
-    @pl.loop(0, width // 512)
-    def _(n):
-        cols = pl.ds(pl.multiple_of(n * 512, 512), 512)
-        up = upstream[:, cols]
-        pair[sub, pl.ds(0, 1), cols] = jnp.sum(up * sums_in[pl.ds(0, 8), cols], axis=0, keepdims=True)
-        pair[sub, pl.ds(1, 1), cols] = jnp.sum(up * sums_in[pl.ds(8, 8), cols], axis=0, keepdims=True)
-
-    wide[pl.ds(0, 8), :] = jnp.zeros((8, inner), f32)
-    wide[pl.ds(ROWS + 8, 8), :] = jnp.zeros((8, inner), f32)
-    for b in range(3):
-        shifted[b, pl.ds(0, 64), :] = jnp.zeros((64, inner), bf16)
-        shifted[b, pl.ds(512, 64), :] = jnp.zeros((64, inner), bf16)
-    greet_wait()
-    third = tree_gen(pair, plane, line, send, recv, grad_norm_expand)
-    next(third)
-    loads["slope"].wait()
-
-    def scale_slope(lo, hi):
-        @pl.loop(lo, hi)
+    def third_norm():
+        @pl.loop(0, width // 512)
+        def _(n):
+            cols = pl.ds(pl.multiple_of(n * 512, 512), 512)
+            up = upstream[:, cols]
+            pair[sub, pl.ds(0, 1), cols] = jnp.sum(up * sums_in[pl.ds(0, 8), cols], axis=0, keepdims=True)
+            pair[sub, pl.ds(1, 1), cols] = jnp.sum(up * sums_in[pl.ds(8, 8), cols], axis=0, keepdims=True)
+
+        wide[pl.ds(0, 8), :] = jnp.zeros((8, inner), f32)
+        wide[pl.ds(ROWS + 8, 8), :] = jnp.zeros((8, inner), f32)
+        shifted[pl.ds(0, 64), :] = jnp.zeros((64, 3 * inner), bf16)
+        shifted[pl.ds(512, 64), :] = jnp.zeros((64, 3 * inner), bf16)
+        greet_wait()
+        third = tree_gen(pair, plane, line, send, recv, grad_norm_expand)
+        next(third)
+        loads["slope"].wait()
+
+        def scale_slope(lo, hi):
+            @pl.loop(lo, hi)
+            def _(n):
+                cols = pl.ds(pl.multiple_of(n * 256, 256), 256)
+                up = upstream[:, cols]
+                for k in range(SLOTS // 8):
+                    rows = pl.ds(64 * k, 64)
+                    value = dsum[rows, cols].reshape(8, 8, 256) * up[None]
+                    dsum[rows, cols] = value.reshape(64, 256)
+
+        parts = width // 256
+        scale_slope(0, parts // 4)
+        next(third)
+        scale_slope(parts // 4, parts * 5 // 8)
+        next(third)
+        scale_slope(parts * 5 // 8, parts)
+        loads["normed"].wait()
+        loads["we"].wait()
+        loads["act2"].wait()
+        next(third, None)
+        share = 1.0 / stats[pl.ds(6, 1), :]
+        plane[0, pl.ds(0, 1), :] = grad_norm_expand[pl.ds(0, 1), :] * share
+        plane[0, pl.ds(1, 1), :] = grad_norm_expand[pl.ds(1, 1), :] * share
+        plane[1, pl.ds(0, 1), :] = norm_expand[pl.ds(0, 1), :] * stats[pl.ds(5, 1), :]
+        first_row = grad_norm_expand[pl.ds(0, 1), :]
+        grad_norm_expand[pl.ds(0, 1), :] = grad_norm_expand[pl.ds(1, 1), :]
+        grad_norm_expand[pl.ds(1, 1), :] = first_row
+
+        @pl.loop(0, width // 256)
         def _(n):
             cols = pl.ds(pl.multiple_of(n * 256, 256), 256)
-            up = upstream[:, cols]
+            total, dot = plane[0, pl.ds(0, 1), cols], plane[0, pl.ds(1, 1), cols]
+            gain = plane[1, pl.ds(0, 1), cols]
             for k in range(SLOTS // 8):
                 rows = pl.ds(64 * k, 64)
-                value = dsum[rows, cols].reshape(8, 8, 256) * up[None]
-                dsum[rows, cols] = value.reshape(64, 256)
-
-    parts = width // 256
-    scale_slope(0, parts // 4)
-    next(third)
-    scale_slope(parts // 4, parts * 5 // 8)
-    next(third)
-    scale_slope(parts * 5 // 8, parts)
-    loads["normed"].wait()
-    loads["we"].wait()
-    loads["act2"].wait()
-    next(third, None)
-    share = 1.0 / stats[pl.ds(6, 1), :]
-    plane[0, pl.ds(0, 1), :] = grad_norm_expand[pl.ds(0, 1), :] * share
-    plane[0, pl.ds(1, 1), :] = grad_norm_expand[pl.ds(1, 1), :] * share
-    plane[1, pl.ds(0, 1), :] = norm_expand[pl.ds(0, 1), :] * stats[pl.ds(5, 1), :]
-    first_row = grad_norm_expand[pl.ds(0, 1), :]
-    grad_norm_expand[pl.ds(0, 1), :] = grad_norm_expand[pl.ds(1, 1), :]
-    grad_norm_expand[pl.ds(1, 1), :] = first_row
-
-    @pl.loop(0, width // 256)
-    def _(n):
-        cols = pl.ds(pl.multiple_of(n * 256, 256), 256)
-        total, dot, gain = plane[0, pl.ds(0, 1), cols], plane[0, pl.ds(1, 1), cols], plane[1, pl.ds(0, 1), cols]
-        for k in range(SLOTS // 8):
-            rows = pl.ds(64 * k, 64)
-            value = dsum[rows, cols] - total - normed[rows, cols] * dot
-            dexp[rows, cols] = (columns_of(mask[rows, :], 256) * (value * gain)).astype(bf16)
-
-
-    small_share = share[:, 0:1]
-    loads["spatial"].wait()
+                value = dsum[rows, cols] - total - normed[rows, cols] * dot
+                dexp[rows, cols] = (columns_of(mask[rows, :], 256) * (value * gain)).astype(bf16)
 
     def slope_pass(values, source, norm, at, buf):
         centre, scale = stats[pl.ds(at, 1), pl.ds(0, inner)], stats[pl.ds(at + 1, 1), pl.ds(0, inner)]
@@ -992,10 +1048,11 @@
 
     def norm_pass(values, source, norm, at, total, grad_norm, store):
         centre, scale = stats[pl.ds(at, 1), pl.ds(0, inner)], stats[pl.ds(at + 1, 1), pl.ds(0, inner)]
+        share = 1.0 / stats[pl.ds(6, 1), pl.ds(0, inner)]
         grad_norm[pl.ds(0, 1), :] = total[1:2]
         grad_norm[pl.ds(1, 1), :] = total[0:1]
         gain = norm[pl.ds(0, 1), :] * scale
-        mean, dot = total[0:1] * small_share, total[1:2] * small_share
+        mean, dot = total[0:1] * share, total[1:2] * share
 
         @pl.loop(0, ROWS // 32)
         def _(k):
@@ -1004,21 +1061,89 @@
             value = values[rows, :] - mean - normal * dot
             store(k, columns_of(mask[rows, :], inner) * (value * gain))
 
-    @pl.loop(0, inner // 256)
-    def _(n):
-        cols = pl.ds(pl.multiple_of(n * 256, 256), 256)
-        level[:, cols] = mm_nt(dexp[...], we[cols, :])
-
-    slope_pass(level, spatial, norm_spatial, 2, buf5)
-    direct_start(buf5, send.at[3], recv.at[3])
-
-    @pl.loop(0, width // 256)
-    def _(n):
-        cols = pl.ds(pl.multiple_of(n * 256, 256), 256)
-        big[:, cols] = mm_tn(act2[...], dexp[:, cols])
+    def expand_weights():
+        @pl.loop(0, width // 256)
+        def _(n):
+            cols = pl.ds(pl.multiple_of(n * 256, 256), 256)
+            big[:, cols] = mm(act2[...], dexp[:, cols])
+
+    def spatial_level():
+        loads["spatial"].wait()
+
+        @pl.loop(0, inner // 256)
+        def _(n):
+            cols = pl.ds(pl.multiple_of(n * 256, 256), 256)
+            level[:, cols] = mm_nt(dexp[...], we[cols, :])
+
+        slope_pass(level, spatial, norm_spatial, 2, buf5)
+        direct_start(buf5, send.at[3], recv.at[3])
+
+    def spatial_norm():
+        total = direct_finish(buf5, send.at[3], recv.at[3])
+
+        def store(k, value):
+            wide[pl.ds(pl.multiple_of(k * 32 + 8, 8), 32), :] = value
+            shifted[pl.ds(pl.multiple_of(k * 32 + 64, 32), 32), pl.ds(inner, inner)] = value.astype(bf16)
+
+        norm_pass(level, spatial, norm_spatial, 2, total, grad_norm_spatial, store)
+
+        @pl.loop(0, ROWS // 32)
+        def _(k):
+            for b in (0, 2):
+                rows = wide[pl.ds(pl.multiple_of(k * 32 + 16 - 8 * b, 8), 32), :]
+                shifted[pl.ds(pl.multiple_of(k * 32 + 64, 32), 32), pl.ds(b * inner, inner)] = rows.astype(bf16)
+
+    def spatial_weights():
+        loads["act1"].wait()
+
+        @pl.loop(0, 9)
+        def _(tap):
+            rows = pl.ds(pl.multiple_of(128 - 64 * (tap // 3), 64), ROWS)
+            right = shifted[rows, pl.ds(pl.multiple_of(lax.rem(tap, 3) * inner, inner), inner)]
+            gs[pl.ds(pl.multiple_of(tap * inner, inner), inner), :] = mm(act1[...], right)
+
+    def reduce_level():
+        loads["ws"].wait()
+        loads["reduced"].wait()
+
+        @pl.loop(0, inner // 256)
+        def _(n):
+            cols = pl.ds(pl.multiple_of(n * 256, 256), 256)
+
+            left = jnp.concatenate([shifted[pl.ds(128 - 64 * a, ROWS), :] for a in range(3)], axis=1)
+            right = [ws[pl.ds(pl.multiple_of(tap * inner + n * 256, 256), 256), :] for tap in range(9)]
+            level[:, cols] = mm_nt(left, jnp.concatenate(right, axis=1))
+
+        slope_pass(level, reduced, norm_reduce, 0, buf6)
+        direct_start(buf6, send.at[4], recv.at[4])
+
+    def reduce_norm():
+        total = direct_finish(buf6, send.at[4], recv.at[4])
+
+        def store(k, value):
+            dred[pl.ds(pl.multiple_of(k * 32, 32), 32), :] = value.astype(bf16)
+
+        norm_pass(level, reduced, norm_reduce, 0, total, grad_norm_reduce, store)
+
+    def reduce_weights():
+        loads["masked"].wait()
+
+        @pl.loop(0, width // 256)
+        def _(n):
+            cols = pl.ds(pl.multiple_of(n * 256, 256), 256)
+            gr[cols, :] = mm_tn(masked[:, cols], dred[...])
+
+    def image_values():
+        loads["wr"].wait()
+
+        @pl.loop(0, width // 256)
+        def _(n):
+            cols = pl.ds(pl.multiple_of(n * 256, 256), 256)
+            value = dsum[:, cols] + mm_nt(dred[...], wr[cols, :])
+            dsum[:, cols] = value * columns_of(mask[...], 256)
+
 
     grads = (gs, gr, big)
-    outs = (grad_spatial, grad_reduce, grad_expand)
     lands = (land_s, land_r, land_e)
 
     def make_job(j):
@@ -1033,109 +1158,26 @@
             rows,
             cut(grads[k], sub * half),
             cut(grads[k], (1 - sub) * half),
-            cut(outs[k], sub * half),
-            cut(outs[k], (1 - sub) * half),
             cut(lands[k], 0),
             scratches[j],
             jsend.at[j],
             jrecv.at[j],
-            jloc.at[j],
+            jfree.at[j],
         ).run()
 
-    live = {}
-
-    def begin(*which):
-        for j in which:
-            live[j] = make_job(j)
-            next(live[j])
-
-    def turn():
-        for j in sorted(live):
-            try:
-                next(live[j])
-            except StopIteration:
-                live.pop(j)
-
-    begin(0, 1)
-    total = direct_finish(buf5, send.at[3], recv.at[3])
-    turn()
-
-    def store_spatial(k, value):
-        wide[pl.ds(pl.multiple_of(k * 32 + 8, 8), 32), :] = value
-        shifted[1, pl.ds(pl.multiple_of(k * 32 + 64, 32), 32), :] = value.astype(bf16)
-
-    norm_pass(level, spatial, norm_spatial, 2, total, grad_norm_spatial, store_spatial)
-
-    @pl.loop(0, ROWS // 32)
-    def _(k):
-        for b in (0, 2):
-            rows = wide[pl.ds(pl.multiple_of(k * 32 + 16 - 8 * b, 8), 32), :]
-            shifted[b, pl.ds(pl.multiple_of(k * 32 + 64, 32), 32), :] = rows.astype(bf16)
-
-    turn()
-    loads["ws"].wait()
-    loads["reduced"].wait()
-    loads["act1"].wait()
-
-    @pl.loop(0, inner // 256)
-    def _(n):
-        cols = pl.ds(pl.multiple_of(n * 256, 256), 256)
-
-        def taps(a, total):
-            for b in range(3):
-                left = shifted[b, pl.ds(128 - 64 * a, ROWS), :]
-                right = ws[pl.ds(pl.multiple_of((a * 3 + b) * inner + n * 256, 256), 256), :]
-                total = total + mm_nt(left, right)
-            return total
-
-        level[:, cols] = taps(0, jnp.zeros((ROWS, 256), f32))
-        level[:, cols] = taps(1, level[:, cols])
-        level[:, cols] = taps(2, level[:, cols])
-
-    turn()
-    slope_pass(level, reduced, norm_reduce, 0, buf6)
-    direct_start(buf6, send.at[4], recv.at[4])
-
-    @pl.loop(0, 9)
-    def _(tap):
-        right = shifted[lax.rem(tap, 3), pl.ds(pl.multiple_of(128 - 64 * (tap // 3), 64), ROWS), :]
-        gs[pl.ds(pl.multiple_of(tap * inner, inner), inner), :] = mm_tn(act1[...], right)
-
-    begin(2, 3, 4, 5)
-    total = direct_finish(buf6, send.at[4], recv.at[4])
-
-    def store_reduce(k, value):
-        dred[pl.ds(pl.multiple_of(k * 32, 32), 32), :] = value.astype(bf16)
-
-    norm_pass(level, reduced, norm_reduce, 0, total, grad_norm_reduce, store_reduce)
-    turn()
-    loads["masked"].wait()
-
-    @pl.loop(0, width // 256)
-    def _(n):
-        cols = pl.ds(pl.multiple_of(n * 256, 256), 256)
-        gr[cols, :] = mm_tn(masked[:, cols], dred[...])
-
-    begin(6, 7)
-    turn()
-    loads["wr"].wait()
-
-    @pl.loop(0, width // 256)
-    def _(n):
-        cols = pl.ds(pl.multiple_of(n * 256, 256), 256)
-        value = dsum[:, cols] + mm_nt(dred[...], wr[cols, :])
-        dsum[:, cols] = value * columns_of(mask[...], 256)
-
-    images_out = [
-        pltpu.make_async_copy(dsum.at[pl.ds(64 * r, 56)], grad_images.at[pl.ds(56 * r, 56)], osem.at[r])
-        for r in range(SIDE)
-    ]
-    for copy in images_out:
-        copy.start()
-    while live:
-        turn()
-    for copy in images_out:
-        copy.wait()
+    steps = (
+        third_norm, expand_weights, spatial_level, spatial_norm, spatial_weights,
+        reduce_level, reduce_norm, reduce_weights, image_values,
+    )
+    jobs = [make_job(j) for j in range(len(JOBS))]
+    for item in ORDER:
+        if item < 0:
+            steps[-1 - item]()
+        else:
+            next(jobs[item], None)
+    for job in jobs:
+        for _ in job:
+            pass
 
 
 def backward(
@@ -1152,34 +1194,30 @@
     return pl.pallas_call(
         back_kernel,
         out_shape=[
-            shape((392, width), f32),
-            shape((9 * inner, inner), f32),
-            shape((width, inner), f32),
-            shape((inner, width), f32),
-            shape((2, inner), f32),
-            shape((2, inner), f32),
-            shape((2, width), f32),
+            pltpu.VMEM((ROWS, width), f32),
+            pltpu.VMEM((9 * inner, inner), f32),
+            pltpu.VMEM((width, inner), f32),
+            pltpu.VMEM((inner, width), f32),
+            pltpu.VMEM((2, inner), f32),
+            pltpu.VMEM((2, inner), f32),
+            pltpu.VMEM((2, width), f32),
         ],
         in_specs=[vmem] + [hbm] * 7 + [vmem] * 3 + [hbm] * 3 + [vmem] * 3,
-        out_specs=[hbm] * 4 + [vmem] * 3,
+        out_specs=[vmem] * 7,
         scratch_shapes=[
             pltpu.VMEM((width, inner), bf16),
             pltpu.VMEM((9 * inner, inner), bf16),
             pltpu.VMEM((inner, width), bf16),
             pltpu.VMEM((ROWS, width), bf16),
             pltpu.VMEM((ROWS, inner), f32),
-            pltpu.VMEM((ROWS, inner), bf16),
+            pltpu.VMEM((inner, ROWS), bf16),
             pltpu.VMEM((ROWS, inner), f32),
-            pltpu.VMEM((ROWS, inner), bf16),
-            pltpu.VMEM((inner, width), f32),
-            pltpu.VMEM((ROWS, width), f32),
+            pltpu.VMEM((inner, ROWS), bf16),
             pltpu.VMEM((ROWS, width), bf16),
             pltpu.VMEM((ROWS, inner), f32),
             pltpu.VMEM((ROWS + 16, inner), f32),
-            pltpu.VMEM((3, ROWS + 128, inner), bf16),
+            pltpu.VMEM((ROWS + 128, 3 * inner), bf16),
             pltpu.VMEM((ROWS, inner), bf16),
-            pltpu.VMEM((9 * inner, inner), f32),
-            pltpu.VMEM((width, inner), f32),
             pltpu.VMEM((9 * inner // 2, inner), f32),
             pltpu.VMEM((width // 2, inner), f32),
             pltpu.VMEM((inner // 2, width), f32),
@@ -1194,16 +1232,110 @@
             pltpu.SemaphoreType.DMA((5,)),
             pltpu.SemaphoreType.DMA((len(JOBS), JOB_SEMS)),
             pltpu.SemaphoreType.DMA((len(JOBS), JOB_SEMS)),
-            pltpu.SemaphoreType.DMA((len(JOBS),)),
-            pltpu.SemaphoreType.DMA((SIDE,)),
+            pltpu.SemaphoreType.REGULAR((len(JOBS),)),
         ],
         compiler_params=pltpu.CompilerParams(
-            collective_id=21, has_side_effects=True, vmem_limit_bytes=63 << 20
+            collective_id=21, has_side_effects=True, vmem_limit_bytes=VM << 20
         ),
     )(
         upstream, masked, reduced, act1, spatial, act2, normed, slope, mask, stats, sums,
         w_reduce, w_spatial, w_expand, norm_reduce, norm_spatial, norm_expand,
     )
+
+
+def finish_kernel(
+    loss, n1, n2, n3, n4, g1, g2, g3, g4, loss_out, o1, o2, o3, o4, h1, h2, h3, h4, sems
+):
+    copies = [
+        pltpu.make_async_copy(g1.at[pl.ds(64 * r, 56)], h1.at[pl.ds(56 * r, 56)], sems.at[r]) for r in range(SIDE)
+    ]
+    for k, (a, b) in enumerate([(g2, h2), (g3, h3), (g4, h4)]):
+        part = a.shape[0] // 4
+        for i in range(4):
+            at = pl.ds(part * i, part)
+            copies.append(pltpu.make_async_copy(a.at[at], b.at[at], sems.at[SIDE + 4 * k + i]))
+    for copy in copies:
+        copy.start()
+    loss_out[...] = loss[pl.ds(0, 1), pl.ds(0, 1)]
+    o1[...] = n1[...]
+    o2[...] = n2[...]
+    o3[...] = n3[...]
+    o4[...] = n4[...]
+    for copy in copies:
+        copy.wait()
+
+
+def finish(loss, norms, grads):
+    width = grads[0].shape[1]
+    hbm = pl.BlockSpec(memory_space=pl.ANY)
+    vmem = pl.BlockSpec(memory_space=pltpu.VMEM)
+    shape = jax.ShapeDtypeStruct
+    return pl.pallas_call(
+        finish_kernel,
+        out_shape=[shape((1, 1), f32)]
+        + [shape(x.shape, f32) for x in norms]
+        + [shape((392, width), f32)]
+        + [shape(x.shape, f32) for x in grads[1:]],
+        in_specs=[vmem] * 9,
+        out_specs=[vmem] * 5 + [hbm] * 4,
+        scratch_shapes=[pltpu.SemaphoreType.DMA((SIDE + 12,))],
+        compiler_params=pltpu.CompilerParams(vmem_limit_bytes=4 << 20),
+    )(loss, *norms, *grads)
+
+
+def project_kernel(
+    pooled_in, dproj, hidden, dcodes, grad_project, grad_code, pooled, terms, result, load, save
+):
+    rows, proj = dproj.shape
+    loads = pltpu.make_async_copy(pooled_in, pooled, load)
+    loads.start()
+    a, b = split(dproj[...])
+    terms[pl.ds(0, rows), :] = a
+    terms[pl.ds(rows, rows), :] = a
+    terms[pl.ds(2 * rows, rows), :] = b
+    loads.wait()
+
+    def block(m):
+        at = pl.ds(pl.multiple_of(m * 256, 256), 256)
+        return pltpu.make_async_copy(result.at[at], grad_project.at[at], save.at[m])
+
+    @pl.loop(0, result.shape[0] // 256)
+    def _(m):
+        at = pl.ds(pl.multiple_of(m * 256, 256), 256)
+        a, b = split(pooled[:, at])
+        left = jnp.concatenate([a, b, a], axis=0)
+        for n in range(proj // 256):
+            cols = pl.ds(256 * n, 256)
+            result[at, cols] = mm_tn(left, terms[:, cols])
+        block(m).start()
+
+    a, b = split(hidden[...])
+    c, d = split(dcodes[...])
+    grad_code[...] = mm_tn(jnp.concatenate([a, b, a], axis=0), jnp.concatenate([c, c, d], axis=0))
+    for m in range(result.shape[0] // 256):
+        block(m).wait()
+
+
+def project_weights(pooled, dproj, hidden, dcodes):
+    rows, width = pooled.shape
+    proj, code = hidden.shape[1], dcodes.shape[1]
+    hbm = pl.BlockSpec(memory_space=pl.ANY)
+    vmem = pl.BlockSpec(memory_space=pltpu.VMEM)
+    shape = jax.ShapeDtypeStruct
+    return pl.pallas_call(
+        project_kernel,
+        out_shape=[shape((width, proj), f32), shape((proj, code), f32)],
+        in_specs=[hbm] + [vmem] * 3,
+        out_specs=[hbm, vmem],
+        scratch_shapes=[
+            pltpu.VMEM((rows, width), f32),
+            pltpu.VMEM((3 * rows, proj), bf16),
+            pltpu.VMEM((width, proj), f32),
+            pltpu.SemaphoreType.DMA,
+            pltpu.SemaphoreType.DMA((width // 256,)),
+        ],
+        compiler_params=pltpu.CompilerParams(vmem_limit_bytes=60 << 20),
+    )(pooled, dproj, hidden, dcodes)
 
 
 def whiten(codes, pairing):
@@ -1556,7 +1688,6 @@
     norm_project,
 ):
     width, inner = w_reduce.shape
-    highest = lax.Precision.HIGHEST
     taps = w_spatial.reshape(9 * inner, inner)
     (
         pooled, hidden, dprojected, dcodes, loss, grad_norm_project, upstream,
@@ -1564,7 +1695,6 @@
     ) = forward(
         jnp.transpose(images, (1, 0, 2)),
         pixel_mask,
-        pairing.reshape(256, 1),
         pairing.reshape(1, 256),
         w_reduce,
         taps,
@@ -1583,8 +1713,15 @@
         upstream, masked, reduced, act1, spatial, act2, normed, slope, mask, stats, sums,
         w_reduce, taps, w_expand, norm_reduce, norm_spatial, norm_expand,
     )
-    grad_project = jnp.dot(pooled.reshape(256, width).T, dprojected, precision=highest)
-    grad_code = jnp.dot(hidden.T, dcodes, precision=highest)
+    grad_project, grad_code = project_weights(pooled.reshape(256, width), dprojected, hidden, dcodes)
+    (
+        loss, grad_norm_reduce, grad_norm_spatial, grad_norm_expand, grad_norm_project,
+        grad_images, grad_spatial, grad_reduce, grad_expand,
+    ) = finish(
+        loss,
+        (grad_norm_reduce, grad_norm_spatial, grad_norm_expand, grad_norm_project),
+        (grad_images, grad_spatial, grad_reduce, grad_expand),
+    )
     return (
         loss[0, 0],
         jnp.transpose(grad_images.reshape(49, 8, width), (1, 0, 2)),

time: 288 us -> 232 us (0.81)
  Pallas kernels: 258 us -> 231 us
  local copies, waits for them, and re-layouts: 16.1 us -> 0.01 us
  matrix products: 13.4 us -> 0 us
    pallas_call x1 -> x3, Pallas kernels: 183 us -> 167 us  [the longest x1 149 us: backward(): pl.pallas_call(back_kernel, out_shape=[pltpu.VMEM((ROWS, width), f32), pl...]
    unnamed x32 -> x4, local copies, waits for them, and re-layouts: 13.4 us -> 0.01 us
    dot_general x2 -> x0, matrix products: 13.4 us -> none  [the longest x1 10.7 us: shards(): jnp.dot(pooled.reshape(256, width).T, dprojected, precision=highest)]
    pallas_call x1, Pallas kernels: 75.2 us -> 64.6 us  [forward(): pl.pallas_call(fwd_kernel, out_shape=[shape((4, 4, 2, 8, width), f32), sh...]
where the time goes in v3:
time: 232 us
  Pallas kernels  231 us (100%)
    pallas_call x1, Pallas kernels, backward(): pl.pallas_call(back_kernel, out_shape=[pltpu.VMEM((ROWS, width), f32), pl...  149 us
    pallas_call x1, Pallas kernels, forward(): pl.pallas_call(fwd_kernel, out_shape=[shape((4, 4, 2, 8, width), f32), sh...  64.6 us
    pallas_call x1, Pallas kernels, project_weights(): pl.pallas_call(project_kernel, out_shape=[shape((width, proj), f32), shap...  9.83 us
    pallas_call x1, Pallas kernels, finish(): pl.pallas_call(finish_kernel, out_shape=[shape((1, 1), f32)] + [shape(x.s...  7.93 us

profile of v3, /device:TPU:0, one launch (start us, length us, event | category | flops | bytes accessed | tf_op | source)
XLA Modules:
  0.0 232.2 jit_solution(17084057134555260605)
XLA Ops:
  0.6 64.6 %shard_map.203 = (f32[4,4,2,8,2048]{4,3,2,1,0:T(8,128)}, f32[256,1024]{1,0:T(8,128)}, f32[256,1024]{1,0:T(8,128)}, f32[256,128]{1,0:T(8,128)}, f32[8,128]{1,0:T(...) custom-call(bf16[49,8,2048]{2,1,0:T(8,128)(2,1)} %bitcast.12, ...), custom_call_target="tpu_custom_call" | custom-call | tf_op jit(solution)/shard_map/pallas_call | solution.py:684
  65.2 0.0 copy-start
  65.3 0.0 copy-start.1
  65.3 149.0 %shard_map.204 = (f32[448,2048]{1,0:T(8,128)S(1)}, f32[4608,512]{1,0:T(8,128)S(1)}, f32[2048,512]{1,0:T(8,128)S(1)}, f32[512,2048]{1,0:T(8,128)S(1)}, f32[2,512]...) custom-call(f32[8,2048]{1,0:T(8,128)} %get-tuple-element.47.upstream, ...), custom_call_target="tpu_custom_call" | custom-call | tf_op jit(solution)/shard_map/pallas_call | solution.py:1194
  214.3 0.0 copy-done
  214.3 0.0 copy-done.1
  214.3 7.9 %shard_map.205 = (f32[1,1]{1,0:T(1,128)}, f32[2,512]{1,0:T(2,128)}, f32[2,512]{1,0:T(2,128)}, f32[2,2048]{1,0:T(2,128)}, f32[2,1024]{1,0:T(2,128)}, /*index=5*/f...) custom-call(f32[8,128]{1,0:T(8,128)S(1)} %copy-done.1, ...), custom_call_target="tpu_custom_call" | custom-call | tf_op jit(solution)/shard_map/pallas_call | solution.py:1273
  222.2 9.8 %shard_map.206 = (f32[2048,1024]{1,0:T(8,128)}, f32[1024,128]{1,0:T(8,128)}) custom-call(f32[256,2048]{1,0:T(8,128)} %bitcast.11, f32[256,1024]{1,0:T(8,128)} %get-tuple-element.72.dproj, f32[256,1024]{1,0:T(8,128)} %get-tuple-element.73.hidden, f32[256,128]{1,0:T(8,128)} %get-tuple-element.74.dcodes), custom_call_target="tpu_custom_call" | custom-call | tf_op jit(solution)/shard_map/pallas_call | solution.py:1325
Async XLA Ops:
  65.2 149.0 %copy-start = (f32[2,1024]{1,0:T(2,128)S(1)}, f32[2,1024]{1,0:T(2,128)}, u32[]{:S(2)}) copy-start(f32[2,1024]{1,0:T(2,128)} %get-tuple-element.61.n4) | copy-start | bytes 24580
  65.3 149.0 %copy-start.1 = (f32[8,128]{1,0:T(8,128)S(1)}, f32[8,128]{1,0:T(8,128)}, u32[]{:S(2)}) copy-start(f32[8,128]{1,0:T(8,128)} %get-tuple-element.46.loss) | copy-start | bytes 12292

commit v4 on v3

--- a/solution.py
+++ b/solution.py
@@ -1,3 +1,4 @@
+import functools
 import jax
 import jax.numpy as jnp
 from jax import lax
@@ -374,22 +375,231 @@
     return jnp.concatenate([mask] * (cols // 128), axis=1)
 
 
-def fwd_kernel(
+def halves(ref, h):
+    cols = ref.shape[1] // 2
+    return ref.at[:, pl.ds(h * cols, cols)]
+
+
+class Job:
+    def __init__(self, ring_first, rows, acc, other, land, scratch, send, recv, free):
+        self.ring_first, self.rows, self.acc, self.other = ring_first, rows, acc, other
+        self.land, self.scratch, self.free = land, scratch, free
+        self.mover = Mover(send, recv)
+        self.taken = 0
+
+    def take(self, rows):
+        ref = rows_at(self.scratch, self.taken, rows)
+        self.taken += rows
+        return ref
+
+    def ring_reduce(self, base, block):
+        dp, sub, z, q = place()
+        go, got = self.mover.go, self.mover.got
+        after_me, before_me = (ring_dp(z, q + 1), sub), (ring_dp(z, q + 3), sub)
+        r0 = self.take(block)
+        r1a, r1b = self.take(block), self.take(block)
+
+        def blk(k):
+            return rows_at(self.land, base + lax.rem(q + k, 4) * block, block)
+
+        go(None, halves(blk(2), 0), halves(r0, 0), 1, 1, after_me)
+        go(None, halves(blk(2), 1), halves(r0, 1), 2, 2, before_me)
+        yield
+        got(None, halves(r0, 0), 1)
+        add_into(halves(blk(1), 0), halves(r0, 0), block)
+        go(None, blk(1), r1a, 3, 3, after_me)
+        got(None, halves(r0, 1), 2)
+        add_into(halves(blk(3), 1), halves(r0, 1), block)
+        go(None, blk(3), r1b, 4, 4, before_me)
+        yield
+        got(None, r1a, 3)
+        got(None, r1b, 4)
+        add_into(blk(0), r1a, block, r1b)
+
+    def line_reduce(self, base, chunk):
+        dp, sub, z, _ = place()
+        go, got = self.mover.go, self.mover.got
+        up, down = (dp + 4, sub), (dp - 4, sub)
+        low = [self.take(chunk) for _ in range(3)]
+        high = [low[0], self.take(chunk), self.take(chunk)]
+
+        def at(j):
+            return rows_at(self.land, base + jnp.clip(j, 0, 3) * chunk, chunk)
+
+        for t in range(3):
+            go(z <= t, at(3 + z - t), low[t], 5 + t, 5 + t, up)
+            go(z >= 3 - t, at(z - 3 + t), high[t], 8 + t, 8 + t, down)
+            yield
+            got(
+                jnp.logical_and(z >= 1, z <= t + 1),
+                low[t],
+                5 + t,
+                lambda: add_into(at(2 + z - t), low[t], chunk),
+            )
+            got(
+                jnp.logical_and(z <= 2, z >= 2 - t),
+                high[t],
+                8 + t,
+                lambda: add_into(at(z - 2 + t), high[t], chunk),
+            )
+
+    def run(self):
+        dp, sub, z, q = place()
+        sib = (dp, 1 - sub)
+        mover, acc, rows = self.mover, self.acc, self.rows
+        mover.go(None, self.other, self.land, 0, 0, sib)
+        yield
+        mover.got(None, self.land, 0)
+        add_into(self.land, acc, rows)
+        big, small = rows // 4, rows // 16
+
+        def hand_over():
+            mover.settle(0)
+            pl.semaphore_signal(self.free, inc=1, device_id=dev(*sib), device_id_type=MESH)
+
+        def total(start):
+            copy_into(rows_at(acc, start, small), rows_at(self.land, start, small), small)
+
+        def share(ref, k):
+            mover.go(None, ref, ref, 21 + k, 21, sib)
+
+        if self.ring_first:
+            yield from self.ring_reduce(0, big)
+            hand_over()
+            yield from self.line_reduce(q * big, small)
+            total(q * big + z * small)
+            at = lambda j: rows_at(acc, q * big + j * small, small)
+            yield from mover.line_gather(at, None, 11)
+            pl.semaphore_wait(self.free, 1)
+            share(rows_at(acc, q * big, big), 3)
+
+            def blk(k, h):
+                ref = rows_at(acc, lax.rem(q + k, 4) * big, big)
+                return ref if h is None else halves(ref, h)
+
+            yield from mover.ring_gather(blk, None, 17, share)
+        else:
+            yield from self.line_reduce(0, big)
+            hand_over()
+            yield from self.ring_reduce(z * big, small)
+            total(z * big + q * small)
+
+            def blk(k, h):
+                ref = rows_at(acc, z * big + lax.rem(q + k, 4) * small, small)
+                return ref if h is None else halves(ref, h)
+
+            yield from mover.ring_gather(blk, None, 17, lambda ref, k: None)
+            pl.semaphore_wait(self.free, 1)
+            share(rows_at(acc, z * big, big), 3)
+            at = lambda j: rows_at(acc, j * big, big)
+            yield from mover.line_gather(at, None, 11)
+            for k in range(1, 4):
+                share(rows_at(acc, lax.rem(z + k, 4) * big, big), k - 1)
+        yield
+        arrived(self.other, mover.recv.at[21])
+        mover.drain()
+
+
+JOB_SEMS = 25
+
+
+def add_into(dst, src, rows, more=None):
+    step = 16 if rows % 16 == 0 else 8
+
+    @pl.loop(0, rows // step)
+    def _(k):
+        at = pl.ds(pl.multiple_of(k * step, 8), step)
+        value = dst[at, :] + src[at, :]
+        dst[at, :] = value if more is None else value + more[at, :]
+
+
+def copy_into(dst, src, rows):
+    @pl.loop(0, rows // 8)
+    def _(k):
+        at = pl.ds(pl.multiple_of(k * 8, 8), 8)
+        dst[at, :] = src[at, :]
+
+
+def rows_at(ref, start, size):
+    return ref.at[pl.ds(pl.multiple_of(start, 8), size)]
+
+
+def landing_rows(ring_first, rows):
+    big, small = rows // 4, rows // 16
+    return 3 * big + 5 * small if ring_first else 3 * small + 5 * big
+
+
+JOBS = (
+    (2, 0, 256, 0, 768, True),
+    (2, 0, 256, 768, 256, False),
+    (2, 0, 256, 1024, 768, True),
+    (2, 0, 256, 1792, 256, False),
+    (0, 0, 384, 0, 512, True),
+    (0, 384, 256, 0, 512, False),
+    (0, 640, 384, 0, 512, True),
+    (0, 1024, 128, 0, 512, False),
+    (0, 1152, 384, 0, 512, True),
+    (0, 1536, 256, 0, 512, False),
+    (0, 1792, 384, 0, 512, True),
+    (0, 2176, 128, 0, 512, False),
+    (1, 0, 384, 0, 512, True),
+    (1, 384, 128, 0, 512, False),
+    (1, 512, 384, 0, 512, True),
+    (1, 896, 128, 0, 512, False),
+)
+
+ORDER = (
+    -1, 1, -2, 1, 2, -3, 2, 1, 0, 3, 0, 3, 1, 2, -4, 3, -5, 7, 5, 10, 8, 3, 0, 7,
+    2, 5, -6, 10, 2, 7, 6, 1, 8, 3, 9, 5, 6, 0, 2, 7, 4, 1, 8, 3, 9, -7, 1, 10,
+    -10, 2, 0, 5, -8, 14, 1, 8, 6, 12, 2, 9, -9, 3, 1, 2, 7, 8, 4, 0, 12, 9, 7, 1,
+    3, 5, 14, 13, 10, -11, 0, 8, 7, 12, 3, -12, 6, 10, 1, 7, 4, 8, 3, 15, -13, 0, 13, 10,
+    8, 6, 9, 2, 7, 5, 10, -14, 3, 12, 15, 13, 6, 9, 0, 14, 7, 10, 2, 4, 12, 5, -15, 15,
+    8, 7, 6, 12, 9, 8, 10, 4, 13, 11, 12, 5, 4, 15, 14, 10, 6, 9, 12, 4, 11, 13, 5, 0,
+    15, 14, 3, -16, 6, 11, 4, 9, 13, 12, 10, 15, 0, 11, 13, 14, 2, 8, 4, 2, 9, 13, 6, 0,
+    13, 11, 14, 15, 5, 4, 9, 11, 1, -17, 8, 14, 15, 13, 1, 12, 0, 11, 15, 6, 14, 3, 5, 11,
+    12, 14, 7, 10, 11, 15, 6, -18, 13, 12, 8, 5, 4, 11, 15, 6, 14, 5, 11, 12, 9, 13, 7, 4,
+    9, 15, 10, 14, 4, 11, 15, 13, 14, 11,
+)
+
+VM = 43
+
+PROJECTOR_ROWS = 12288
+
+
+def step_kernel(
     images, pixel_mask, pair_row, w_reduce, w_spatial, w_expand, w_project, w_code,
     norm_reduce, norm_spatial, norm_expand, norm_project,
-    pooled_out, hidden_out, dprojected_out, dcodes_out, loss_out, grad_norm_out, upstream,
-    masked_out, reduced_out, act1_out, spatial_out, act2_out, normed_out, slope_out, mask, stats, sums_out,
-    img, masked, wr, ws, we, wp, wc, reduced, wide, shifted, spatial, act2, normed, slope, own,
-    own_proj, proj_all, same, totals, act1_turned, act2_turned, level, normal, hidden, dproj, counts,
-    counts_buf, buf1, buf2, pair, plane, line,
-    load, save, send, recv, gsend, grecv, hsend, hrecv,
+    pooled_out, projector, masked_out, loss_out,
+    grad_norm_out, third_grad, grad_norm_reduce, grad_norm_spatial, dsum, gs, gr, big,
+    img, wr, ws, we, wc, masked, reduced, spatial, act1, act2, dred, level, wide, shifted, mask, stats,
+    own, own_proj, proj_all, same, codes_buf, counts, sums, totals, third_sums, upstream,
+    buf1, buf2, buf5, buf6, pair, plane, line, pair4, plane4, line4, land_s, land_r, land_e, *rest,
 ):
+    scratches = rest[: len(JOBS)]
+    load, save, send, recv, gsend, grecv, hsend, hrecv, jsend, jrecv, jfree, wsem = rest[len(JOBS) :]
     dp, sub, z, q = place()
     me = dp * 2 + sub
-    inner = wr.shape[1]
-    width = wr.shape[0]
-    loads = [pltpu.make_async_copy(a, b, load.at[k]) for k, (a, b) in enumerate(
-        [(images, img), (w_reduce, wr), (w_spatial, ws), (w_expand, we), (w_project, wp), (w_code, wc)])]
+    width, inner = wr.shape
+    proj = wc.shape[0]
+    normed = big.at[pl.ds(0, ROWS)]
+    slope, dexp, act2_rows = dsum, masked, dred
+    half_proj = proj // 2
+    loads = [
+        pltpu.make_async_copy(a, b, load.at[k])
+        for k, (a, b) in enumerate(
+            [(images, img), (w_reduce, wr), (w_spatial, ws), (w_expand, we), (w_code, wc)]
+            + [
+                (w_project.at[:, pl.ds(h * half_proj, half_proj)], ws.at[pl.ds(h * width, width)])
+                for h in range(2)
+            ]
+            + [(w_spatial, ws), (masked_out, masked)]
+        )
+    ]
+
+    def block(k, n):
+        start = pl.multiple_of(512 * k + 256 * (n // 2), 256)
+        return gr.at[pl.ds(start, 256), pl.ds(pl.multiple_of(lax.rem(n, 2) * 256, 256), 256)]
+
     loads[0].start()
     loads[1].start()
     greet_start()
@@ -406,11 +616,8 @@
     wide[pl.ds(ROWS + 8, 8), :] = jnp.zeros((8, inner), f32)
     shifted[pl.ds(0, 64), :] = jnp.zeros((64, 3 * inner), bf16)
     shifted[pl.ds(512, 64), :] = jnp.zeros((64, 3 * inner), bf16)
-    greet_wait()
-    counts_buf[me] = counts[...]
-    direct_start(counts_buf, send.at[0], recv.at[0])
     loads[0].wait()
-    for copy in loads[2:]:
+    for copy in loads[2:5]:
         copy.start()
     gap = jnp.zeros((8, 256), f32)
 
@@ -440,11 +647,15 @@
         buf1[me, pl.ds(0, 1), cols] = jnp.sum(got, axis=0, keepdims=True)
         buf1[me, pl.ds(1, 1), cols] = jnp.sum(got * got, axis=0, keepdims=True)
 
+    extra = pl.ds(inner, 128)
+    buf1[me, pl.ds(0, 1), extra] = jnp.sum(counts[...], axis=0, keepdims=True)
+    buf1[me, pl.ds(1, 1), extra] = jnp.zeros((1, 128), f32)
+    greet_wait()
     direct_start(buf1, send.at[1], recv.at[1])
-    keep(reduced, reduced_out)
     pairs = jnp.broadcast_to(pair_row[...].astype(f32), (256, 256))
     same[...] = (pairs == jnp.transpose(pairs)).astype(f32)
-    valid = jnp.sum(direct_finish(counts_buf, send.at[0], recv.at[0]), axis=0, keepdims=True)[:, 0:1]
+    first = direct_finish(buf1, send.at[1], recv.at[1])
+    valid = first[0:1, inner : inner + 1]
     inverse_valid = 1.0 / valid
 
     def moments(total):
@@ -461,7 +672,7 @@
             level = src[rows, :] * gain + bias
             store(k, columns_of(mask[rows, :], inner) * (level * sigmoid(level)))
 
-    centre1, scale1 = moments(direct_finish(buf1, send.at[1], recv.at[1]))
+    centre1, scale1 = moments(first[:, :inner])
     stats[pl.ds(0, 1), pl.ds(0, inner)] = centre1
     stats[pl.ds(1, 1), pl.ds(0, inner)] = scale1
 
@@ -490,16 +701,16 @@
         buf2[me, pl.ds(1, 1), cols] = jnp.sum(got * got, axis=0, keepdims=True)
 
     direct_start(buf2, send.at[2], recv.at[2])
-    keep(spatial, spatial_out)
-    act1_turned[...] = jnp.transpose(wide[pl.ds(8, ROWS), :]).astype(bf16)
-    keep(act1_turned, act1_out)
+    loads[5].start()
+    loads[6].start()
+    act1[...] = jnp.transpose(wide[pl.ds(8, ROWS), :]).astype(bf16)
     centre2, scale2 = moments(direct_finish(buf2, send.at[2], recv.at[2]))
     stats[pl.ds(2, 1), pl.ds(0, inner)] = centre2
     stats[pl.ds(3, 1), pl.ds(0, inner)] = scale2
 
     def store_act2(k, value):
         wide[pl.ds(pl.multiple_of(k * 32 + 8, 8), 32), :] = value
-        act2[pl.ds(pl.multiple_of(k * 32, 32), 32), :] = value.astype(bf16)
+        act2_rows[pl.ds(pl.multiple_of(k * 32, 32), 32), :] = value.astype(bf16)
 
     activate(spatial, norm_spatial, centre2, scale2, store_act2)
     loads[3].wait()
@@ -507,7 +718,7 @@
     @pl.loop(0, width // 256)
     def _(n):
         cols = pl.ds(pl.multiple_of(n * 256, 256), 256)
-        got = mm(act2[...], we[:, cols])
+        got = mm(act2_rows[...], we[:, cols])
         normed[:, cols] = got
         pair[sub, pl.ds(0, 1), cols] = jnp.sum(got, axis=0, keepdims=True)
         pair[sub, pl.ds(1, 1), cols] = jnp.sum(got * got, axis=0, keepdims=True)
@@ -515,8 +726,7 @@
     third = tree_gen(pair, plane, line, send.at[pl.ds(3, 3)], recv.at[pl.ds(3, 3)], totals)
     next(third)
     next(third)
-    act2_turned[...] = jnp.transpose(wide[pl.ds(8, ROWS), :]).astype(bf16)
-    keep(act2_turned, act2_out)
+    act2[...] = jnp.transpose(wide[pl.ds(8, ROWS), :]).astype(bf16)
     next(third)
     next(third, None)
     centre3, scale3 = moments(totals[...])
@@ -555,20 +765,20 @@
                 normed[rows, cols] = n3
                 slope[rows, cols] = slope3
                 s1, s2 = s1 + fold8(slope3), s2 + fold8(slope3 * n3)
-            sums_out[pl.ds(0, 8), cols] = s1
-            sums_out[pl.ds(8, 8), cols] = s2
+            sums[pl.ds(0, 8), cols] = s1
+            sums[pl.ds(8, 8), cols] = s2
 
     rows_all = 256
-    loads[4].wait()
-    loads[5].wait()
+    for k in (4, 5, 6):
+        loads[k].wait()
     high = own[...].astype(bf16).astype(f32)
     both_terms = jnp.concatenate([high, own[...] - high], axis=0).astype(bf16)
-    proj = hidden.shape[1]
 
     @pl.loop(0, proj // 256)
     def _(n):
         cols = pl.ds(pl.multiple_of(n * 256, 256), 256)
-        value = mm(both_terms, wp[:, cols])
+        rows = pl.ds(pl.multiple_of((n // 2) * width, 256), width)
+        value = mm(both_terms, ws[rows, pl.ds(pl.multiple_of(lax.rem(n, 2) * 256, 256), 256)])
         own_proj[:, cols] = value[0:8] + value[8:16]
 
     proj_all[z, lax.rem(dp, 4), sub] = own_proj[...]
@@ -588,14 +798,13 @@
     slopes(3, 6)
     move(proj_movers)
     slopes(6, 8)
-    keep(normed, normed_out)
-    keep(slope, slope_out)
     mine.wait()
     move(proj_movers)
     move(proj_movers)
     move(pool_movers)
 
     share = 1.0 / rows_all
+    codes_buf[...] = jnp.zeros_like(codes_buf)
 
     @pl.loop(0, proj // 256)
     def _(n):
@@ -606,14 +815,15 @@
         scale = lax.rsqrt(square - centre * centre + epsilon)
         normal_here = (value - centre) * scale
         level_here = norm_project[pl.ds(0, 1), cols] * normal_here + norm_project[pl.ds(1, 1), cols]
-        normal[:, cols] = normal_here
-        level[:, cols] = level_here
-        hidden[:, cols] = level_here * sigmoid(level_here)
+        block(1, n)[...] = normal_here
+        block(0, n)[...] = level_here
+        value = level_here * sigmoid(level_here)
+        block(2, n)[...] = value
+        high, low = split(value)
+        codes_buf[...] += mm(high, wc[cols, :]) + mm(low, wc[cols, :])
         upstream[pl.ds(0, 1), cols] = scale * norm_project[pl.ds(0, 1), cols]
 
-    keep(hidden, hidden_out)
-    high, low = split(hidden[...])
-    codes = mm(high, wc[...]) + mm(low, wc[...])
+    codes = codes_buf[...]
 
     centre = jnp.sum(codes, axis=0, keepdims=True) * share
     moved = codes - centre
@@ -634,7 +844,6 @@
     both = half + jnp.transpose(half)
     grad_moved = exact(grad_white - exact(white, both, ((1,), (0,))) * share, inverse, ((1,), (0,)))
     dcodes = grad_moved - jnp.sum(grad_moved, axis=0, keepdims=True) * share
-    dcodes_out[...] = dcodes
 
     move(pool_movers)
     high, low = split(dcodes)
@@ -644,389 +853,84 @@
         cols = pl.ds(pl.multiple_of(n * 256, 256), 256)
         right = wc[cols, :]
         grad = mm_nt(high, right) + mm_nt(low, right)
-        level_here = level[:, cols]
+        level_here = block(0, n)[...]
         sig = sigmoid(level_here)
         grad = grad * (sig * (1.0 + level_here * (1.0 - sig)))
-        normal_here = normal[:, cols]
+        normal_here = block(1, n)[...]
         total = jnp.sum(grad, axis=0, keepdims=True)
         dot = jnp.sum(grad * normal_here, axis=0, keepdims=True)
         grad_norm_out[pl.ds(0, 1), cols] = dot
         grad_norm_out[pl.ds(1, 1), cols] = total
-        dproj[:, cols] = upstream[pl.ds(0, 1), cols] * (grad - (total + normal_here * dot) * share)
-
-    keep(dproj, dprojected_out)
+        block(3, n)[...] = upstream[pl.ds(0, 1), cols] * (grad - (total + normal_here * dot) * share)
+
+    move(pool_movers)
+    own_rows = [gr[pl.ds(pl.multiple_of(1536 + 256 * h + me * 8, 8), 8), :] for h in range(2)]
+    mine = jnp.concatenate(own_rows, axis=1)
+    high = mine.astype(bf16).astype(f32)
+    both_terms = jnp.concatenate([high, mine - high], axis=0).astype(bf16)
+
+    @pl.loop(0, width // 256)
+    def _(n):
+        cols = pl.ds(pl.multiple_of(n * 256, 256), 256)
+        value = mm_nt(both_terms[:, :half_proj], ws[cols, :])
+        value = value + mm_nt(both_terms[:, half_proj:], ws[pl.ds(pl.multiple_of(width + n * 256, 256), 256), :])
+        up = (value[0:8] + value[8:16]) * columns_of(inverse_counts, 256)
+        upstream[:, cols] = up
+        pair4[sub, pl.ds(0, 1), cols] = jnp.sum(up * sums[pl.ds(0, 8), cols], axis=0, keepdims=True)
+        pair4[sub, pl.ds(1, 1), cols] = jnp.sum(up * sums[pl.ds(8, 8), cols], axis=0, keepdims=True)
+
+    loads[7].start()
+    fourth = tree_gen(pair4, plane4, line4, send.at[pl.ds(6, 3)], recv.at[pl.ds(6, 3)], third_sums)
+    next(fourth)
+    code_out = []
+    code_high, code_low = split(dcodes)
+    code_terms = jnp.concatenate([code_high, code_high, code_low], axis=0)
+    for n in range(proj // 256):
+        high, low = split(block(2, n)[...])
+        place_at = codes_buf if n == 2 else same.at[:, pl.ds(128 * (n % 2), 128)]
+        if n == 3:
+            code_out[1].wait()
+        place_at[...] = mm_tn(jnp.concatenate([high, low, high], axis=0), code_terms)
+        code_out.append(pltpu.make_async_copy(place_at, projector.at[pl.ds(width + 256 * n, 256), pl.ds(0, codes_buf.shape[1])], save.at[1 + n]))
+        code_out[n].start()
+    next(fourth)
+    saves.extend(code_out[k] for k in (0, 2, 3))
     for mover in pool_movers:
         for _ in mover:
             pass
-    mine = dproj[pl.ds(pl.multiple_of(me * 8, 8), 8), :]
-    high = mine.astype(bf16).astype(f32)
-    both_terms = jnp.concatenate([high, mine - high], axis=0).astype(bf16)
-
-    @pl.loop(0, width // 256)
-    def _(n):
-        cols = pl.ds(pl.multiple_of(n * 256, 256), 256)
-        value = mm_nt(both_terms, wp[cols, :])
-        upstream[:, cols] = (value[0:8] + value[8:16]) * columns_of(inverse_counts, 256)
-
-    for copy in saves:
-        copy.wait()
-
-
-def forward(
-    images, pixel_mask, pair_row, w_reduce, w_spatial, w_expand, w_project, w_code,
-    norm_reduce, norm_spatial, norm_expand, norm_project,
-):
-    width, inner = w_reduce.shape
-    proj, code = w_code.shape
-    hbm = pl.BlockSpec(memory_space=pl.ANY)
-    vmem = pl.BlockSpec(memory_space=pltpu.VMEM)
-    shape = jax.ShapeDtypeStruct
-    return pl.pallas_call(
-        fwd_kernel,
-        out_shape=[
-            shape((4, 4, 2, 8, width), f32),
-            shape((256, proj), f32),
-            shape((256, proj), f32),
-            shape((256, code), f32),
-            shape((8, 128), f32),
-            shape((2, proj), f32),
-            shape((8, width), f32),
-            shape((ROWS, width), bf16),
-            shape((ROWS, inner), f32),
-            shape((inner, ROWS), bf16),
-            shape((ROWS, inner), f32),
-            shape((inner, ROWS), bf16),
-            shape((ROWS, width), f32),
-            shape((ROWS, width), f32),
-            shape((ROWS, 128), f32),
-            shape((8, width), f32),
-            shape((16, width), f32),
-        ],
-        in_specs=[hbm, vmem, vmem, hbm, hbm, hbm, hbm, hbm, vmem, vmem, vmem, vmem],
-        out_specs=[hbm, hbm, hbm, vmem, vmem, vmem, vmem] + [hbm] * 7 + [vmem] * 3,
-        scratch_shapes=[
-            pltpu.VMEM((49, 8, width), bf16),
-            pltpu.VMEM((ROWS, width), bf16),
-            pltpu.VMEM((width, inner), bf16),
-            pltpu.VMEM((9 * inner, inner), bf16),
-            pltpu.VMEM((inner, width), bf16),
-            pltpu.VMEM((width, proj), bf16),
-            pltpu.VMEM((proj, code), bf16),
-            pltpu.VMEM((ROWS, inner), f32),
-            pltpu.VMEM((ROWS + 16, inner), f32),
-            pltpu.VMEM((ROWS + 128, 3 * inner), bf16),
-            pltpu.VMEM((ROWS, inner), f32),
-            pltpu.VMEM((ROWS, inner), bf16),
-            pltpu.VMEM((ROWS, width), f32),
-            pltpu.VMEM((ROWS, width), f32),
-            pltpu.VMEM((8, width), f32),
-            pltpu.VMEM((8, proj), f32),
-            pltpu.VMEM((4, 4, 2, 8, proj), f32),
-            pltpu.VMEM((256, 256), f32),
-            pltpu.VMEM((2, width), f32),
-            pltpu.VMEM((inner, ROWS), bf16),
-            pltpu.VMEM((inner, ROWS), bf16),
-            pltpu.VMEM((256, proj), f32),
-            pltpu.VMEM((256, proj), f32),
-            pltpu.VMEM((256, proj), f32),
-            pltpu.VMEM((256, proj), f32),
-            pltpu.VMEM((8, 128), f32),
-            pltpu.VMEM((32, 8, 128), f32),
-            pltpu.VMEM((32, 2, inner), f32),
-            pltpu.VMEM((32, 2, inner), f32),
-            pltpu.VMEM((2, 2, width), f32),
-            pltpu.VMEM((4, 2, width), f32),
-            pltpu.VMEM((4, 2, width), f32),
-            pltpu.SemaphoreType.DMA((6,)),
-            pltpu.SemaphoreType.DMA((10,)),
-            pltpu.SemaphoreType.DMA((6,)),
-            pltpu.SemaphoreType.DMA((6,)),
-            pltpu.SemaphoreType.DMA((2, 14)),
-            pltpu.SemaphoreType.DMA((2, 14)),
-            pltpu.SemaphoreType.DMA((2, 14)),
-            pltpu.SemaphoreType.DMA((2, 14)),
-        ],
-        compiler_params=pltpu.CompilerParams(
-            collective_id=20, has_side_effects=True, vmem_limit_bytes=58 << 20
-        ),
-    )(
-        images, pixel_mask, pair_row, w_reduce, w_spatial, w_expand, w_project, w_code,
-        norm_reduce, norm_spatial, norm_expand, norm_project,
-    )
-
-
-def halves(ref, h):
-    cols = ref.shape[1] // 2
-    return ref.at[:, pl.ds(h * cols, cols)]
-
-
-class Job:
-    def __init__(self, ring_first, rows, acc, other, land, scratch, send, recv, free):
-        self.ring_first, self.rows, self.acc, self.other = ring_first, rows, acc, other
-        self.land, self.scratch, self.free = land, scratch, free
-        self.mover = Mover(send, recv)
-        self.taken = 0
-
-    def take(self, rows):
-        ref = rows_at(self.scratch, self.taken, rows)
-        self.taken += rows
-        return ref
-
-    def ring_reduce(self, base, block):
-        dp, sub, z, q = place()
-        go, got = self.mover.go, self.mover.got
-        after_me, before_me = (ring_dp(z, q + 1), sub), (ring_dp(z, q + 3), sub)
-        r0 = self.take(block)
-        r1a, r1b = self.take(block), self.take(block)
-
-        def blk(k):
-            return rows_at(self.land, base + lax.rem(q + k, 4) * block, block)
-
-        go(None, halves(blk(2), 0), halves(r0, 0), 1, 1, after_me)
-        go(None, halves(blk(2), 1), halves(r0, 1), 2, 2, before_me)
-        yield
-        got(None, halves(r0, 0), 1)
-        add_into(halves(blk(1), 0), halves(r0, 0), block)
-        go(None, blk(1), r1a, 3, 3, after_me)
-        got(None, halves(r0, 1), 2)
-        add_into(halves(blk(3), 1), halves(r0, 1), block)
-        go(None, blk(3), r1b, 4, 4, before_me)
-        yield
-        got(None, r1a, 3)
-        got(None, r1b, 4)
-        add_into(blk(0), r1a, block, r1b)
-
-    def line_reduce(self, base, chunk):
-        dp, sub, z, _ = place()
-        go, got = self.mover.go, self.mover.got
-        up, down = (dp + 4, sub), (dp - 4, sub)
-        low = [self.take(chunk) for _ in range(3)]
-        high = [self.take(chunk) for _ in range(3)]
-
-        def at(j):
-            return rows_at(self.land, base + jnp.clip(j, 0, 3) * chunk, chunk)
-
-        for t in range(3):
-            go(z <= t, at(3 + z - t), low[t], 5 + t, 5 + t, up)
-            go(z >= 3 - t, at(z - 3 + t), high[t], 8 + t, 8 + t, down)
-            yield
-            got(
-                jnp.logical_and(z >= 1, z <= t + 1),
-                low[t],
-                5 + t,
-                lambda: add_into(at(2 + z - t), low[t], chunk),
-            )
-            got(
-                jnp.logical_and(z <= 2, z >= 2 - t),
-                high[t],
-                8 + t,
-                lambda: add_into(at(z - 2 + t), high[t], chunk),
-            )
-
-    def run(self):
-        dp, sub, z, q = place()
-        sib = (dp, 1 - sub)
-        mover, acc, rows = self.mover, self.acc, self.rows
-        mover.go(None, self.other, self.land, 0, 0, sib)
-        yield
-        mover.got(None, self.land, 0)
-        add_into(self.land, acc, rows)
-        big, small = rows // 4, rows // 16
-
-        def hand_over():
-            mover.settle(0)
-            pl.semaphore_signal(self.free, inc=1, device_id=dev(*sib), device_id_type=MESH)
-
-        def total(start):
-            copy_into(rows_at(acc, start, small), rows_at(self.land, start, small), small)
-
-        def share(ref, k):
-            mover.go(None, ref, ref, 21 + k, 21, sib)
-
-        if self.ring_first:
-            yield from self.ring_reduce(0, big)
-            hand_over()
-            yield from self.line_reduce(q * big, small)
-            total(q * big + z * small)
-            at = lambda j: rows_at(acc, q * big + j * small, small)
-            yield from mover.line_gather(at, None, 11)
-            pl.semaphore_wait(self.free, 1)
-            share(rows_at(acc, q * big, big), 3)
-
-            def blk(k, h):
-                ref = rows_at(acc, lax.rem(q + k, 4) * big, big)
-                return ref if h is None else halves(ref, h)
-
-            yield from mover.ring_gather(blk, None, 17, share)
-        else:
-            yield from self.line_reduce(0, big)
-            hand_over()
-            yield from self.ring_reduce(z * big, small)
-            total(z * big + q * small)
-
-            def blk(k, h):
-                ref = rows_at(acc, z * big + lax.rem(q + k, 4) * small, small)
-                return ref if h is None else halves(ref, h)
-
-            yield from mover.ring_gather(blk, None, 17, lambda ref, k: None)
-            pl.semaphore_wait(self.free, 1)
-            share(rows_at(acc, z * big, big), 3)
-            at = lambda j: rows_at(acc, j * big, big)
-            yield from mover.line_gather(at, None, 11)
-            for k in range(1, 4):
-                share(rows_at(acc, lax.rem(z + k, 4) * big, big), k - 1)
-        yield
-        arrived(self.other, mover.recv.at[21])
-        mover.drain()
-
-
-JOB_SEMS = 25
-
-
-def add_into(dst, src, rows, more=None):
-    step = 16 if rows % 16 == 0 else 8
-
-    @pl.loop(0, rows // step)
-    def _(k):
-        at = pl.ds(pl.multiple_of(k * step, 8), step)
-        value = dst[at, :] + src[at, :]
-        dst[at, :] = value if more is None else value + more[at, :]
-
-
-def copy_into(dst, src, rows):
-    @pl.loop(0, rows // 8)
-    def _(k):
-        at = pl.ds(pl.multiple_of(k * 8, 8), 8)
-        dst[at, :] = src[at, :]
-
-
-def rows_at(ref, start, size):
-    return ref.at[pl.ds(pl.multiple_of(start, 8), size)]
-
-
-def landing_rows(ring_first, rows):
-    big, small = rows // 4, rows // 16
-    return 3 * big + 6 * small if ring_first else 3 * small + 6 * big
-
-
-JOBS = (
-    (2, 0, 256, 0, 768, True),
-    (2, 0, 256, 768, 256, False),
-    (2, 0, 256, 1024, 768, True),
-    (2, 0, 256, 1792, 256, False),
-    (0, 0, 512, 0, 512, True),
-    (0, 512, 256, 0, 512, False),
-    (0, 768, 512, 0, 512, True),
-    (0, 1280, 256, 0, 512, False),
-    (0, 1536, 512, 0, 512, True),
-    (0, 2048, 256, 0, 512, False),
-    (1, 0, 384, 0, 512, True),
-    (1, 384, 128, 0, 512, False),
-    (1, 512, 384, 0, 512, True),
-    (1, 896, 128, 0, 512, False),
-)
-
-ORDER = (
-    -1, -2, 1, 0, -3, 1, 3, 2, 0, 3, 1, 2, 3, 0, -4, 1, 3, -5, 9, 0, 1, 8, 2, 0,
-    5, 9, 4, 8, 7, 3, 5, 1, 0, 4, 9, -6, 1, 8, 5, 2, 6, 3, 9, 2, 1, 0, 4, 5,
-    -7, -8, 2, 13, 0, 6, 12, 1, 10, 4, 5, 2, 3, 12, 7, 0, 1, 4, 5, 2, 10, 13, 11, 7,
-    5, 12, 3, 1, 2, 9, 13, 5, 4, 7, 0, 10, 9, 4, 12, 6, 5, 4, 13, 0, 12, 11, 3, 8,
-    7, 5, 13, 4, 12, 3, 5, 11, 6, 2, 12, 3, 10, 8, 13, 4, 11, 12, 7, 6, 10, 2, 8, 12,
-    1, 6, 10, 9, 11, 8, 13, 6, 7, 4, 10, 9, 8, 7, 6, 13, 11, 12, 10, 8, 11, 6, 5, 7,
-    9, 8, 11, 6, 12, 9, 10, 7, 10, 13, 8, 11, 9, 9, 2, 0, 11, 11, 6, 1, 13, 4, 7, 9,
-    -9, 10, 13, 3, 12, 8, 6, 8, 7, 11, 6, 10, 2, 13, 12, 0, 10, 4, 13, 11, 7, 3, 5,
-)
-
-
-VM = 42
-
-
-def back_kernel(
-    upstream, masked_in, reduced_in, act1_in, spatial_in, act2_in, normed_in, slope_in, mask, stats, sums_in,
-    w_reduce, w_spatial, w_expand, norm_reduce, norm_spatial, norm_expand,
-    dsum, gs, gr, big, grad_norm_reduce, grad_norm_spatial, grad_norm_expand,
-    wr, ws, we, masked, reduced, act1, spatial, act2, dexp, level, wide, shifted, dred,
-    land_s, land_r, land_e, *rest,
-):
-    scratches = rest[: len(JOBS)]
-    buf5, buf6, pair, plane, line, load, send, recv, jsend, jrecv, jfree = rest[len(JOBS) :]
-    dp, sub, z, q = place()
-    me = dp * 2 + sub
-    width, inner = wr.shape
-    normed = big.at[pl.ds(0, ROWS)]
-    loads = {}
-    for k, (name, a, b) in enumerate(
-        [
-            ("slope", slope_in, dsum),
-            ("normed", normed_in, normed),
-            ("we", w_expand, we),
-            ("act2", act2_in, act2),
-            ("spatial", spatial_in, spatial),
-            ("ws", w_spatial, ws),
-            ("act1", act1_in, act1),
-            ("reduced", reduced_in, reduced),
-            ("masked", masked_in, masked),
-            ("wr", w_reduce, wr),
-        ]
-    ):
-        loads[name] = pltpu.make_async_copy(a, b, load.at[k])
-        loads[name].start()
-    greet_start()
-
-    def third_norm():
-        @pl.loop(0, width // 512)
-        def _(n):
-            cols = pl.ds(pl.multiple_of(n * 512, 512), 512)
-            up = upstream[:, cols]
-            pair[sub, pl.ds(0, 1), cols] = jnp.sum(up * sums_in[pl.ds(0, 8), cols], axis=0, keepdims=True)
-            pair[sub, pl.ds(1, 1), cols] = jnp.sum(up * sums_in[pl.ds(8, 8), cols], axis=0, keepdims=True)
-
-        wide[pl.ds(0, 8), :] = jnp.zeros((8, inner), f32)
-        wide[pl.ds(ROWS + 8, 8), :] = jnp.zeros((8, inner), f32)
-        shifted[pl.ds(0, 64), :] = jnp.zeros((64, 3 * inner), bf16)
-        shifted[pl.ds(512, 64), :] = jnp.zeros((64, 3 * inner), bf16)
-        greet_wait()
-        third = tree_gen(pair, plane, line, send, recv, grad_norm_expand)
-        next(third)
-        loads["slope"].wait()
-
-        def scale_slope(lo, hi):
-            @pl.loop(lo, hi)
-            def _(n):
-                cols = pl.ds(pl.multiple_of(n * 256, 256), 256)
-                up = upstream[:, cols]
-                for k in range(SLOTS // 8):
-                    rows = pl.ds(64 * k, 64)
-                    value = dsum[rows, cols].reshape(8, 8, 256) * up[None]
-                    dsum[rows, cols] = value.reshape(64, 256)
-
-        parts = width // 256
-        scale_slope(0, parts // 4)
-        next(third)
-        scale_slope(parts // 4, parts * 5 // 8)
-        next(third)
-        scale_slope(parts * 5 // 8, parts)
-        loads["normed"].wait()
-        loads["we"].wait()
-        loads["act2"].wait()
-        next(third, None)
-        share = 1.0 / stats[pl.ds(6, 1), :]
-        plane[0, pl.ds(0, 1), :] = grad_norm_expand[pl.ds(0, 1), :] * share
-        plane[0, pl.ds(1, 1), :] = grad_norm_expand[pl.ds(1, 1), :] * share
-        plane[1, pl.ds(0, 1), :] = norm_expand[pl.ds(0, 1), :] * stats[pl.ds(5, 1), :]
-        first_row = grad_norm_expand[pl.ds(0, 1), :]
-        grad_norm_expand[pl.ds(0, 1), :] = grad_norm_expand[pl.ds(1, 1), :]
-        grad_norm_expand[pl.ds(1, 1), :] = first_row
-
-        @pl.loop(0, width // 256)
+    next(fourth)
+    next(fourth, None)
+    third_grad[pl.ds(0, 1), :] = third_sums[pl.ds(1, 1), :]
+    third_grad[pl.ds(1, 1), :] = third_sums[pl.ds(0, 1), :]
+
+
+    def third_part(lo, hi):
+        @pl.loop(lo, hi)
         def _(n):
             cols = pl.ds(pl.multiple_of(n * 256, 256), 256)
-            total, dot = plane[0, pl.ds(0, 1), cols], plane[0, pl.ds(1, 1), cols]
-            gain = plane[1, pl.ds(0, 1), cols]
-            for k in range(SLOTS // 8):
+            share = 1.0 / stats[pl.ds(6, 1), cols]
+            total, dot = third_sums[pl.ds(0, 1), cols] * share, third_sums[pl.ds(1, 1), cols] * share
+            gain = norm_expand[pl.ds(0, 1), cols] * stats[pl.ds(5, 1), cols]
+            up = upstream[:, cols]
+            for k in range(SIDE):
                 rows = pl.ds(64 * k, 64)
-                value = dsum[rows, cols] - total - normed[rows, cols] * dot
-                dexp[rows, cols] = (columns_of(mask[rows, :], 256) * (value * gain)).astype(bf16)
+                value = (dsum[rows, cols].reshape(8, 8, 256) * up[None]).reshape(64, 256)
+                dsum[rows, cols] = value
+                value = (value - total - normed[rows, cols] * dot) * gain
+                dexp[rows, cols] = (columns_of(mask[rows, :], 256) * value).astype(bf16)
+
+        @pl.loop(lo, hi)
+        def _(n):
+            cols = pl.ds(pl.multiple_of(n * 256, 256), 256)
+            big[:, cols] = mm(act2[...], dexp[:, cols])
+
+    def third_norm():
+        for copy in saves:
+            copy.wait()
+        third_part(0, width // 512)
+
+    def third_rest():
+        third_part(width // 512, width // 256)
 
     def slope_pass(values, source, norm, at, buf):
         centre, scale = stats[pl.ds(at, 1), pl.ds(0, inner)], stats[pl.ds(at + 1, 1), pl.ds(0, inner)]
@@ -1061,25 +965,19 @@
             value = values[rows, :] - mean - normal * dot
             store(k, columns_of(mask[rows, :], inner) * (value * gain))
 
-    def expand_weights():
-        @pl.loop(0, width // 256)
-        def _(n):
-            cols = pl.ds(pl.multiple_of(n * 256, 256), 256)
-            big[:, cols] = mm(act2[...], dexp[:, cols])
-
     def spatial_level():
-        loads["spatial"].wait()
 
         @pl.loop(0, inner // 256)
         def _(n):
             cols = pl.ds(pl.multiple_of(n * 256, 256), 256)
             level[:, cols] = mm_nt(dexp[...], we[cols, :])
 
+        loads[8].start()
         slope_pass(level, spatial, norm_spatial, 2, buf5)
-        direct_start(buf5, send.at[3], recv.at[3])
+        direct_start(buf5, send.at[9], recv.at[9])
 
     def spatial_norm():
-        total = direct_finish(buf5, send.at[3], recv.at[3])
+        total = direct_finish(buf5, send.at[9], recv.at[9])
 
         def store(k, value):
             wide[pl.ds(pl.multiple_of(k * 32 + 8, 8), 32), :] = value
@@ -1094,8 +992,6 @@
                 shifted[pl.ds(pl.multiple_of(k * 32 + 64, 32), 32), pl.ds(b * inner, inner)] = rows.astype(bf16)
 
     def spatial_weights():
-        loads["act1"].wait()
-
         @pl.loop(0, 9)
         def _(tap):
             rows = pl.ds(pl.multiple_of(128 - 64 * (tap // 3), 64), ROWS)
@@ -1103,8 +999,7 @@
             gs[pl.ds(pl.multiple_of(tap * inner, inner), inner), :] = mm(act1[...], right)
 
     def reduce_level():
-        loads["ws"].wait()
-        loads["reduced"].wait()
+        loads[7].wait()
 
         @pl.loop(0, inner // 256)
         def _(n):
@@ -1115,10 +1010,10 @@
             level[:, cols] = mm_nt(left, jnp.concatenate(right, axis=1))
 
         slope_pass(level, reduced, norm_reduce, 0, buf6)
-        direct_start(buf6, send.at[4], recv.at[4])
+        direct_start(buf6, send.at[10], recv.at[10])
 
     def reduce_norm():
-        total = direct_finish(buf6, send.at[4], recv.at[4])
+        total = direct_finish(buf6, send.at[10], recv.at[10])
 
         def store(k, value):
             dred[pl.ds(pl.multiple_of(k * 32, 32), 32), :] = value.astype(bf16)
@@ -1126,7 +1021,7 @@
         norm_pass(level, reduced, norm_reduce, 0, total, grad_norm_reduce, store)
 
     def reduce_weights():
-        loads["masked"].wait()
+        loads[8].wait()
 
         @pl.loop(0, width // 256)
         def _(n):
@@ -1134,14 +1029,47 @@
             gr[cols, :] = mm_tn(masked[:, cols], dred[...])
 
     def image_values():
-        loads["wr"].wait()
-
         @pl.loop(0, width // 256)
         def _(n):
             cols = pl.ds(pl.multiple_of(n * 256, 256), 256)
             value = dsum[:, cols] + mm_nt(dred[...], wr[cols, :])
             dsum[:, cols] = value * columns_of(mask[...], 256)
 
+
+    def pooled_part(h):
+        cols = pl.ds(h * half_proj * 2, half_proj * 2)
+        return pltpu.make_async_copy(pooled_out.at[:, :, :, :, cols], proj_all, load.at[9 + h])
+
+    def project_terms():
+        pooled_part(0).start()
+        for h in range(2):
+            high, low = split(gr[pl.ds(1536 + 256 * h, 256), :])
+            for k, part in enumerate((high, high, low)):
+                ws[pl.ds(768 * h + 256 * k, 256), :] = part
+
+    project_out = []
+
+    def project_block(m):
+        spare = ((level, 0), (reduced, 0)) if m % 2 == 0 else ((spatial, 0), (wide, 8))
+        if m == 0:
+            pooled_part(0).wait()
+        if m == 4:
+            pooled_part(1).start()
+            pooled_part(1).wait()
+        for copy in project_out[2 * m - 4 : 2 * m - 2] if m >= 2 else []:
+            copy.wait()
+        block_rows = proj_all[:, :, :, :, pl.ds(256 * (m % 4), 256)].reshape(256, 256)
+        high, low = split(jnp.transpose(block_rows))
+        left = jnp.concatenate([high, low, high], axis=1)
+        for h, (ref, start) in enumerate(spare):
+            ref[pl.ds(start, 256), :] = mm(left, ws[pl.ds(768 * h, 768), :])
+            copy = pltpu.make_async_copy(
+                ref.at[pl.ds(start, 256)],
+                projector.at[pl.ds(256 * m, 256), pl.ds(512 * h, 512)],
+                wsem.at[m, h],
+            )
+            copy.start()
+            project_out.append(copy)
 
     grads = (gs, gr, big)
     lands = (land_s, land_r, land_e)
@@ -1166,8 +1094,9 @@
         ).run()
 
     steps = (
-        third_norm, expand_weights, spatial_level, spatial_norm, spatial_weights,
-        reduce_level, reduce_norm, reduce_weights, image_values,
+        third_norm, third_rest, spatial_level, spatial_norm, spatial_weights,
+        reduce_level, reduce_norm, reduce_weights, image_values, project_terms,
+        *[functools.partial(project_block, m) for m in range(8)],
     )
     jobs = [make_job(j) for j in range(len(JOBS))]
     for item in ORDER:
@@ -1178,13 +1107,16 @@
     for job in jobs:
         for _ in job:
             pass
-
-
-def backward(
-    upstream, masked, reduced, act1, spatial, act2, normed, slope, mask, stats, sums,
-    w_reduce, w_spatial, w_expand, norm_reduce, norm_spatial, norm_expand,
+    for copy in project_out[-4:]:
+        copy.wait()
+
+
+def training_step(
+    images, pixel_mask, pair_row, w_reduce, w_spatial, w_expand, w_project, w_code,
+    norm_reduce, norm_spatial, norm_expand, norm_project,
 ):
     width, inner = w_reduce.shape
+    proj, code = w_code.shape
     hbm = pl.BlockSpec(memory_space=pl.ANY)
     vmem = pl.BlockSpec(memory_space=pltpu.VMEM)
     shape = jax.ShapeDtypeStruct
@@ -1192,68 +1124,124 @@
         pltpu.VMEM((landing_rows(ring_first, rows), cols), f32) for _, _, rows, _, cols, ring_first in JOBS
     ]
     return pl.pallas_call(
-        back_kernel,
+        step_kernel,
         out_shape=[
+            shape((4, 4, 2, 8, width), f32),
+            shape((PROJECTOR_ROWS, proj), f32),
+            shape((ROWS, width), bf16),
+            pltpu.VMEM((8, 128), f32),
+            pltpu.VMEM((2, proj), f32),
+            pltpu.VMEM((2, width), f32),
+            pltpu.VMEM((2, inner), f32),
+            pltpu.VMEM((2, inner), f32),
             pltpu.VMEM((ROWS, width), f32),
             pltpu.VMEM((9 * inner, inner), f32),
             pltpu.VMEM((width, inner), f32),
             pltpu.VMEM((inner, width), f32),
-            pltpu.VMEM((2, inner), f32),
-            pltpu.VMEM((2, inner), f32),
-            pltpu.VMEM((2, width), f32),
         ],
-        in_specs=[vmem] + [hbm] * 7 + [vmem] * 3 + [hbm] * 3 + [vmem] * 3,
-        out_specs=[vmem] * 7,
+        in_specs=[hbm, vmem, vmem] + [hbm] * 5 + [vmem] * 4,
+        out_specs=[hbm] * 3 + [vmem] * 9,
         scratch_shapes=[
+            pltpu.VMEM((49, 8, width), bf16),
             pltpu.VMEM((width, inner), bf16),
             pltpu.VMEM((9 * inner, inner), bf16),
             pltpu.VMEM((inner, width), bf16),
+            pltpu.VMEM((proj, code), bf16),
             pltpu.VMEM((ROWS, width), bf16),
             pltpu.VMEM((ROWS, inner), f32),
-            pltpu.VMEM((inner, ROWS), bf16),
             pltpu.VMEM((ROWS, inner), f32),
             pltpu.VMEM((inner, ROWS), bf16),
-            pltpu.VMEM((ROWS, width), bf16),
+            pltpu.VMEM((inner, ROWS), bf16),
+            pltpu.VMEM((ROWS, inner), bf16),
             pltpu.VMEM((ROWS, inner), f32),
             pltpu.VMEM((ROWS + 16, inner), f32),
             pltpu.VMEM((ROWS + 128, 3 * inner), bf16),
-            pltpu.VMEM((ROWS, inner), bf16),
-            pltpu.VMEM((9 * inner // 2, inner), f32),
-            pltpu.VMEM((width // 2, inner), f32),
-            pltpu.VMEM((inner // 2, width), f32),
-            *landings,
+            pltpu.VMEM((ROWS, 128), f32),
+            pltpu.VMEM((8, width), f32),
+            pltpu.VMEM((8, width), f32),
+            pltpu.VMEM((8, proj), f32),
+            pltpu.VMEM((4, 4, 2, 8, proj), f32),
+            pltpu.VMEM((256, 256), f32),
+            pltpu.VMEM((256, code), f32),
+            pltpu.VMEM((8, 128), f32),
+            pltpu.VMEM((16, width), f32),
+            pltpu.VMEM((2, width), f32),
+            pltpu.VMEM((2, width), f32),
+            pltpu.VMEM((8, width), f32),
+            pltpu.VMEM((32, 2, inner + 128), f32),
+            pltpu.VMEM((32, 2, inner), f32),
             pltpu.VMEM((32, 2, inner), f32),
             pltpu.VMEM((32, 2, inner), f32),
             pltpu.VMEM((2, 2, width), f32),
             pltpu.VMEM((4, 2, width), f32),
             pltpu.VMEM((4, 2, width), f32),
-            pltpu.SemaphoreType.DMA((10,)),
-            pltpu.SemaphoreType.DMA((5,)),
-            pltpu.SemaphoreType.DMA((5,)),
+            pltpu.VMEM((2, 2, width), f32),
+            pltpu.VMEM((4, 2, width), f32),
+            pltpu.VMEM((4, 2, width), f32),
+            pltpu.VMEM((9 * inner // 2, inner), f32),
+            pltpu.VMEM((width // 2, inner), f32),
+            pltpu.VMEM((inner // 2, width), f32),
+            *landings,
+            pltpu.SemaphoreType.DMA((11,)),
+            pltpu.SemaphoreType.DMA((6,)),
+            pltpu.SemaphoreType.DMA((11,)),
+            pltpu.SemaphoreType.DMA((11,)),
+            pltpu.SemaphoreType.DMA((2, 14)),
+            pltpu.SemaphoreType.DMA((2, 14)),
+            pltpu.SemaphoreType.DMA((2, 14)),
+            pltpu.SemaphoreType.DMA((2, 14)),
             pltpu.SemaphoreType.DMA((len(JOBS), JOB_SEMS)),
             pltpu.SemaphoreType.DMA((len(JOBS), JOB_SEMS)),
             pltpu.SemaphoreType.REGULAR((len(JOBS),)),
+            pltpu.SemaphoreType.DMA((8, 2)),
         ],
         compiler_params=pltpu.CompilerParams(
-            collective_id=21, has_side_effects=True, vmem_limit_bytes=VM << 20
+            collective_id=20, has_side_effects=True, vmem_limit_bytes=VM << 20
         ),
     )(
-        upstream, masked, reduced, act1, spatial, act2, normed, slope, mask, stats, sums,
-        w_reduce, w_spatial, w_expand, norm_reduce, norm_spatial, norm_expand,
-    )
+        images, pixel_mask, pair_row, w_reduce, w_spatial, w_expand, w_project, w_code,
+        norm_reduce, norm_spatial, norm_expand, norm_project,
+    )
+
+
+PARTS = 2
 
 
 def finish_kernel(
-    loss, n1, n2, n3, n4, g1, g2, g3, g4, loss_out, o1, o2, o3, o4, h1, h2, h3, h4, sems
+    projector, loss, n1, n2, n3, n4, g1, g2, g3, g4,
+    project_out, code_out, loss_out, o1, o2, o3, o4, h1, h2, h3, h4,
+    held, held_code, sems, load, save,
 ):
+    steps = held.shape[0] // 256
+
+    def through(m):
+        at = pl.ds(256 * m, 256)
+        return (
+            pltpu.make_async_copy(projector.at[at], held.at[at], load.at[m]),
+            pltpu.make_async_copy(held.at[at], project_out.at[at], save.at[m]),
+        )
+
+    pairs = [through(m) for m in range(steps)]
+    pairs.append(
+        (
+            pltpu.make_async_copy(
+                projector.at[pl.ds(held.shape[0], held_code.shape[0]), pl.ds(0, held_code.shape[1])],
+                held_code,
+                load.at[steps],
+            ),
+            pltpu.make_async_copy(held_code, code_out, save.at[steps]),
+        )
+    )
+    for read, _ in pairs:
+        read.start()
     copies = [
         pltpu.make_async_copy(g1.at[pl.ds(64 * r, 56)], h1.at[pl.ds(56 * r, 56)], sems.at[r]) for r in range(SIDE)
     ]
     for k, (a, b) in enumerate([(g2, h2), (g3, h3), (g4, h4)]):
-        part = a.shape[0] // 4
-        for i in range(4):
+        part = a.shape[0] // PARTS
+        for i in range(PARTS):
             at = pl.ds(part * i, part)
-            copies.append(pltpu.make_async_copy(a.at[at], b.at[at], sems.at[SIDE + 4 * k + i]))
+            copies.append(pltpu.make_async_copy(a.at[at], b.at[at], sems.at[SIDE + PARTS * k + i]))
     for copy in copies:
         copy.start()
     loss_out[...] = loss[pl.ds(0, 1), pl.ds(0, 1)]
@@ -1261,81 +1249,37 @@
     o2[...] = n2[...]
     o3[...] = n3[...]
     o4[...] = n4[...]
+    for read, write in pairs:
+        read.wait()
+        write.start()
+    for _, write in pairs:
+        write.wait()
     for copy in copies:
         copy.wait()
 
 
-def finish(loss, norms, grads):
+def finish(projector, project, code, loss, norms, grads):
     width = grads[0].shape[1]
     hbm = pl.BlockSpec(memory_space=pl.ANY)
     vmem = pl.BlockSpec(memory_space=pltpu.VMEM)
     shape = jax.ShapeDtypeStruct
     return pl.pallas_call(
         finish_kernel,
-        out_shape=[shape((1, 1), f32)]
+        out_shape=[shape(project, f32), shape(code, f32), shape((1, 1), f32)]
         + [shape(x.shape, f32) for x in norms]
         + [shape((392, width), f32)]
         + [shape(x.shape, f32) for x in grads[1:]],
-        in_specs=[vmem] * 9,
-        out_specs=[vmem] * 5 + [hbm] * 4,
-        scratch_shapes=[pltpu.SemaphoreType.DMA((SIDE + 12,))],
-        compiler_params=pltpu.CompilerParams(vmem_limit_bytes=4 << 20),
-    )(loss, *norms, *grads)
-
-
-def project_kernel(
-    pooled_in, dproj, hidden, dcodes, grad_project, grad_code, pooled, terms, result, load, save
-):
-    rows, proj = dproj.shape
-    loads = pltpu.make_async_copy(pooled_in, pooled, load)
-    loads.start()
-    a, b = split(dproj[...])
-    terms[pl.ds(0, rows), :] = a
-    terms[pl.ds(rows, rows), :] = a
-    terms[pl.ds(2 * rows, rows), :] = b
-    loads.wait()
-
-    def block(m):
-        at = pl.ds(pl.multiple_of(m * 256, 256), 256)
-        return pltpu.make_async_copy(result.at[at], grad_project.at[at], save.at[m])
-
-    @pl.loop(0, result.shape[0] // 256)
-    def _(m):
-        at = pl.ds(pl.multiple_of(m * 256, 256), 256)
-        a, b = split(pooled[:, at])
-        left = jnp.concatenate([a, b, a], axis=0)
-        for n in range(proj // 256):
-            cols = pl.ds(256 * n, 256)
-            result[at, cols] = mm_tn(left, terms[:, cols])
-        block(m).start()
-
-    a, b = split(hidden[...])
-    c, d = split(dcodes[...])
-    grad_code[...] = mm_tn(jnp.concatenate([a, b, a], axis=0), jnp.concatenate([c, c, d], axis=0))
-    for m in range(result.shape[0] // 256):
-        block(m).wait()
-
-
-def project_weights(pooled, dproj, hidden, dcodes):
-    rows, width = pooled.shape
-    proj, code = hidden.shape[1], dcodes.shape[1]
-    hbm = pl.BlockSpec(memory_space=pl.ANY)
-    vmem = pl.BlockSpec(memory_space=pltpu.VMEM)
-    shape = jax.ShapeDtypeStruct
-    return pl.pallas_call(
-        project_kernel,
-        out_shape=[shape((width, proj), f32), shape((proj, code), f32)],
-        in_specs=[hbm] + [vmem] * 3,
-        out_specs=[hbm, vmem],
+        in_specs=[hbm] + [vmem] * 9,
+        out_specs=[hbm] * 2 + [vmem] * 5 + [hbm] * 4,
         scratch_shapes=[
-            pltpu.VMEM((rows, width), f32),
-            pltpu.VMEM((3 * rows, proj), bf16),
-            pltpu.VMEM((width, proj), f32),
-            pltpu.SemaphoreType.DMA,
-            pltpu.SemaphoreType.DMA((width // 256,)),
+            pltpu.VMEM(project, f32),
+            pltpu.VMEM(code, f32),
+            pltpu.SemaphoreType.DMA((SIDE + 3 * PARTS,)),
+            pltpu.SemaphoreType.DMA((project[0] // 256 + 1,)),
+            pltpu.SemaphoreType.DMA((project[0] // 256 + 1,)),
         ],
-        compiler_params=pltpu.CompilerParams(vmem_limit_bytes=60 << 20),
-    )(pooled, dproj, hidden, dcodes)
+        compiler_params=pltpu.CompilerParams(vmem_limit_bytes=14 << 20),
+    )(projector, loss, *norms, *grads)
 
 
 def whiten(codes, pairing):
@@ -1690,9 +1634,10 @@
     width, inner = w_reduce.shape
     taps = w_spatial.reshape(9 * inner, inner)
     (
-        pooled, hidden, dprojected, dcodes, loss, grad_norm_project, upstream,
-        masked, reduced, act1, spatial, act2, normed, slope, mask, stats, sums,
-    ) = forward(
+        _, projector, _, loss,
+        grad_norm_project, grad_norm_expand, grad_norm_reduce, grad_norm_spatial,
+        grad_images, grad_spatial, grad_reduce, grad_expand,
+    ) = training_step(
         jnp.transpose(images, (1, 0, 2)),
         pixel_mask,
         pairing.reshape(1, 256),
@@ -1707,17 +1652,13 @@
         norm_project,
     )
     (
-        grad_images, grad_spatial, grad_reduce, grad_expand,
-        grad_norm_reduce, grad_norm_spatial, grad_norm_expand,
-    ) = backward(
-        upstream, masked, reduced, act1, spatial, act2, normed, slope, mask, stats, sums,
-        w_reduce, taps, w_expand, norm_reduce, norm_spatial, norm_expand,
-    )
-    grad_project, grad_code = project_weights(pooled.reshape(256, width), dprojected, hidden, dcodes)
-    (
-        loss, grad_norm_reduce, grad_norm_spatial, grad_norm_expand, grad_norm_project,
+        grad_project, grad_code, loss,
+        grad_norm_reduce, grad_norm_spatial, grad_norm_expand, grad_norm_project,
         grad_images, grad_spatial, grad_reduce, grad_expand,
     ) = finish(
+        projector,
+        w_project.shape,
+        w_code.shape,
         loss,
         (grad_norm_reduce, grad_norm_spatial, grad_norm_expand, grad_norm_project),
         (grad_images, grad_spatial, grad_reduce, grad_expand),

time: 232 us -> 221 us (0.953)
  Pallas kernels: 231 us -> 220 us
    pallas_call x4 -> x2, Pallas kernels: 231 us -> 220 us  [the longest x1 207 us: training_step(): pl.pallas_call(step_kernel, out_shape=[shape((4, 4, 2, 8, width), f32), s...]
where the time goes in v4:
time: 221 us
  Pallas kernels  220 us (100%)
    pallas_call x1, Pallas kernels, training_step(): pl.pallas_call(step_kernel, out_shape=[shape((4, 4, 2, 8, width), f32), s...  207 us
    pallas_call x1, Pallas kernels, finish(): pl.pallas_call(finish_kernel, out_shape=[shape(project, f32), shape(code,...  13.4 us

profile of v4, /device:TPU:0, one launch (start us, length us, event | category | flops | bytes accessed | tf_op | source)
XLA Modules:
  0.0 221.0 jit_solution(17273810946602138324)
XLA Ops:
  0.6 206.8 %shard_map.203 = (f32[4,4,2,8,2048]{4,3,2,1,0:T(8,128)}, f32[12288,1024]{1,0:T(8,128)}, bf16[448,2048]{1,0:T(8,128)(2,1)}, f32[8,128]{1,0:T(8,128)S(1)}, f32[2,1...) custom-call(bf16[49,8,2048]{2,1,0:T(8,128)(2,1)} %bitcast.9, ...), custom_call_target="tpu_custom_call" | custom-call | tf_op jit(solution)/shard_map/pallas_call | solution.py:1126
  207.5 13.4 %shard_map.204 = (f32[2048,1024]{1,0:T(8,128)}, f32[1024,128]{1,0:T(8,128)}, f32[1,1]{1,0:T(1,128)}, f32[2,512]{1,0:T(2,128)}, f32[2,512]{1,0:T(2,128)}, /*index...) custom-call(f32[12288,1024]{1,0:T(8,128)} %get-tuple-element.32.proj, ...), custom_call_target="tpu_custom_call" | custom-call | tf_op jit(solution)/shard_map/pallas_call | solution.py:1266

commit v5 on v4

--- a/solution.py
+++ b/solution.py
@@ -530,35 +530,26 @@
 
 
 JOBS = (
-    (2, 0, 256, 0, 768, True),
-    (2, 0, 256, 768, 256, False),
-    (2, 0, 256, 1024, 768, True),
-    (2, 0, 256, 1792, 256, False),
-    (0, 0, 384, 0, 512, True),
-    (0, 384, 256, 0, 512, False),
-    (0, 640, 384, 0, 512, True),
-    (0, 1024, 128, 0, 512, False),
-    (0, 1152, 384, 0, 512, True),
-    (0, 1536, 256, 0, 512, False),
-    (0, 1792, 384, 0, 512, True),
-    (0, 2176, 128, 0, 512, False),
-    (1, 0, 384, 0, 512, True),
-    (1, 384, 128, 0, 512, False),
-    (1, 512, 384, 0, 512, True),
-    (1, 896, 128, 0, 512, False),
+    (2, 0, 256, 0, 1536, True),
+    (2, 0, 256, 1536, 512, False),
+    (0, 0, 512, 0, 512, True),
+    (0, 512, 256, 0, 512, False),
+    (0, 768, 512, 0, 512, True),
+    (0, 1280, 256, 0, 512, False),
+    (0, 1536, 512, 0, 512, True),
+    (0, 2048, 256, 0, 512, False),
+    (1, 0, 768, 0, 512, True),
+    (1, 768, 256, 0, 512, False),
 )
 
 ORDER = (
-    -1, 1, -2, 1, 2, -3, 2, 1, 0, 3, 0, 3, 1, 2, -4, 3, -5, 7, 5, 10, 8, 3, 0, 7,
-    2, 5, -6, 10, 2, 7, 6, 1, 8, 3, 9, 5, 6, 0, 2, 7, 4, 1, 8, 3, 9, -7, 1, 10,
-    -10, 2, 0, 5, -8, 14, 1, 8, 6, 12, 2, 9, -9, 3, 1, 2, 7, 8, 4, 0, 12, 9, 7, 1,
-    3, 5, 14, 13, 10, -11, 0, 8, 7, 12, 3, -12, 6, 10, 1, 7, 4, 8, 3, 15, -13, 0, 13, 10,
-    8, 6, 9, 2, 7, 5, 10, -14, 3, 12, 15, 13, 6, 9, 0, 14, 7, 10, 2, 4, 12, 5, -15, 15,
-    8, 7, 6, 12, 9, 8, 10, 4, 13, 11, 12, 5, 4, 15, 14, 10, 6, 9, 12, 4, 11, 13, 5, 0,
-    15, 14, 3, -16, 6, 11, 4, 9, 13, 12, 10, 15, 0, 11, 13, 14, 2, 8, 4, 2, 9, 13, 6, 0,
-    13, 11, 14, 15, 5, 4, 9, 11, 1, -17, 8, 14, 15, 13, 1, 12, 0, 11, 15, 6, 14, 3, 5, 11,
-    12, 14, 7, 10, 11, 15, 6, -18, 13, 12, 8, 5, 4, 11, 15, 6, 14, 5, 11, 12, 9, 13, 7, 4,
-    9, 15, 10, 14, 4, 11, 15, 13, 14, 11,
+    -1, -2, 0, -3, 1, 1, 0, -4, 1, -5, 3, 0, 1, 3, 2, 7, 4, -6, 7, 1, 2, 3, 6, 7,
+    1, 4, 0, 3, -7, 1, 4, -10, 0, -8, 1, 7, 2, 0, -9, 5, 4, 1, 7, 8, 6, -11, 0, 4,
+    3, 2, 7, 8, 1, 4, 9, 0, 7, 5, 6, 2, 1, 3, 4, 9, 0, 7, 5, -12, 8, 2, 6, 4,
+    7, -13, 3, 4, 5, 2, 0, 6, 7, -14, 8, 2, 9, 4, -15, 6, 1, 5, 2, 8, 3, 7, 9, 6,
+    2, 8, 5, 3, -16, 9, 6, 4, -17, 8, 9, 0, 6, 3, 9, 8, 5, 2, 3, 9, 4, 5, 6, 8,
+    5, 0, 2, 7, -18, 9, 3, 8, 6, 5, 3, 7, 4, 9, 5, 8, 5, 9, 1, 6, 6, 5, 9, 2,
+    8, 0, 9, 8,
 )
 
 VM = 43

time: 221 us -> 220 us (level)
  no operation moved by 1% of the time
where the time goes in v5:
time: 220 us; the launch traced here: 219 us
  Pallas kernels  219 us (100%)
    pallas_call x1, Pallas kernels, training_step(): pl.pallas_call(step_kernel, out_shape=[shape((4, 4, 2, 8, width), f32), s...  205 us
    pallas_call x1, Pallas kernels, finish(): pl.pallas_call(finish_kernel, out_shape=[shape(project, f32), shape(code,...  13.4 us

profile of v5, /device:TPU:0, one launch (start us, length us, event | category | flops | bytes accessed | tf_op | source)
XLA Modules:
  0.0 219.4 jit_solution(11456674942386505344)
XLA Ops:
  0.6 205.2 %shard_map.203 = (f32[4,4,2,8,2048]{4,3,2,1,0:T(8,128)}, f32[12288,1024]{1,0:T(8,128)}, bf16[448,2048]{1,0:T(8,128)(2,1)}, f32[8,128]{1,0:T(8,128)S(1)}, f32[2,1...) custom-call(bf16[49,8,2048]{2,1,0:T(8,128)(2,1)} %bitcast.9, ...), custom_call_target="tpu_custom_call" | custom-call | tf_op jit(solution)/shard_map/pallas_call | solution.py:1117
  205.8 13.4 %shard_map.204 = (f32[2048,1024]{1,0:T(8,128)}, f32[1024,128]{1,0:T(8,128)}, f32[1,1]{1,0:T(1,128)}, f32[2,512]{1,0:T(2,128)}, f32[2,512]{1,0:T(2,128)}, /*index...) custom-call(f32[12288,1024]{1,0:T(8,128)} %get-tuple-element.32.proj, ...), custom_call_target="tpu_custom_call" | custom-call | tf_op jit(solution)/shard_map/pallas_call | solution.py:1257

commit v6 on v5

--- a/solution.py
+++ b/solution.py
@@ -314,6 +314,12 @@
     return lax.dot_general(
         a, b, (dims, ((), ())), precision=lax.Precision.HIGHEST, preferred_element_type=f32
     )
+
+
+def three_terms(a, b):
+    a_high, a_low = split(a)
+    b_high, b_low = split(b)
+    return mm(a_high, b_high) + mm(a_low, b_high) + mm(a_high, b_low)
 
 
 def factor_inverse(cov, block=8):
@@ -827,13 +833,16 @@
     white = exact(moved, inverse, ((1,), (1,)))
     unit_scale = lax.rsqrt(jnp.sum(white * white, axis=1, keepdims=True) + epsilon)
     unit = white * unit_scale
-    gap = 2.0 * unit - exact(same[...], unit, ((1,), (0,)))
+    pairs_low = same[...].astype(bf16)
+    high, low = split(unit)
+    pair_sum = mm(pairs_low, high) + mm(pairs_low, low)
+    gap = 2.0 * unit - pair_sum
     loss_out[...] = jnp.broadcast_to(jnp.sum(jnp.sum(gap * gap, axis=1, keepdims=True), axis=0, keepdims=True) * share, (8, 128))
     grad_white = unit_scale * (gap - unit * jnp.sum(unit * gap, axis=1, keepdims=True))
     gram = exact(grad_white, white, ((0,), (0,)))
     half = jnp.where(row > column, gram, jnp.where(row == column, 0.5 * gram, 0.0))
     both = half + jnp.transpose(half)
-    grad_moved = exact(grad_white - exact(white, both, ((1,), (0,))) * share, inverse, ((1,), (0,)))
+    grad_moved = exact(grad_white - three_terms(white, both) * share, inverse, ((1,), (0,)))
     dcodes = grad_moved - jnp.sum(grad_moved, axis=0, keepdims=True) * share
 
     move(pool_movers)

time: 220 us -> 220 us (level)
  no operation moved by 1% of the time
where the time goes in v6:
time: 220 us; the launch traced here: 219 us
  Pallas kernels  219 us (100%)
    pallas_call x1, Pallas kernels, training_step(): pl.pallas_call(step_kernel, out_shape=[shape((4, 4, 2, 8, width), f32), s...  205 us
    pallas_call x1, Pallas kernels, finish(): pl.pallas_call(finish_kernel, out_shape=[shape(project, f32), shape(code,...  13.4 us

profile of v6, /device:TPU:0, one launch (start us, length us, event | category | flops | bytes accessed | tf_op | source)
XLA Modules:
  0.0 219.4 jit_solution(3992658769409531865)
XLA Ops:
  0.6 205.2 %shard_map.203 = (f32[4,4,2,8,2048]{4,3,2,1,0:T(8,128)}, f32[12288,1024]{1,0:T(8,128)}, bf16[448,2048]{1,0:T(8,128)(2,1)}, f32[8,128]{1,0:T(8,128)S(1)}, f32[2,1...) custom-call(bf16[49,8,2048]{2,1,0:T(8,128)(2,1)} %bitcast.9, ...), custom_call_target="tpu_custom_call" | custom-call | tf_op jit(solution)/shard_map/pallas_call | solution.py:1126
  205.8 13.4 %shard_map.204 = (f32[2048,1024]{1,0:T(8,128)}, f32[1024,128]{1,0:T(8,128)}, f32[1,1]{1,0:T(1,128)}, f32[2,512]{1,0:T(2,128)}, f32[2,512]{1,0:T(2,128)}, /*index...) custom-call(f32[12288,1024]{1,0:T(8,128)} %get-tuple-element.32.proj, ...), custom_call_target="tpu_custom_call" | custom-call | tf_op jit(solution)/shard_map/pallas_call | solution.py:1266
